TPU v7x, 32 devices: a whole 2x2x4 slice. The times are simulated.
32 devices in a mesh: dp: 8 (over z, core), heads: 2 (over x), expert: 2 (over y).
Axes of the slice: x: 2, y: 2, z: 4, core: 2. Of those that a mesh axis runs over, the one named last changes fastest.
Arguments:
- block_in: bfloat16 [64, 197, 768], P(('dp', 'expert'), None, 'heads'), may hold values from -6 to 6
- cotangent: bfloat16 [64, 197, 768], P(('dp', 'expert'), None, 'heads'), may hold values from -8 to 8
- route_ids: int32 [64, 197, 2], P(('dp', 'expert')), may hold values from 0 to 7, all different within a row; in each aligned block of 788 rows (0 to 787, 788 to 1575, ..., all dimensions but the last counted through in order) at most 281 rows name the same one
- gain_attn: bfloat16 [768], P(('dp', 'expert')), may hold values from 0.099609375 to 1.8984375
- w_qkv: bfloat16 [768, 3, 768], P(('dp', 'expert'), None, 'heads'), may hold values from -0.21875 to 0.21875
- w_out_attn: bfloat16 [768, 768], P(('dp', 'expert'), 'heads'), may hold values from -0.875 to 0.875
- gain_moe: bfloat16 [768], P(('dp', 'expert')), may hold values from 0.099609375 to 1.8984375
- router: bfloat16 [768, 8], P(('dp', 'expert')), may hold values from -0.21875 to 0.21875
- w_in: bfloat16 [768, 8, 3072], P('dp', 'expert', 'heads'), may hold values from -0.21875 to 0.21875
- w_out: bfloat16 [768, 8, 3072], P('dp', 'expert', 'heads'), may hold values from -2.5 to 2.5
Outputs:
- block_out: bfloat16 [64, 197, 768], P(('dp', 'expert'), None, 'heads')
- grad_block_in: bfloat16 [64, 197, 768], P(('dp', 'expert'), None, 'heads')
- grad_gain_attn: float32 [768], P(('dp', 'expert'))
- grad_w_qkv: float32 [768, 3, 768], P(('dp', 'expert'), None, 'heads')
- grad_w_out_attn: float32 [768, 768], P(('dp', 'expert'), 'heads')
- grad_gain_moe: float32 [768], P(('dp', 'expert'))
- grad_router: float32 [768, 8], P(('dp', 'expert'))
- grad_w_in: float32 [768, 8, 3072], P('dp', 'expert', 'heads')
- grad_w_out: float32 [768, 8, 3072], P('dp', 'expert', 'heads')
Inputs may be any that keep to these rules, and one draw needn't show every extreme that they name: `route_ids`: each token names two different experts. Within each aligned block of 788 tokens (the images of one index of dp and expert) no expert is named more than 281 times, a bound that some block reaches.
All inputs are finite; a program needn't handle non-finite values.
Results may differ from a plain program's by a relative error of at most 0.022.
Values may be sent and summed in bfloat16 or wider, within the bound.
No kernel may reach another device: no remote copies, remote signals or barrier semaphores. Data moves between devices by JAX's collectives and lax.ppermute only.
A program may use at most 192 MiB of HBM per device.

v0:
```python
import functools

import jax
import jax.numpy as jnp
from jax import lax
from jax.experimental import pallas as pl
from jax.experimental.pallas import tpu as pltpu
from jax.sharding import PartitionSpec as P

HEAD_DIM = 64
CORES = 2
EPS = 1e-06
LOW = -1e30
F32 = jnp.float32
BF16 = jnp.bfloat16
VMEM_LIMIT = 56 * 1024 * 1024
SHARE = 64
PARTS = 2


def dot(a, b, ca, cb):
    return lax.dot_general(a, b, (((ca,), (cb,)), ((), ())), preferred_element_type=F32)


def shaped(shape, kind):
    return jax.ShapeDtypeStruct(shape, kind)


def params(dims=1):
    return pltpu.CompilerParams(
        dimension_semantics=("arbitrary",) * dims, vmem_limit_bytes=VMEM_LIMIT
    )


def cost(flops, size, powers=0):
    return pl.CostEstimate(
        flops=flops // SHARE, bytes_accessed=size // SHARE, transcendentals=powers // SHARE
    )


def after(value, *others):
    return lax.optimization_barrier((value,) + others)[0]


def norm_parts(rows):
    average = jnp.mean(rows, axis=-1, keepdims=True)
    centred = rows - average
    spread = jnp.mean(centred * centred, axis=-1, keepdims=True)
    scale = lax.rsqrt(spread + EPS)
    return centred * scale, scale


def softmax_rows(q, own_k, real):
    scores = jnp.where(real, dot(q, own_k, 1, 1) * (HEAD_DIM**-0.5), LOW)
    powers = jnp.exp(scores - jnp.max(scores, axis=-1, keepdims=True))
    return powers / jnp.sum(powers, axis=-1, keepdims=True)


def attend_kernel(
    seq, gain_at, x_ref, side_ref, wqkv_ref, wo_ref, part_ref, qkv_ref, ctx_ref, gain_ref
):
    width = wo_ref.shape[1]
    span = x_ref.shape[0]

    @pl.when(pl.program_id(0) == 0)
    def _():
        gain_ref[...] = side_ref[...].astype(F32).T[gain_at : gain_at + 1, :]

    unit, _ = norm_parts(x_ref[...].astype(F32))
    normed = (unit * gain_ref[...]).astype(BF16)
    for part in range(3):
        cols = slice(part * width, (part + 1) * width)
        qkv_ref[:, cols] = dot(normed, wqkv_ref[:, cols], 1, 0).astype(BF16)
    lane = lax.broadcasted_iota(jnp.int32, (span, 128), 1)
    real = lax.broadcasted_iota(jnp.int32, (span, span), 1) < seq
    for pair in range(width // 128):
        q, k, v = (
            qkv_ref[:, part * width + pair * 128 : part * width + (pair + 1) * 128]
            for part in range(3)
        )
        ctx = jnp.zeros((span, 128), F32)
        for side in range(2):
            mine = (lane >= 64) if side else (lane < 64)
            own_k = jnp.where(mine, k, jnp.zeros_like(k))
            own_v = jnp.where(mine, v, jnp.zeros_like(v))
            weights = softmax_rows(q, own_k, real)
            ctx = ctx + dot(weights.astype(BF16), own_v, 1, 0)
        ctx_ref[:, pair * 128 : (pair + 1) * 128] = ctx.astype(BF16)
    part_ref[...] = dot(ctx_ref[...], wo_ref[...], 1, 1).astype(BF16)


def attend(inputs, gain_at, packed, width, images, seq):
    rows, model = inputs.shape
    span = rows // images
    image = lambda last: pl.BlockSpec((span, last), lambda i: (i, 0))
    return pl.pallas_call(
        functools.partial(attend_kernel, seq, gain_at),
        grid=(images,),
        in_specs=[
            image(model),
            pl.BlockSpec((model, 128), lambda i: (0, 4 * width // 128)),
            pl.BlockSpec((model, 3 * width), lambda i: (0, 0)),
            pl.BlockSpec((model, width), lambda i: (0, 3)),
        ],
        out_specs=[image(model), image(3 * width), image(width)],
        scratch_shapes=[pltpu.VMEM((1, model), F32)],
        out_shape=[
            shaped((rows, model), BF16), shaped((rows, 3 * width), BF16), shaped((rows, width), BF16)
        ],
        compiler_params=params(),
        cost_estimate=cost(10 * rows * model * width, 8 * rows * model, rows * span * width // 64),
        name="attend",
    )(inputs, packed, packed, packed)


def attend_back_kernel(
    seq, gain_at, depth,
    core_ref, x_ref, gain_ref, datt_ref, qkv_ref, ctx_ref, wqkv_ref, wo_ref, side_ref,
    dnorm_ref, stats_ref, keep_ref, send_ref, dproj_ref, dgain_ref, dwqkv_ref, dwo_ref, dside_ref,
):
    width = wo_ref.shape[1]
    span, model = x_ref.shape
    step = pl.program_id(0)

    @pl.when(step == 0)
    def _():
        dgain_ref[...] = jnp.zeros_like(dgain_ref)
        dwqkv_ref[...] = jnp.zeros_like(dwqkv_ref)
        dwo_ref[...] = jnp.zeros_like(dwo_ref)

    datt = datt_ref[...]
    dwo_ref[...] += dot(datt, ctx_ref[...], 0, 0)
    dctx_all = dot(datt, wo_ref[...], 1, 0).astype(BF16)
    lane = lax.broadcasted_iota(jnp.int32, (span, 128), 1)
    real = lax.broadcasted_iota(jnp.int32, (span, span), 1) < seq
    for pair in range(width // 128):
        q, k, v = (
            qkv_ref[:, part * width + pair * 128 : part * width + (pair + 1) * 128]
            for part in range(3)
        )
        dctx = dctx_all[:, pair * 128 : (pair + 1) * 128]
        dq = jnp.zeros((span, 128), F32)
        dk = jnp.zeros((span, 128), F32)
        dv = jnp.zeros((span, 128), F32)
        for side in range(2):
            mine = (lane >= 64) if side else (lane < 64)
            own = lambda t: jnp.where(mine, t, jnp.zeros_like(t))
            own_k, own_v = own(k), own(v)
            weights = softmax_rows(q, own_k, real)
            dweights = dot(dctx, own_v, 1, 1)
            inner = jnp.sum(dweights * weights, axis=-1, keepdims=True)
            dscores = (weights * (dweights - inner)).astype(BF16)
            dq = dq + dot(dscores, own_k, 1, 0)
            dk = dk + dot(dscores, own(q), 0, 0)
            dv = dv + dot(weights.astype(BF16), own(dctx), 0, 0)
        for part, value in enumerate((dq * HEAD_DIM**-0.5, dk * HEAD_DIM**-0.5, dv)):
            start = part * width + pair * 128
            dproj_ref[:, start : start + 128] = value.astype(BF16)
    dproj = dproj_ref[...]
    gain = gain_ref[...]
    unit, _ = norm_parts(x_ref[...].astype(F32))
    normed = (unit * gain).astype(BF16)
    dwqkv_ref[...] += dot(normed, dproj, 0, 0)
    dnormed = dot(dproj, wqkv_ref[...], 1, 1)
    halves, _, half = dnorm_ref.shape
    for h in range(halves):
        dnorm_ref[h] = dnormed[:, h * half : (h + 1) * half].astype(BF16)
    along = dnormed * unit
    dgain_ref[...] += jnp.sum(along, axis=0, keepdims=True)
    first = jnp.sum(dnormed * gain, axis=-1, keepdims=True)
    second = jnp.sum(along * gain, axis=-1, keepdims=True)
    stats_ref[...] = jnp.where(lane == 0, first, jnp.where(lane == 1, second, 0.0))

    @pl.when(step == pl.num_programs(0) - 1)
    def _():
        line = lax.broadcasted_iota(jnp.int32, (128, model), 0)
        dside_ref[...] = side_ref[...] + jnp.where(line == gain_at, dgain_ref[...], 0.0).T
        part = model // (depth * CORES)
        for out_ref, which in ((keep_ref, core_ref[0]), (send_ref, 1 - core_ref[0])):
            for z in range(depth):
                rows = pl.ds(pl.multiple_of((z * CORES + which) * part, 16), part)
                here = slice(z * part, (z + 1) * part)
                out_ref[here, : 3 * width] = dwqkv_ref[rows, :].astype(BF16)
                out_ref[here, 3 * width : 4 * width] = dwo_ref[rows, :].astype(BF16)
                out_ref[here, 4 * width :] = dside_ref[rows, :].astype(BF16)


def attend_back(inputs, gain, datt, qkv, ctx, packed, dside, gain_at, width, images, seq, halves, core, depth):
    rows, model = inputs.shape
    span = rows // images
    image = lambda last: pl.BlockSpec((span, last), lambda i, s: (i, 0))
    fixed = lambda *size: pl.BlockSpec(size, lambda i, s: (0, 0))
    return pl.pallas_call(
        functools.partial(attend_back_kernel, seq, gain_at, depth),
        grid_spec=pltpu.PrefetchScalarGridSpec(
            num_scalar_prefetch=1,
            grid=(images,),
            in_specs=[
            image(model), fixed(1, model), image(model), image(3 * width), image(width),
            fixed(model, 3 * width), pl.BlockSpec((model, width), lambda i, s: (0, 3)),
            fixed(model, 128),
        ],
        out_specs=[
            pl.BlockSpec((halves, span, model // halves), lambda i, s: (0, i, 0)),
            image(128),
            fixed(model // CORES, packed.shape[1]),
            fixed(model // CORES, packed.shape[1]),
        ],
        scratch_shapes=[
            pltpu.VMEM((span, 3 * width), BF16),
            pltpu.VMEM((1, model), F32),
            pltpu.VMEM((model, 3 * width), F32),
            pltpu.VMEM((model, width), F32),
            pltpu.VMEM((model, 128), F32),
        ],
        ),
        out_shape=[
            shaped((halves, rows, model // halves), BF16),
            shaped((rows, 128), F32),
            shaped((model // CORES, packed.shape[1]), BF16),
            shaped((model // CORES, packed.shape[1]), BF16),
        ],
        compiler_params=params(),
        cost_estimate=cost(28 * rows * model * width, 12 * rows * model, rows * span * width // 64),
        name="attend_back",
    )(core, inputs, gain, datt, qkv, ctx, packed, packed, dside)


def slot_kernel(slots, place_ref, ids_ref, rows_ref, cols_ref):
    local, tokens = rows_ref.shape[1:]
    ids = ids_ref[0]
    line = lax.broadcasted_iota(jnp.int32, (8, tokens), 0)
    chosen = jnp.zeros((8, tokens), F32)
    for e in range(local):
        named = jnp.max(jnp.where(ids == place_ref[1] + e, 1.0, 0.0), axis=0, keepdims=True)
        chosen = jnp.where(line == e, named, chosen)
    first = lax.broadcasted_iota(jnp.int32, (tokens, tokens), 0)
    second = lax.broadcasted_iota(jnp.int32, (tokens, tokens), 1)
    before = jnp.where(first < second, 1.0, 0.0).astype(BF16)
    same = jnp.where(first == second, 1.0, 0.0).astype(BF16)
    marks = chosen.astype(BF16)
    rank = dot(marks, before, 1, 0)
    rows_ref[0] = jnp.where(chosen > 0.5, rank, -1.0)[:local].astype(jnp.int32)
    column = lax.broadcasted_iota(jnp.int32, (tokens, 8), 1).astype(F32) * slots
    found = jnp.where(dot(same, marks, 1, 1) > 0.5, dot(before, marks, 0, 1) + column, -1.0)
    cols_ref[0] = found[:, :local].astype(jnp.int32)


def find_slots(place, ids, local, slots):
    blocks, _, tokens = ids.shape
    block = lambda *size: pl.BlockSpec((1,) + size, lambda b, s: (b, 0, 0))
    return pl.pallas_call(
        functools.partial(slot_kernel, slots),
        grid_spec=pltpu.PrefetchScalarGridSpec(
            num_scalar_prefetch=1,
            grid=(blocks,),
            in_specs=[block(2, tokens)],
            out_specs=[block(local, tokens), block(tokens, local)],
        ),
        out_shape=[
            shaped((blocks, local, tokens), jnp.int32), shaped((blocks, tokens, local), jnp.int32)
        ],
        compiler_params=params(),
        cost_estimate=cost(64 * blocks * tokens * tokens, 64 * blocks * tokens),
        name="find_slots",
    )(place, ids)


def expert_kernel(index, depth, blocks, place_ref, slot_ref, router_ref, *refs):
    x_refs, refs = refs[:blocks], refs[blocks:]
    grad_refs, refs = refs[:blocks], refs[blocks:]
    win_refs, refs = refs[:depth], refs[depth:]
    wout_refs, refs = refs[:depth], refs[depth:]
    (
        rows_ref, mids_ref, dchosen_ref, drows_ref, yrows_ref, probs_ref, win_all, wout_all,
    ) = refs
    slots, model = rows_ref.shape[2:]
    tokens = x_refs[0].shape[0]
    part_rows, width = win_refs[0].shape[1:]
    step = pl.program_id(0)

    @pl.when(step == 0)
    def _():
        for k in range(depth):
            owner = lax.rem(place_ref[0] - k + depth, depth)
            at = pl.ds(pl.multiple_of(owner * part_rows, 16), part_rows)
            win_all[at, :] = win_refs[k][0]
            wout_all[at, :] = wout_refs[k][0]

    mask = lax.broadcasted_iota(jnp.int32, (slots, tokens), 0) == slot_ref[0, index : index + 1, :]
    pick = jnp.where(mask, 1.0, 0.0).astype(BF16)
    for b in range(blocks):

        @pl.when(step == b)
        def _(b=b):
            rows_ref[0, 0] = dot(pick, grad_refs[b][...], 1, 0).astype(BF16)
            rows_ref[1, 0] = dot(pick, x_refs[b][...], 1, 0).astype(BF16)
            logits = dot(router_ref[...], x_refs[b][...], 1, 1)
            powers = jnp.exp(logits - jnp.max(logits, axis=0, keepdims=True))
            probs_ref[0] = powers / jnp.sum(powers, axis=0, keepdims=True)

    probs = probs_ref[0]
    line = lax.broadcasted_iota(jnp.int32, probs.shape, 0)
    own = jnp.sum(jnp.where(line == place_ref[1], probs, 0.0), axis=0, keepdims=True)
    gate = jnp.sum(jnp.where(mask, own, 0.0), axis=1, keepdims=True)
    grows, rows = rows_ref[0, 0], rows_ref[1, 0]
    dgate = jnp.zeros((slots, 1), F32)
    drows = jnp.zeros((slots, model), F32)
    yrows = jnp.zeros((slots, model), F32)
    tile = 512 if width % 512 == 0 else width
    curve = 0.7978845608028654

    def products(start):
        cols = slice(start, start + tile)
        return dot(rows, win_all[:, cols], 1, 0), dot(grows, wout_all[:, cols], 1, 0)

    ahead = products(0)
    for start in range(0, width, tile):
        cols = slice(start, start + tile)
        hidden, pulled = ahead
        if start + tile < width:
            ahead = products(start + tile)
        square = hidden * hidden
        bend = jnp.tanh(hidden * (curve + curve * 0.044715 * square))
        half = 0.5 + 0.5 * bend
        active = hidden * half
        slope = half + 0.5 * hidden * (1.0 - bend * bend) * (
            curve + 3.0 * curve * 0.044715 * square
        )
        dgate = dgate + jnp.sum(active * pulled, axis=1, keepdims=True)
        gact = (gate * active).astype(BF16)
        dhid = (gate * pulled * slope).astype(BF16)
        mids_ref[0, 0, :, cols] = gact
        mids_ref[1, 0, :, cols] = dhid
        drows = drows + dot(dhid, win_all[:, cols], 1, 1)
        yrows = yrows + dot(gact, wout_all[:, cols], 1, 1)
    dchosen_ref[0] = jnp.sum(jnp.where(mask, dgate, 0.0), axis=0, keepdims=True)
    drows_ref[0] = drows.astype(BF16)
    yrows_ref[0] = yrows.astype(BF16)


def run_expert(index, place, slot_of, router_rows, xs, grads, pieces, slots):
    blocks, depth = len(xs), len(pieces)
    tokens, model = xs[0].shape
    _, part_rows, width = pieces[0].shape
    experts = router_rows.shape[0]
    fixed = lambda *size: pl.BlockSpec(
        size, lambda b, s: (0,) * len(size), pipeline_mode=pl.Buffered(1)
    )
    block = lambda *size: pl.BlockSpec((1,) + size, lambda b, s: (b, 0, 0))
    both = lambda last: pl.BlockSpec((2, 1, slots, last), lambda b, s: (0, b, 0, 0))
    weight = lambda which: pl.BlockSpec(
        (1, part_rows, width), lambda b, s: (which, 0, 0), pipeline_mode=pl.Buffered(1)
    )
    return pl.pallas_call(
        functools.partial(expert_kernel, index, depth, blocks),
        grid_spec=pltpu.PrefetchScalarGridSpec(
            num_scalar_prefetch=1,
            grid=(blocks,),
            in_specs=[block(slot_of.shape[1], tokens), fixed(experts, model)]
            + [fixed(tokens, model)] * (2 * blocks)
            + [weight(1)] * depth
            + [weight(0)] * depth,
            out_specs=[
                both(model), both(width), block(1, tokens), block(slots, model),
                block(slots, model), block(experts, tokens),
            ],
            scratch_shapes=[pltpu.VMEM((model, width), BF16)] * 2,
        ),
        out_shape=[
            shaped((2, blocks, slots, model), BF16), shaped((2, blocks, slots, width), BF16),
            shaped((blocks, 1, tokens), F32), shaped((blocks, slots, model), BF16),
            shaped((blocks, slots, model), BF16), shaped((blocks, experts, tokens), F32),
        ],
        compiler_params=params(),
        cost_estimate=cost(
            8 * blocks * slots * model * width + 4 * blocks * slots * model * tokens,
            16 * blocks * slots * model,
            blocks * slots * width,
        ),
        name="expert",
    )(place, slot_of, router_rows, *xs, *grads, *pieces, *pieces)


def weight_grad_kernel(depth, place_ref, rows_ref, cols_ref, *refs):
    out_refs, total_ref = refs[:depth], refs[depth]
    _, blocks, slots, model = rows_ref.shape
    width = cols_ref.shape[3]
    part_rows = model // depth
    left = rows_ref[0].reshape(blocks * slots, model)
    right = cols_ref[0].reshape(blocks * slots, width)
    total_ref[...] = dot(left, right, 0, 0)
    for k in range(depth):
        owner = lax.rem(place_ref[0] - k + depth, depth)
        at = pl.ds(pl.multiple_of(owner * part_rows, 16), part_rows)
        out_refs[k][0] = total_ref[at, :].astype(BF16)


def weight_grad(place, rows, cols, depth):
    _, blocks, slots, model = rows.shape
    width = cols.shape[3]
    both = lambda last: pl.BlockSpec((1, blocks, slots, last), lambda i, s: (i, 0, 0, 0))
    return pl.pallas_call(
        functools.partial(weight_grad_kernel, depth),
        grid_spec=pltpu.PrefetchScalarGridSpec(
            num_scalar_prefetch=1,
            grid=(2,),
            in_specs=[both(model), both(width)],
            out_specs=[pl.BlockSpec((1, model // depth, width), lambda i, s: (i, 0, 0))] * depth,
            scratch_shapes=[pltpu.VMEM((model, width), F32)],
        ),
        out_shape=[shaped((2, model // depth, width), BF16)] * depth,
        compiler_params=params(),
        cost_estimate=cost(
            4 * blocks * slots * model * width,
            4 * (blocks * slots * (model + width) + model * width),
        ),
        name="weight_grad",
    )(place, rows, cols)


def gathered(local, slot_ref, rows_refs, all_ref):
    slots, tokens = rows_refs[0].shape[1], slot_ref.shape[1]
    at = lax.broadcasted_iota(jnp.int32, (tokens, local * slots), 1)
    mask = at == slot_ref[0, :, 0:1]
    all_ref[0:slots, :] = rows_refs[0][0]
    for e in range(1, local):
        mask = mask | (at == slot_ref[0, :, e : e + 1])
        all_ref[e * slots : (e + 1) * slots, :] = rows_refs[e][0]
    return dot(jnp.where(mask, 1.0, 0.0).astype(BF16), all_ref[...], 1, 0)


def combine_kernel(local, added, slot_ref, *refs):
    rows_refs, refs = refs[:local], refs[local:]
    out_ref, all_ref = refs[-2:]
    total = gathered(local, slot_ref, rows_refs, all_ref)
    if added:
        total = total + refs[0][...].astype(F32)
    out_ref[...] = total.astype(BF16)


def combine(slot_cols, rows, b, add=None):
    _, tokens, local = slot_cols.shape
    slots, model = rows[0].shape[1:]
    whole = pl.BlockSpec((tokens, model), lambda i: (0, 0))
    return pl.pallas_call(
        functools.partial(combine_kernel, local, add is not None),
        grid=(1,),
        in_specs=[pl.BlockSpec((1, tokens, local), lambda i: (b, 0, 0))]
        + [pl.BlockSpec((1, slots, model), lambda i: (b, 0, 0))] * local
        + [whole] * (add is not None),
        out_specs=whole,
        out_shape=shaped((tokens, model), BF16),
        scratch_shapes=[pltpu.VMEM((local * slots, model), BF16)],
        compiler_params=params(),
        cost_estimate=cost(
            2 * local * slots * model * tokens, 2 * model * (local * slots + 2 * tokens)
        ),
        name="combine",
    )(slot_cols, *rows, *(() if add is None else (add,)))


def combine_back_kernel(local, added, place_ref, slot_ref, *refs):
    rows_refs, refs = refs[:local], refs[local:]
    dchosen_refs, refs = refs[:local], refs[local:]
    probs_ref, router_ref, x_ref = refs[:3]
    out_refs, (drouter_ref, all_ref) = refs[-2 - PARTS : -2], refs[-2:]
    probs = probs_ref[0]
    line = lax.broadcasted_iota(jnp.int32, probs.shape, 0)
    dprobs = jnp.zeros_like(probs)
    for e in range(local):
        dprobs = jnp.where(line == place_ref[1] + e, dchosen_refs[e][0], dprobs)
    inner = jnp.sum(dprobs * probs, axis=0, keepdims=True)
    dlogits = (probs * (dprobs - inner)).astype(BF16)
    drouter_ref[...] = dot(dlogits, x_ref[...], 1, 0)
    total = gathered(local, slot_ref, rows_refs, all_ref) + dot(dlogits, router_ref[...], 0, 0)
    part = out_refs[0].shape[1]
    for p in range(PARTS):
        piece = total[:, p * part : (p + 1) * part]
        if added:
            piece = piece + refs[3 + p][...].astype(F32)
        out_refs[p][...] = piece.astype(BF16)


def combine_back(place, slot_cols, rows, dchosen, probs, router_rows, x, b, add=None):
    _, tokens, local = slot_cols.shape
    slots, model = rows[0].shape[1:]
    experts = router_rows.shape[0]
    whole = pl.BlockSpec((tokens, model), lambda i, s: (0, 0))
    part = pl.BlockSpec((tokens, model // PARTS), lambda i, s: (0, 0))
    block = lambda *size: pl.BlockSpec((1,) + size, lambda i, s: (b, 0, 0))
    small = pl.BlockSpec((experts, model), lambda i, s: (0, 0))
    return pl.pallas_call(
        functools.partial(combine_back_kernel, local, add is not None),
        grid_spec=pltpu.PrefetchScalarGridSpec(
            num_scalar_prefetch=1,
            grid=(1,),
            in_specs=[block(tokens, local)]
            + [block(slots, model)] * local
            + [block(1, tokens)] * local
            + [block(experts, tokens), small, whole]
            + [part] * (PARTS * (add is not None)),
            out_specs=[part] * PARTS + [small],
            scratch_shapes=[pltpu.VMEM((local * slots, model), BF16)],
        ),
        out_shape=[shaped((tokens, model // PARTS), BF16)] * PARTS
        + [shaped((experts, model), F32)],
        compiler_params=params(),
        cost_estimate=cost(
            2 * local * slots * model * tokens, 2 * model * (local * slots + 3 * tokens)
        ),
        name="combine_back",
    )(place, slot_cols, *rows, *dchosen, probs, router_rows, x, *(() if add is None else add))


def per_device(
    block_in, cotangent, route_ids, gain_attn, w_qkv, w_out_attn, gain_moe, router, w_in, w_out
):
    n_dp, n_heads, n_exp = (lax.axis_size(name) for name in ("dp", "heads", "expert"))
    n_z = n_dp // CORES
    dp, head, exp = (lax.axis_index(name) for name in ("dp", "heads", "expert"))
    z, core = dp // CORES, dp % CORES
    low = core == 0
    images, seq, half_width = block_in.shape
    span = -(-seq // 16) * 16
    rows = images * span
    model = half_width * n_heads
    width = w_qkv.shape[2]
    shard = w_qkv.shape[0]
    expert_count = router.shape[1]
    group = w_in.shape[1]
    local = group // CORES
    part_rows, _, hidden_width = w_in.shape
    capacity = 20 * images * seq // (7 * expert_count)
    slots = -(-capacity // 16) * 16
    blocks = n_exp * CORES
    rest = 128

    def shift(value, axis, step):
        size = lax.axis_size(axis)
        return lax.ppermute(value, axis, [(i, (i + step) % size) for i in range(size)])

    def shift_z(value, step):
        pairs = [
            (a * CORES + c, ((a + step) % n_z) * CORES + c) for a in range(n_z) for c in range(CORES)
        ]
        return lax.ppermute(value, "dp", pairs)

    def swap_core(value):
        return lax.ppermute(value, "dp", [(i, i ^ 1) for i in range(n_dp)])

    def place_at(pieces, index, count):
        if count == 2:
            first = index == 0
            return jnp.stack(
                [jnp.where(first, pieces[0], pieces[1]), jnp.where(first, pieces[1], pieces[0])]
            )
        out = jnp.zeros((count,) + pieces[0].shape, pieces[0].dtype)
        for k, piece in enumerate(pieces):
            out = lax.dynamic_update_index_in_dim(out, piece, (index - k) % count, 0)
        return out

    def spread(value, axis):
        return [value] + [shift(value, axis, k) for k in range(1, lax.axis_size(axis))]

    def take(value, index, dim=0):
        return lax.dynamic_index_in_dim(value, index, dim, keepdims=False)

    def expert_shards():
        both = jnp.stack([w_out, w_in]).reshape(2, part_rows, CORES, local, hidden_width)
        by_core = both.transpose(2, 3, 0, 1, 4)
        other = swap_core(take(by_core, 1 - core))
        mine = take(by_core, core)
        return jnp.concatenate(
            [jnp.where(low, mine, other), jnp.where(low, other, mine)], axis=2
        )

    ways_up = n_z // 2
    ways_down = n_z - 1 - ways_up

    def ring(piece):
        pieces = [piece] + [None] * (n_z - 1)
        for k in range(1, ways_up + 1):
            pieces[k] = shift_z(pieces[k - 1], 1)
        for k in range(1, ways_down + 1):
            pieces[n_z - k] = shift_z(pieces[(n_z - k + 1) % n_z], -1)
        return pieces

    def blocks_of(value, hold=()):
        along = spread(value, "expert")
        along = along[:1] + [after(part, *hold) for part in along[1:]]
        return along + [swap_core(part) for part in along]

    def full_rows(value):
        padded = jnp.pad(value, ((0, 0), (0, span - seq), (0, 0))).reshape(rows, half_width)
        parts = place_at(spread(padded, "heads"), head, n_heads)
        return jnp.concatenate([parts[i] for i in range(n_heads)], axis=-1)

    inputs = full_rows(block_in)
    grad_full = full_rows(cotangent)

    tail = jnp.concatenate(
        [router, gain_attn[:, None], gain_moe[:, None],
         jnp.zeros((shard, rest - expert_count - 2), BF16)], axis=1
    )
    own_pack = jnp.concatenate([w_qkv.reshape(shard, 3 * width), w_out_attn, tail], axis=1)
    columns = own_pack.shape[1]
    shards = expert_shards()
    ids = jnp.pad(route_ids, ((0, 0), (0, span - seq), (0, 0)), constant_values=-1)
    ids_all = jnp.stack(blocks_of(ids.reshape(rows, 2).T))
    pack_z = place_at(
        [own_pack] + [after(shift_z(own_pack, k), shards) for k in range(1, n_z)], z, n_z
    )
    pack = place_at(spread(after(pack_z, ids_all), "expert"), exp, n_exp)
    pieces = []
    for e in range(local):
        pieces.append(ring(after(shards[e], pieces[-1][1]) if e else shards[e]))
    last = local - 1

    pack = after(pack, pieces[0][1], inputs, grad_full)
    other_pack = swap_core(pack)
    pack = jnp.stack([jnp.where(low, pack, other_pack), jnp.where(low, other_pack, pack)])
    pack = pack.transpose(2, 0, 1, 3, 4).reshape(model, columns)
    side = pack[:, 4 * width :].T
    router_rows = side[:expert_count]
    gain_one = side[expert_count : expert_count + 1].astype(F32)
    gain_two = side[expert_count + 1 : expert_count + 2].astype(F32)

    first_expert = exp * group + core * local
    place = [jnp.stack([z, first_expert + e]).astype(jnp.int32) for e in range(local)]
    slot_of, slot_cols = find_slots(place[0], ids_all, local, slots)

    grads_all = blocks_of(grad_full)
    inputs_ready = inputs
    part, qkv, ctx = attend(inputs_ready, expert_count, pack, width, images, seq)
    part = after(part, pieces[0][-1])
    part_other = shift(part, "heads", 1)
    for k in range(2, n_heads):
        part_other = part_other + shift(part, "heads", k)
    part_other = after(part_other, pieces[0][ways_up], slot_cols)
    middle = inputs.astype(F32) + (part.astype(F32) + part_other.astype(F32))
    unit_two, scale_two = norm_parts(middle)
    normed_two = (unit_two * gain_two).astype(BF16)
    tokens_all = blocks_of(normed_two, (pieces[last][1],))

    done = []

    def begin_rings(e, *hold):
        rows_e, mids_e = done[e][:2]
        rings.append(weight_grad(place[e], after(rows_e, *hold), mids_e, n_z))

    def ring_first(e):
        return shift_z(rings[e][-ways_up % n_z], 1)

    def ring_down(e):
        chunks = rings[e]
        downward = chunks[ways_down]
        for k in range(ways_down - 1, 0, -1):
            downward = (shift_z(downward, -1).astype(F32) + chunks[k].astype(F32)).astype(BF16)
        return shift_z(downward, -1)

    def ring_middle(e, upward, *hold):
        chunks = rings[e]
        for k in range(ways_up - 1, 0, -1):
            own = after(chunks[n_z - k], *hold)
            upward = (upward.astype(F32) + own.astype(F32)).astype(BF16)
            if k > 1:
                upward = shift_z(upward, 1)
        return upward

    def ring_end(e, upward, downward, *hold):
        own = after(rings[e][0], *hold).astype(F32)
        return own + shift_z(upward, 1).astype(F32) + downward.astype(F32)

    rings = []
    for e in range(local):
        here = list(pieces[e])
        if e:
            here[0] = after(here[0], rings[-1][0])
        done.append(
            run_expert(
                e, place[e], slot_of, router_rows, tokens_all, grads_all, here, slots
            )
        )
        if e < local - 1:
            begin_rings(e)
    drows, yrows, dchosen = ([r[i] for r in done] for i in (3, 4, 2))
    probs = done[0][5]

    begin_rings(last)
    arrived_zero, down_zero = ring_first(0), ring_down(0)
    early = ring_middle(0, arrived_zero, rings[last][0])
    arrived_last, down_last = ring_first(last), ring_down(last)
    drows[0] = after(drows[0], early, down_zero, rings[last][0])

    def back_of(b, add=None):
        *parts, more = combine_back(
            place[0], slot_cols, drows, dchosen, probs, router_rows, tokens_all[b], b, add
        )
        return parts, more

    drouter = jnp.zeros((expert_count, model), F32)
    arrived = [None] * n_exp
    for k in reversed(range(n_exp)):
        sent, more = back_of(n_exp + k)
        arrived[k] = [swap_core(part) for part in sent]
        drouter = drouter + more
    from_exp = []
    for k in reversed(range(n_exp)):
        if k < n_exp - 1:
            arrived[k][0] = after(arrived[k][0], total[0])
        total, more = back_of(k, arrived[k])
        drouter = drouter + more
        if k:
            from_exp.append([shift(part, "expert", -k) for part in total])
    ends = [ring_end(0, early, down_zero)]
    dsum, dsum_other = [], []
    for p in range(PARTS):
        value = (after(total[p], ends[0]) if p == 0 else total[p]).astype(F32)
        for came in from_exp:
            value = value + came[p].astype(F32)
        dsum.append(value.astype(BF16))
        other = shift(dsum[p], "heads", 1)
        for k in range(2, n_heads):
            other = other + shift(dsum[p], "heads", k)
        dsum_other.append(other)
    dsum_other[-1] = after(dsum_other[-1], arrived_last)

    yrows[0] = after(yrows[0], dsum[0])
    y_came = [swap_core(combine(slot_cols, yrows, n_exp + k)) for k in range(n_exp)]
    y_from = [
        shift(combine(slot_cols, yrows, k, after(y_came[k], dsum[-1])), "expert", -k)
        for k in range(1, n_exp)
    ]
    dnormed_two = jnp.concatenate(
        [own.astype(F32) + other.astype(F32) for own, other in zip(dsum, dsum_other)], axis=1
    )
    scaled = dnormed_two * gain_two
    grad_gain_two = jnp.sum(dnormed_two * unit_two, axis=0)
    dmiddle = grad_full.astype(F32) + scale_two * (
        scaled
        - jnp.mean(scaled, axis=-1, keepdims=True)
        - unit_two * jnp.mean(scaled * unit_two, axis=-1, keepdims=True)
    )
    late = ring_middle(last, arrived_last, dsum_other[-1])
    datt = after(dmiddle.astype(BF16), late, *y_came)

    dside = jnp.concatenate(
        [drouter, jnp.zeros((1, model), F32), grad_gain_two[None, :],
         jnp.zeros((rest - expert_count - 2, model), F32)], axis=0
    ).T
    dnorm, stats, dkeep, dsend = attend_back(
        inputs, gain_one, datt, qkv, ctx, pack, dside, expert_count, width, images, seq, n_heads,
        core.astype(jnp.int32)[None], n_z,
    )
    dsend = after(dsend, *y_from, down_last)

    dcame = swap_core(dsend)
    dpack = (dkeep.astype(F32) + dcame.astype(F32)).astype(BF16)
    dpack = dpack.reshape(n_z, n_exp, shard, columns)
    y_own = combine(slot_cols, yrows, 0, after(y_came[0], dcame)).astype(F32)
    for value in y_from:
        y_own = y_own + value.astype(F32)
    y_own = y_own.astype(BF16)

    ends.append(ring_end(last, late, down_last, dsend))
    dtotal = take(dpack, exp, 1).astype(F32)
    for k in range(1, n_exp):
        came = shift(take(dpack, (exp + k) % n_exp, 1), "expert", k)
        dtotal = dtotal + after(came, ends[last]).astype(F32)
    dpack = dtotal.astype(BF16)
    dtotal = take(dpack, z).astype(F32)
    for k in range(1, n_z):
        dtotal = dtotal + shift_z(take(dpack, (z + k) % n_z), k).astype(F32)
    dside = dtotal[:, 4 * width :]
    over_heads = dside[:, : expert_count + 1].T
    summed = over_heads
    for k in range(1, n_heads):
        summed = summed + shift(over_heads, "heads", k)

    def own_half(value):
        return lax.dynamic_slice_in_dim(value, head * half_width, half_width, 1)

    def cut(value):
        return value.astype(BF16).reshape(images, span, half_width)[:, :seq]

    dnorm, stats = lax.optimization_barrier((dnorm, stats, dcame))[:2]
    dn_own = take(dnorm, head).astype(F32)
    sums = stats[:, :2].T
    sums_total = sums
    for k in range(1, n_heads):
        came = shift(take(dnorm, (head + k) % n_heads), "heads", k)
        dn_own = dn_own + after(came, dtotal).astype(F32)
        sums_total = sums_total + after(shift(sums, "heads", k), dtotal)
    unit_one, scale_one = norm_parts(inputs.astype(F32))
    grad_in = own_half(dmiddle) + scale_one * (
        dn_own * own_half(gain_one)
        - sums_total[0][:, None] / model
        - own_half(unit_one) * (sums_total[1][:, None] / model)
    )

    y_total = own_half(y_own).astype(F32)
    for k in range(1, n_heads):
        there = (head + k) % n_heads
        part_y = lax.dynamic_slice_in_dim(y_own, there * half_width, half_width, 1)
        y_total = y_total + after(shift(part_y, "heads", k), dtotal).astype(F32)
    block_out = own_half(middle) + y_total

    stacked = jnp.stack(ends).reshape(local, 2, CORES, part_rows, hidden_width)
    other = swap_core(take(stacked, 1 - core, 2).astype(BF16)).astype(F32)
    own = take(stacked, core, 2)
    joined = jnp.concatenate([jnp.where(low, own, other), jnp.where(low, other, own)], axis=0)
    grads = joined.transpose(1, 2, 0, 3)

    return (
        cut(block_out),
        cut(grad_in),
        summed[expert_count],
        dtotal[:, : 3 * width].reshape(shard, 3, width),
        dtotal[:, 3 * width : 4 * width],
        dside[:, expert_count + 1],
        summed[:expert_count].T,
        grads[1],
        grads[0],
    )


def solution(mesh):
    return jax.shard_map(
        per_device,
        mesh=mesh,
        in_specs=(
            P(("dp", "expert"), None, "heads"),
            P(("dp", "expert"), None, "heads"),
            P(("dp", "expert"), None, None),
            P(("dp", "expert")),
            P(("dp", "expert"), None, "heads"),
            P(("dp", "expert"), "heads"),
            P(("dp", "expert")),
            P(("dp", "expert"), None),
            P("dp", "expert", "heads"),
            P("dp", "expert", "heads"),
        ),
        out_specs=(
            P(("dp", "expert"), None, "heads"),
            P(("dp", "expert"), None, "heads"),
            P(("dp", "expert")),
            P(("dp", "expert"), None, "heads"),
            P(("dp", "expert"), "heads"),
            P(("dp", "expert")),
            P(("dp", "expert"), None),
            P("dp", "expert", "heads"),
            P("dp", "expert", "heads"),
        ),
        check_vma=False,
    )
```

profile of v0, /device:TPU:18, one launch (start us, length us, event | category | flops | bytes accessed | tf_op | source)
XLA Modules:
  0.0 454.2 jit_solution(4188569299180283484)
XLA Ops:
  15.1 5.7 %collective-permute-done.10 = bf16[832,384]{1,0:T(8,128)(2,1)} collective-permute-done((bf16[832,384]{1,0:T(8,128)(2,1)S(1)}, bf16[832,384]{1,0:T(8,128)(2,1)}, u32[]{:S(2)}, u32[]{:S(2)}) %collective-permute-start.10) | collective-permute-done | bytes 639008 | tf_op jit(solution)/shard_map/ppermute | solution.py:541
  38.5 6.2 %collective-permute-done.8 = bf16[4,48,1664]{2,1,0:T(8,128)(2,1)S(1)} collective-permute-done((bf16[4,48,1664]{2,1,0:T(8,128)(2,1)}, bf16[4,48,1664]{2,1,0:T(8,128)(2,1)S(1)}, u32[]{:S(2)}, u32[]{:S(2)}) %collective-permute-start.8) | collective-permute-done | bytes 639008 | tf_op jit(solution)/shard_map/ppermute | solution.py:541
  46.1 12.5 %collective-permute-done.9.refs_9_.refs_13_ = bf16[2,192,1536]{2,1,0:T(8,128)(2,1)S(1)} collective-permute-done((bf16[2,192,1536]{2,1,0:T(8,128)(2,1)S(1)}, bf16[2,192,1536]{2,1,0:T(8,128)(2,1)S(1)}, u32[]{:S(2)}, u32[]{:S(2)}) %collective-permute-start.9) | collective-permute-done | bytes 1179680 | tf_op jit(solution)/shard_map/ppermute | solution.py:547
  63.5 10.9 %attend.1 = (bf16[832,768]{1,0:T(8,128)(2,1)}, bf16[832,1152]{1,0:T(8,128)(2,1)}, bf16[832,384]{1,0:T(8,128)(2,1)}) custom-call(bf16[832,768]{1,0:T(8,128)(2,1)} %pad_maximum_fusion.3.x_ref, bf16[768,1664]{1,0:T(8,128)(2,1)} %bitcast.131, bf16[768,1664]{1,0:T(8,128)(2,1)} %bitcast.132, bf16[768,1664]{1,0:T(8,128)(2,1)} %bitcast.133), custom_call_target="tpu_custom_call" | custom-call | flops 38338560 | bytes 79872 | tf_op jit(solution)/shard_map/attend/pallas_call | solution.py:96
  74.4 12.6 %collective-permute-done.12.refs_11_.refs_15_ = bf16[2,192,1536]{2,1,0:T(8,128)(2,1)} collective-permute-done((bf16[2,192,1536]{2,1,0:T(8,128)(2,1)S(1)}, bf16[2,192,1536]{2,1,0:T(8,128)(2,1)}, u32[]{:S(2)}, u32[]{:S(2)}) %collective-permute-start.12) | collective-permute-done | bytes 1179680 | tf_op jit(solution)/shard_map/ppermute | solution.py:547
  91.9 6.5 %find_slots.1 = (s32[4,2,832]{2,1,0:T(2,128)}, s32[4,832,2]{2,1,0:T(8,128)}) custom-call(s32[2]{0:T(128)} %pad_add_fusion.1.place_ref, s32[4,2,832]{2,1,0:T(2,128)} %pad_add_fusion.ids_ref), custom_call_target="tpu_custom_call" | custom-call | flops 2768896 | bytes 3328 | tf_op jit(solution)/shard_map/find_slots/pallas_call | solution.py:252
  100.4 15.9 %collective-permute-done.14.refs_10_.refs_14_ = bf16[2,192,1536]{2,1,0:T(8,128)(2,1)} collective-permute-done((bf16[2,192,1536]{2,1,0:T(8,128)(2,1)S(1)}, bf16[2,192,1536]{2,1,0:T(8,128)(2,1)}, u32[]{:S(2)}, u32[]{:S(2)}) %collective-permute-start.14) | collective-permute-done | bytes 1179680 | tf_op jit(solution)/shard_map/ppermute | solution.py:547
  130.2 20.4 %collective-permute-done.16.refs_9_.refs_13_ = bf16[2,192,1536]{2,1,0:T(8,128)(2,1)} collective-permute-done((bf16[2,192,1536]{2,1,0:T(8,128)(2,1)}, bf16[2,192,1536]{2,1,0:T(8,128)(2,1)}, u32[]{:S(2)}, u32[]{:S(2)}) %collective-permute-start.16) | collective-permute-done | bytes 1179680 | tf_op jit(solution)/shard_map/ppermute | solution.py:547
  158.7 28.1 %expert.2 = (bf16[2,4,288,768]{3,2,1,0:T(8,128)(2,1)}, bf16[2,4,288,1536]{3,2,1,0:T(8,128)(2,1)}, f32[4,1,832]{2,1,0:T(1,128)}, bf16[4,288,768]{2,1,0:T(8,128)(2...) custom-call(s32[2]{0:T(128)} %pad_add_fusion.1.place_ref, s32[4,2,832]{2,1,0:T(2,128)} %get-tuple-element.86.slot_ref, ...), custom_call_target="tpu_custom_call" | custom-call | flops 215875584 | bytes 221184 | tf_op jit(solution)/shard_map/expert/pallas_call | solution.py:355
  186.8 11.9 %weight_grad.2 = (bf16[2,192,1536]{2,1,0:T(8,128)(2,1)}, bf16[2,192,1536]{2,1,0:T(8,128)(2,1)}, bf16[2,192,1536]{2,1,0:T(8,128)(2,1)}, bf16[2,192,1536]{2,1,0:T(8,128)(2,1)}) custom-call(s32[2]{0:T(128)} %pad_add_fusion.1.place_ref, bf16[2,4,288,768]{3,2,1,0:T(8,128)(2,1)} %get-tuple-element.91.rows_ref, bf16[2,4,288,1536]{3,2,1,0:T(8,128)(2,1)} %get-tuple-element.92.cols_ref), custom_call_target="tpu_custom_call" | custom-call | flops 84934656 | bytes 239616 | tf_op jit(solution)/shard_map/weight_grad/pallas_call | solution.py:403
  202.7 8.0 %collective-permute-done.23.refs_10_.refs_14_ = bf16[2,192,1536]{2,1,0:T(8,128)(2,1)} collective-permute-done((bf16[2,192,1536]{2,1,0:T(8,128)(2,1)}, bf16[2,192,1536]{2,1,0:T(8,128)(2,1)}, u32[]{:S(2)}, u32[]{:S(2)}) %collective-permute-start.23) | collective-permute-done | bytes 1179680 | tf_op jit(solution)/shard_map/ppermute | solution.py:547
  210.6 28.1 %expert.3 = (bf16[2,4,288,768]{3,2,1,0:T(8,128)(2,1)}, bf16[2,4,288,1536]{3,2,1,0:T(8,128)(2,1)}, f32[4,1,832]{2,1,0:T(1,128)}, bf16[4,288,768]{2,1,0:T(8,128)(2...) custom-call(s32[2]{0:T(128)} %pad_add_fusion.2.place_ref, s32[4,2,832]{2,1,0:T(2,128)} %get-tuple-element.86.slot_ref, ...), custom_call_target="tpu_custom_call" | custom-call | flops 215875584 | bytes 221184 | tf_op jit(solution)/shard_map/expert/pallas_call | solution.py:355
  238.7 12.2 %weight_grad.3 = (bf16[2,192,1536]{2,1,0:T(8,128)(2,1)}, bf16[2,192,1536]{2,1,0:T(8,128)(2,1)}, bf16[2,192,1536]{2,1,0:T(8,128)(2,1)}, bf16[2,192,1536]{2,1,0:T(8,128)(2,1)}) custom-call(s32[2]{0:T(128)} %pad_add_fusion.2.place_ref, bf16[2,4,288,768]{3,2,1,0:T(8,128)(2,1)} %get-tuple-element.97.rows_ref, bf16[2,4,288,1536]{3,2,1,0:T(8,128)(2,1)} %get-tuple-element.98.cols_ref), custom_call_target="tpu_custom_call" | custom-call | flops 84934656 | bytes 239616 | tf_op jit(solution)/shard_map/weight_grad/pallas_call | solution.py:403
  253.5 6.5 %collective-permute-done.25 = bf16[2,192,1536]{2,1,0:T(8,128)(2,1)} collective-permute-done((bf16[2,192,1536]{2,1,0:T(8,128)(2,1)}, bf16[2,192,1536]{2,1,0:T(8,128)(2,1)}, u32[]{:S(2)}, u32[]{:S(2)}) %collective-permute-start.25) | collective-permute-done | bytes 1179680 | tf_op jit(solution)/shard_map/ppermute | solution.py:547
  260.0 5.3 %combine_back.5 = (bf16[832,384]{1,0:T(8,128)(2,1)}, bf16[832,384]{1,0:T(8,128)(2,1)}, f32[8,768]{1,0:T(8,128)}) custom-call(s32[2]{0:T(128)} %pad_add_fusion.1.place_ref, s32[4,832,2]{2,1,0:T(8,128)} %get-tuple-element.84.slot_ref, bf16[4,288,768]{2,1,0:T(8,128)(2,1)} %get-tuple-element.102.refs_0_, bf16[4,288,768]{2,1,0:T(8,128)(2,1)} %get-tuple-element.103.refs_1_, ...), custom_call_target="tpu_custom_call" | custom-call | flops 11501568 | bytes 73728 | tf_op jit(solution)/shard_map/combine_back/pallas_call | solution.py:493
  269.0 5.3 %combine_back.4 = (bf16[832,384]{1,0:T(8,128)(2,1)}, bf16[832,384]{1,0:T(8,128)(2,1)}, f32[8,768]{1,0:T(8,128)}) custom-call(s32[2]{0:T(128)} %pad_add_fusion.1.place_ref, s32[4,832,2]{2,1,0:T(8,128)} %get-tuple-element.84.slot_ref, bf16[4,288,768]{2,1,0:T(8,128)(2,1)} %get-tuple-element.102.refs_0_, bf16[4,288,768]{2,1,0:T(8,128)(2,1)} %get-tuple-element.103.refs_1_, ...), custom_call_target="tpu_custom_call" | custom-call | flops 11501568 | bytes 73728 | tf_op jit(solution)/shard_map/combine_back/pallas_call | solution.py:493
  276.5 5.6 %combine_back.6 = (bf16[832,384]{1,0:T(8,128)(2,1)}, bf16[832,384]{1,0:T(8,128)(2,1)}, f32[8,768]{1,0:T(8,128)}) custom-call(s32[2]{0:T(128)} %pad_add_fusion.1.place_ref, s32[4,832,2]{2,1,0:T(8,128)} %get-tuple-element.84.slot_ref, bf16[4,288,768]{2,1,0:T(8,128)(2,1)} %get-tuple-element.102.refs_0_, bf16[4,288,768]{2,1,0:T(8,128)(2,1)} %get-tuple-element.103.refs_1_, ...), custom_call_target="tpu_custom_call" | custom-call | flops 11501568 | bytes 73728 | tf_op jit(solution)/shard_map/combine_back/pallas_call | solution.py:493
  287.2 5.6 %combine_back.7 = (bf16[832,384]{1,0:T(8,128)(2,1)}, bf16[832,384]{1,0:T(8,128)(2,1)}, f32[8,768]{1,0:T(8,128)}) custom-call(s32[2]{0:T(128)} %pad_add_fusion.1.place_ref, s32[4,832,2]{2,1,0:T(8,128)} %get-tuple-element.84.slot_ref, bf16[4,288,768]{2,1,0:T(8,128)(2,1)} %get-tuple-element.102.refs_0_, bf16[4,288,768]{2,1,0:T(8,128)(2,1)} %get-tuple-element.103.refs_1_, ...), custom_call_target="tpu_custom_call" | custom-call | flops 11501568 | bytes 73728 | tf_op jit(solution)/shard_map/combine_back/pallas_call | solution.py:493
  292.9 6.8 %collective-permute-done.34 = bf16[832,384]{1,0:T(8,128)(2,1)} collective-permute-done((bf16[832,384]{1,0:T(8,128)(2,1)}, bf16[832,384]{1,0:T(8,128)(2,1)}, u32[]{:S(2)}, u32[]{:S(2)}) %collective-permute-start.34) | collective-permute-done | bytes 639008 | tf_op jit(solution)/shard_map/ppermute | solution.py:541
  305.2 7.1 %collective-permute-done.31 = bf16[832,384]{1,0:T(8,128)(2,1)S(1)} collective-permute-done((bf16[832,384]{1,0:T(8,128)(2,1)}, bf16[832,384]{1,0:T(8,128)(2,1)S(1)}, u32[]{:S(2)}, u32[]{:S(2)}) %collective-permute-start.31) | collective-permute-done | bytes 639008 | tf_op jit(solution)/shard_map/ppermute | solution.py:541
  322.2 23.0 %collective-permute-done.36 = bf16[2,192,1536]{2,1,0:T(8,128)(2,1)} collective-permute-done((bf16[2,192,1536]{2,1,0:T(8,128)(2,1)}, bf16[2,192,1536]{2,1,0:T(8,128)(2,1)}, u32[]{:S(2)}, u32[]{:S(2)}) %collective-permute-start.36) | collective-permute-done | bytes 1179680 | tf_op jit(solution)/shard_map/ppermute | solution.py:547
  361.4 20.8 %attend_back.1 = (bf16[2,832,384]{2,1,0:T(8,128)(2,1)}, f32[832,128]{1,0:T(8,128)}, bf16[384,1664]{1,0:T(8,128)(2,1)}, bf16[384,1664]{1,0:T(8,128)(2,1)}) custom-call(s32[1]{0:T(128)} %bitcast.35.core_ref, bf16[832,768]{1,0:T(8,128)(2,1)} %pad_maximum_fusion.3.x_ref, f32[1,768]{1,0:T(1,128)} %copy.165.gain_ref, ...), custom_call_target="tpu_custom_call" | custom-call | flops 107347968 | bytes 119808 | tf_op jit(solution)/shard_map/attend_back/pallas_call | solution.py:193
  422.8 8.9 %collective-permute-done.44 = bf16[48,1664]{1,0:T(8,128)(2,1)S(1)} collective-permute-done((bf16[48,1664]{1,0:T(8,128)(2,1)S(1)}, bf16[48,1664]{1,0:T(8,128)(2,1)S(1)}, u32[]{:S(2)}, u32[]{:S(2)}) %collective-permute-start.44) | collective-permute-done | bytes 159776 | tf_op jit(solution)/shard_map/ppermute | solution.py:547
  435.9 11.5 %collective-permute-done.41 = bf16[832,384]{1,0:T(8,128)(2,1)S(1)} collective-permute-done((bf16[832,384]{1,0:T(8,128)(2,1)S(1)}, bf16[832,384]{1,0:T(8,128)(2,1)S(1)}, u32[]{:S(2)}, u32[]{:S(2)}) %collective-permute-start.41) | collective-permute-done | bytes 639008 | tf_op jit(solution)/shard_map/ppermute | solution.py:541
  (275 shorter events, 167.1 us)
Async XLA Ops:
  30.9 27.7 %collective-permute-start.9 = (bf16[2,192,1536]{2,1,0:T(8,128)(2,1)S(1)}, bf16[2,192,1536]{2,1,0:T(8,128)(2,1)S(1)}, u32[]{:S(2)}, u32[]{:S(2)}) collective-permute-start(bf16[2,192,1536]{2,1,0:T(8,128)(2,1)S(1)} %get-tuple-element.208.refs_8_.refs_12_), channel_id=1, source_target_pairs={{0,8},{4,12},{8,16},{12,20},{16,24},{20,28},{24,0},{28,4},{1,9},{5... | collective-permute-start | bytes 3538952 | tf_op jit(solution)/shard_map/ppermute | solution.py:547
  58.6 28.5 %collective-permute-start.12 = (bf16[2,192,1536]{2,1,0:T(8,128)(2,1)S(1)}, bf16[2,192,1536]{2,1,0:T(8,128)(2,1)}, u32[]{:S(2)}, u32[]{:S(2)}) collective-permute-start(bf16[2,192,1536]{2,1,0:T(8,128)(2,1)S(1)} %get-tuple-element.208.refs_8_.refs_12_), channel_id=1, source_target_pairs={{0,24},{4,28},{8,0},{12,4},{16,8},{20,12},{24,16},{28,20},{1,25},{... | collective-permute-start | bytes 3538952 | tf_op jit(solution)/shard_map/ppermute | solution.py:547
  87.1 30.0 %collective-permute-start.13 = (bf16[832,768]{1,0:T(8,128)(2,1)}, bf16[832,768]{1,0:T(8,128)(2,1)}, u32[]{:S(2)}, u32[]{:S(2)}) collective-permute-start(bf16[832,768]{1,0:T(8,128)(2,1)} %get-tuple-element.83), channel_id=1, source_target_pairs={{0,2},{2,0},{1,3},{3,1},{4,6},{6,4},{5,7},{7,5},{8,10},{10,8},{9,1... | collective-permute-start | bytes 3833864 | tf_op jit(solution)/shard_map/ppermute | solution.py:541
  88.5 27.7 %collective-permute-start.14 = (bf16[2,192,1536]{2,1,0:T(8,128)(2,1)S(1)}, bf16[2,192,1536]{2,1,0:T(8,128)(2,1)}, u32[]{:S(2)}, u32[]{:S(2)}) collective-permute-start(bf16[2,192,1536]{2,1,0:T(8,128)(2,1)S(1)} %copy-done.12), channel_id=1, source_target_pairs={{0,8},{4,12},{8,16},{12,20},{16,24},{20,28},{24,0},{28,4},{1,9},{5... | collective-permute-start | bytes 3538952 | tf_op jit(solution)/shard_map/ppermute | solution.py:547
  98.4 31.3 %collective-permute-start.19 = (bf16[832,768]{1,0:T(8,128)(2,1)}, bf16[832,768]{1,0:T(8,128)(2,1)}, u32[]{:S(2)}, u32[]{:S(2)}) collective-permute-start(bf16[832,768]{1,0:T(8,128)(2,1)} %pad_maximum_fusion.5.refs_4_), channel_id=1, source_target_pairs={{0,1},{1,0},{2,3},{3,2},{4,5},{5,4},{6,7},{7,6},{8,9},{9,8},{10,11... | collective-permute-start | bytes 3833864 | tf_op jit(solution)/shard_map/ppermute | solution.py:541
  122.6 32.7 %collective-permute-start.15 = (bf16[832,768]{1,0:T(8,128)(2,1)}, bf16[832,768]{1,0:T(8,128)(2,1)}, u32[]{:S(2)}, u32[]{:S(2)}) collective-permute-start(bf16[832,768]{1,0:T(8,128)(2,1)} %multiply_convert_fusion.refs_0_.refs_6_), channel_id=1, source_target_pairs={{0,1},{1,0},{2,3},{3,2},{4,5},{5,4},{6,7},{7,6},{8,9},{9,8},{10,11... | collective-permute-start | bytes 3833864 | tf_op jit(solution)/shard_map/ppermute | solution.py:541
  123.1 27.5 %collective-permute-start.16 = (bf16[2,192,1536]{2,1,0:T(8,128)(2,1)}, bf16[2,192,1536]{2,1,0:T(8,128)(2,1)}, u32[]{:S(2)}, u32[]{:S(2)}) collective-permute-start(bf16[2,192,1536]{2,1,0:T(8,128)(2,1)} %get-tuple-element.96.refs_8_.refs_12_), channel_id=1, source_target_pairs={{0,8},{4,12},{8,16},{12,20},{16,24},{20,28},{24,0},{28,4},{1,9},{5... | collective-permute-start | bytes 3538952 | tf_op jit(solution)/shard_map/ppermute | solution.py:547
  126.2 29.9 %collective-permute-start.20 = (bf16[832,768]{1,0:T(8,128)(2,1)}, bf16[832,768]{1,0:T(8,128)(2,1)}, u32[]{:S(2)}, u32[]{:S(2)}) collective-permute-start(bf16[832,768]{1,0:T(8,128)(2,1)} %pad_maximum_fusion.5.refs_4_), channel_id=1, source_target_pairs={{0,4},{4,0},{8,12},{12,8},{16,20},{20,16},{24,28},{28,24},{1,5},{5... | collective-permute-start | bytes 3833864 | tf_op jit(solution)/shard_map/ppermute | solution.py:550
  129.7 28.6 %collective-permute-start.21 = (bf16[832,768]{1,0:T(8,128)(2,1)}, bf16[832,768]{1,0:T(8,128)(2,1)}, u32[]{:S(2)}, u32[]{:S(2)}) collective-permute-start(bf16[832,768]{1,0:T(8,128)(2,1)} %collective-permute-done.19.refs_5_), channel_id=1, source_target_pairs={{0,4},{4,0},{8,12},{12,8},{16,20},{20,16},{24,28},{28,24},{1,5},{5... | collective-permute-start | bytes 3833864 | tf_op jit(solution)/shard_map/ppermute | solution.py:550
  129.7 28.6 %collective-permute-start.17 = (bf16[832,768]{1,0:T(8,128)(2,1)}, bf16[832,768]{1,0:T(8,128)(2,1)}, u32[]{:S(2)}, u32[]{:S(2)}) collective-permute-start(bf16[832,768]{1,0:T(8,128)(2,1)} %multiply_convert_fusion.refs_0_.refs_6_), channel_id=1, source_target_pairs={{0,4},{4,0},{8,12},{12,8},{16,20},{20,16},{24,28},{28,24},{1,5},{5... | collective-permute-start | bytes 3833864 | tf_op jit(solution)/shard_map/ppermute | solution.py:550
  155.4 47.3 %collective-permute-start.24 = (bf16[2,192,1536]{2,1,0:T(8,128)(2,1)}, bf16[2,192,1536]{2,1,0:T(8,128)(2,1)}, u32[]{:S(2)}, u32[]{:S(2)}) collective-permute-start(bf16[2,192,1536]{2,1,0:T(8,128)(2,1)} %get-tuple-element.96.refs_8_.refs_12_), channel_id=1, source_target_pairs={{0,24},{4,28},{8,0},{12,4},{16,8},{20,12},{24,16},{28,20},{1,25},{... | collective-permute-start | bytes 3538952 | tf_op jit(solution)/shard_map/ppermute | solution.py:547
  156.1 54.5 %collective-permute-start.23 = (bf16[2,192,1536]{2,1,0:T(8,128)(2,1)}, bf16[2,192,1536]{2,1,0:T(8,128)(2,1)}, u32[]{:S(2)}, u32[]{:S(2)}) collective-permute-start(bf16[2,192,1536]{2,1,0:T(8,128)(2,1)} %collective-permute-done.16.refs_9_.refs_13_), channel_id=1, source_target_pairs={{0,8},{4,12},{8,16},{12,20},{16,24},{20,28},{24,0},{28,4},{1,9},{5... | collective-permute-start | bytes 3538952 | tf_op jit(solution)/shard_map/ppermute | solution.py:547
  198.7 52.2 %collective-permute-start.22 = (bf16[2,192,1536]{2,1,0:T(8,128)(2,1)}, bf16[2,192,1536]{2,1,0:T(8,128)(2,1)}, u32[]{:S(2)}, u32[]{:S(2)}) collective-permute-start(bf16[2,192,1536]{2,1,0:T(8,128)(2,1)} %get-tuple-element.93), channel_id=1, source_target_pairs={{0,8},{4,12},{8,16},{12,20},{16,24},{20,28},{24,0},{28,4},{1,9},{5... | collective-permute-start | bytes 3538952 | tf_op jit(solution)/shard_map/ppermute | solution.py:547
  201.7 58.3 %collective-permute-start.25 = (bf16[2,192,1536]{2,1,0:T(8,128)(2,1)}, bf16[2,192,1536]{2,1,0:T(8,128)(2,1)}, u32[]{:S(2)}, u32[]{:S(2)}) collective-permute-start(bf16[2,192,1536]{2,1,0:T(8,128)(2,1)} %get-tuple-element.101), channel_id=1, source_target_pairs={{0,24},{4,28},{8,0},{12,4},{16,8},{20,12},{24,16},{28,20},{1,25},{... | collective-permute-start | bytes 3538952 | tf_op jit(solution)/shard_map/ppermute | solution.py:547
  265.7 36.0 %collective-permute-start.30 = (bf16[2,192,1536]{2,1,0:T(8,128)(2,1)}, bf16[2,192,1536]{2,1,0:T(8,128)(2,1)}, u32[]{:S(2)}, u32[]{:S(2)}) collective-permute-start(bf16[2,192,1536]{2,1,0:T(8,128)(2,1)} %add_convert_fusion.3), channel_id=1, source_target_pairs={{0,8},{4,12},{8,16},{12,20},{16,24},{20,28},{24,0},{28,4},{1,9},{5... | collective-permute-start | bytes 3538952 | tf_op jit(solution)/shard_map/ppermute | solution.py:547
  283.8 61.4 %collective-permute-start.36 = (bf16[2,192,1536]{2,1,0:T(8,128)(2,1)}, bf16[2,192,1536]{2,1,0:T(8,128)(2,1)}, u32[]{:S(2)}, u32[]{:S(2)}) collective-permute-start(bf16[2,192,1536]{2,1,0:T(8,128)(2,1)} %get-tuple-element.119), channel_id=1, source_target_pairs={{0,8},{4,12},{8,16},{12,20},{16,24},{20,28},{24,0},{28,4},{1,9},{5... | collective-permute-start | bytes 3538952 | tf_op jit(solution)/shard_map/ppermute | solution.py:547
  284.2 98.0 %collective-permute-start.39 = (bf16[2,192,1536]{2,1,0:T(8,128)(2,1)}, bf16[2,192,1536]{2,1,0:T(8,128)(2,1)}, u32[]{:S(2)}, u32[]{:S(2)}) collective-permute-start(bf16[2,192,1536]{2,1,0:T(8,128)(2,1)} %get-tuple-element.132), channel_id=1, source_target_pairs={{0,24},{4,28},{8,0},{12,4},{16,8},{20,12},{24,16},{28,20},{1,25},{... | collective-permute-start | bytes 3538952 | tf_op jit(solution)/shard_map/ppermute | solution.py:547
  285.8 26.5 %collective-permute-start.31 = (bf16[832,384]{1,0:T(8,128)(2,1)}, bf16[832,384]{1,0:T(8,128)(2,1)S(1)}, u32[]{:S(2)}, u32[]{:S(2)}) collective-permute-start(bf16[832,384]{1,0:T(8,128)(2,1)} %get-tuple-element.110), channel_id=1, source_target_pairs={{0,1},{1,0},{2,3},{3,2},{4,5},{5,4},{6,7},{7,6},{8,9},{9,8},{10,11... | collective-permute-start | bytes 1916936 | tf_op jit(solution)/shard_map/ppermute | solution.py:541
  301.2 44.0 %collective-permute-start.35 = (bf16[832,384]{1,0:T(8,128)(2,1)S(1)}, bf16[832,384]{1,0:T(8,128)(2,1)}, u32[]{:S(2)}, u32[]{:S(2)}) collective-permute-start(bf16[832,384]{1,0:T(8,128)(2,1)S(1)} %add_convert_fusion.5), channel_id=1, source_target_pairs={{0,2},{2,0},{1,3},{3,1},{4,6},{6,4},{5,7},{7,5},{8,10},{10,8},{9,1... | collective-permute-start | bytes 1916936 | tf_op jit(solution)/shard_map/ppermute | solution.py:541
  317.0 34.9 %collective-permute-start.37 = (bf16[832,768]{1,0:T(8,128)(2,1)}, bf16[832,768]{1,0:T(8,128)(2,1)}, u32[]{:S(2)}, u32[]{:S(2)}) collective-permute-start(bf16[832,768]{1,0:T(8,128)(2,1)} %combine.5), channel_id=1, source_target_pairs={{0,4},{4,0},{8,12},{12,8},{16,20},{20,16},{24,28},{28,24},{1,5},{5... | collective-permute-start | bytes 3833864 | tf_op jit(solution)/shard_map/ppermute | solution.py:550
  318.0 33.8 %collective-permute-start.33 = (bf16[832,384]{1,0:T(8,128)(2,1)}, bf16[832,384]{1,0:T(8,128)(2,1)S(1)}, u32[]{:S(2)}, u32[]{:S(2)}) collective-permute-start(bf16[832,384]{1,0:T(8,128)(2,1)} %add_convert_fusion.6), channel_id=1, source_target_pairs={{0,2},{2,0},{1,3},{3,1},{4,6},{6,4},{5,7},{7,5},{8,10},{10,8},{9,1... | collective-permute-start | bytes 1916936 | tf_op jit(solution)/shard_map/ppermute | solution.py:541
  347.8 38.8 %collective-permute-start.43 = (bf16[2,192,1536]{2,1,0:T(8,128)(2,1)}, bf16[2,192,1536]{2,1,0:T(8,128)(2,1)}, u32[]{:S(2)}, u32[]{:S(2)}) collective-permute-start(bf16[2,192,1536]{2,1,0:T(8,128)(2,1)} %add_convert_fusion.2), channel_id=1, source_target_pairs={{0,8},{4,12},{8,16},{12,20},{16,24},{20,28},{24,0},{28,4},{1,9},{5... | collective-permute-start | bytes 3538952 | tf_op jit(solution)/shard_map/ppermute | solution.py:547
  356.1 30.5 %collective-permute-start.38 = (bf16[832,768]{1,0:T(8,128)(2,1)}, bf16[832,768]{1,0:T(8,128)(2,1)}, u32[]{:S(2)}, u32[]{:S(2)}) collective-permute-start(bf16[832,768]{1,0:T(8,128)(2,1)} %combine.6), channel_id=1, source_target_pairs={{0,1},{1,0},{2,3},{3,2},{4,5},{5,4},{6,7},{7,6},{8,9},{9,8},{10,11... | collective-permute-start | bytes 3833864 | tf_op jit(solution)/shard_map/ppermute | solution.py:541
  408.4 26.0 %collective-permute-start.47 = (bf16[832,384]{1,0:T(8,128)(2,1)S(1)}, bf16[832,384]{1,0:T(8,128)(2,1)S(1)}, u32[]{:S(2)}, u32[]{:S(2)}) collective-permute-start(bf16[832,384]{1,0:T(8,128)(2,1)S(1)} %dynamic-slice_bitcast_fusion), channel_id=1, source_target_pairs={{0,2},{2,0},{1,3},{3,1},{4,6},{6,4},{5,7},{7,5},{8,10},{10,8},{9,1... | collective-permute-start | bytes 1916936 | tf_op jit(solution)/shard_map/ppermute | solution.py:541
  (69 other events, 714.3 us)
where the time goes:
time: 463 us; the launch traced here: 454 us
  waiting for transfers between devices  174 us (38%)
  Pallas kernels  156 us (34%)
  other arithmetic  49.7 us (11%)
  starting transfers between devices  44 us (10%)
  local copies, waits for them, and re-layouts  29.3 us (6%)
    ppermute x18, waiting for transfers between devices, shift_z(): return lax.ppermute(value, 'dp', pairs)  108 us
    ppermute x17, waiting for transfers between devices, shift(): lax.ppermute(value, axis, [(i, (i + step) % size) for i in range(size)])  60.4 us
    pallas_call x2, Pallas kernels, run_expert(): pl.pallas_call(functools.partial(expert_kernel, index, depth, blocks), gr...  56.2 us
    ppermute x18, starting transfers between devices, shift_z(): return lax.ppermute(value, 'dp', pairs)  26.4 us
    pallas_call x2, Pallas kernels, weight_grad(): pl.pallas_call(functools.partial(weight_grad_kernel, depth), grid_spec=pl...  24 us
    pallas_call x4, Pallas kernels, combine_back(): pl.pallas_call(functools.partial(combine_back_kernel, local, add is not N...  21.8 us
    pallas_call x1, Pallas kernels, attend_back(): pl.pallas_call(functools.partial(attend_back_kernel, seq, gain_at, depth)...  20.8 us
    unnamed x95, local copies, waits for them, and re-layouts  16.4 us
  transfers between devices with their start and end apart: 51, of which 25 were waited for; matrix products, arithmetic and copies ran while one was open for 14% of the time, Pallas kernels for 33%

commit v1 on v0

--- a/solution.py
+++ b/solution.py
@@ -588,7 +588,8 @@
 
     def blocks_of(value, hold=()):
         along = spread(value, "expert")
-        along = along[:1] + [after(part, *hold) for part in along[1:]]
+        if hold:
+            along[0] = after(along[0], *hold)
         return along + [swap_core(part) for part in along]
 
     def full_rows(value):
@@ -611,11 +612,11 @@
     pack_z = place_at(
         [own_pack] + [after(shift_z(own_pack, k), shards) for k in range(1, n_z)], z, n_z
     )
-    pack = place_at(spread(after(pack_z, ids_all), "expert"), exp, n_exp)
     pieces = []
     for e in range(local):
         pieces.append(ring(after(shards[e], pieces[-1][1]) if e else shards[e]))
     last = local - 1
+    pack = place_at(spread(after(pack_z, ids_all), "expert"), exp, n_exp)
 
     pack = after(pack, pieces[0][1], inputs, grad_full)
     other_pack = swap_core(pack)
@@ -687,11 +688,8 @@
     drows, yrows, dchosen = ([r[i] for r in done] for i in (3, 4, 2))
     probs = done[0][5]
 
-    begin_rings(last)
     arrived_zero, down_zero = ring_first(0), ring_down(0)
-    early = ring_middle(0, arrived_zero, rings[last][0])
-    arrived_last, down_last = ring_first(last), ring_down(last)
-    drows[0] = after(drows[0], early, down_zero, rings[last][0])
+    drows[0] = after(drows[0], arrived_zero)
 
     def back_of(b, add=None):
         *parts, more = combine_back(
@@ -707,16 +705,19 @@
         drouter = drouter + more
     from_exp = []
     for k in reversed(range(n_exp)):
-        if k < n_exp - 1:
-            arrived[k][0] = after(arrived[k][0], total[0])
+        arrived[k][0] = after(arrived[k][0], total[0] if k < n_exp - 1 else down_zero)
         total, more = back_of(k, arrived[k])
         drouter = drouter + more
         if k:
             from_exp.append([shift(part, "expert", -k) for part in total])
+        if k == 1:
+            begin_rings(last, total[0])
+            early = ring_middle(0, arrived_zero, total[0])
+    arrived_last, down_last = ring_first(last), ring_down(last)
     ends = [ring_end(0, early, down_zero)]
     dsum, dsum_other = [], []
     for p in range(PARTS):
-        value = (after(total[p], ends[0]) if p == 0 else total[p]).astype(F32)
+        value = (after(total[p], rings[last][0]) if p else total[p]).astype(F32)
         for came in from_exp:
             value = value + came[p].astype(F32)
         dsum.append(value.astype(BF16))
@@ -724,7 +725,7 @@
         for k in range(2, n_heads):
             other = other + shift(dsum[p], "heads", k)
         dsum_other.append(other)
-    dsum_other[-1] = after(dsum_other[-1], arrived_last)
+    dsum_other[0] = after(dsum_other[0], ends[0])
 
     yrows[0] = after(yrows[0], dsum[0])
     y_came = [swap_core(combine(slot_cols, yrows, n_exp + k)) for k in range(n_exp)]
@@ -763,7 +764,7 @@
         y_own = y_own + value.astype(F32)
     y_own = y_own.astype(BF16)
 
-    ends.append(ring_end(last, late, down_last, dsend))
+    ends.append(ring_end(last, late, down_last, dcame))
     dtotal = take(dpack, exp, 1).astype(F32)
     for k in range(1, n_exp):
         came = shift(take(dpack, (exp + k) % n_exp, 1), "expert", k)

time: 463 us -> 459 us (level)
  the two profiles are of different devices: /device:TPU:18 before, /device:TPU:0 now
where the time goes in v1:
time: 459 us; the launch traced here: 450 us
  waiting for transfers between devices  170 us (37%)
  Pallas kernels  155 us (34%)
  other arithmetic  49.3 us (11%)
  starting transfers between devices  43.7 us (10%)
  local copies, waits for them, and re-layouts  30.5 us (7%)
    ppermute x18, waiting for transfers between devices, shift_z(): return lax.ppermute(value, 'dp', pairs)  124 us
    pallas_call x2, Pallas kernels, run_expert(): pl.pallas_call(functools.partial(expert_kernel, index, depth, blocks), gr...  56.3 us
    ppermute x17, waiting for transfers between devices, shift(): lax.ppermute(value, axis, [(i, (i + step) % size) for i in range(size)])  38.7 us
    pallas_call x2, Pallas kernels, weight_grad(): pl.pallas_call(functools.partial(weight_grad_kernel, depth), grid_spec=pl...  23.9 us
    pallas_call x4, Pallas kernels, combine_back(): pl.pallas_call(functools.partial(combine_back_kernel, local, add is not N...  21.7 us
    ppermute x18, starting transfers between devices, shift_z(): return lax.ppermute(value, 'dp', pairs)  21.4 us
    pallas_call x1, Pallas kernels, attend_back(): pl.pallas_call(functools.partial(attend_back_kernel, seq, gain_at, depth)...  20.5 us
    ppermute x17, starting transfers between devices, shift(): lax.ppermute(value, axis, [(i, (i + step) % size) for i in range(size)])  19.8 us
  transfers between devices with their start and end apart: 51, of which 22 were waited for; matrix products, arithmetic and copies ran while one was open for 14% of the time, Pallas kernels for 35%

profile of v1, /device:TPU:0, one launch (start us, length us, event | category | flops | bytes accessed | tf_op | source)
XLA Modules:
  0.0 450.3 jit_solution(3128479828555751361)
XLA Ops:
  39.9 8.3 %collective-permute-done.8 = bf16[4,48,1664]{2,1,0:T(8,128)(2,1)S(1)} collective-permute-done((bf16[4,48,1664]{2,1,0:T(8,128)(2,1)}, bf16[4,48,1664]{2,1,0:T(8,128)(2,1)S(1)}, u32[]{:S(2)}, u32[]{:S(2)}) %collective-permute-start.8) | collective-permute-done | bytes 639008 | tf_op jit(solution)/shard_map/ppermute | solution.py:541
  49.6 14.3 %collective-permute-done.9.refs_9_.refs_13_ = bf16[2,192,1536]{2,1,0:T(8,128)(2,1)} collective-permute-done((bf16[2,192,1536]{2,1,0:T(8,128)(2,1)S(1)}, bf16[2,192,1536]{2,1,0:T(8,128)(2,1)}, u32[]{:S(2)}, u32[]{:S(2)}) %collective-permute-start.9) | collective-permute-done | bytes 1179680 | tf_op jit(solution)/shard_map/ppermute | solution.py:547
  68.8 10.8 %attend.1 = (bf16[832,768]{1,0:T(8,128)(2,1)}, bf16[832,1152]{1,0:T(8,128)(2,1)}, bf16[832,384]{1,0:T(8,128)(2,1)}) custom-call(bf16[832,768]{1,0:T(8,128)(2,1)} %pad_maximum_fusion.3.x_ref, bf16[768,1664]{1,0:T(8,128)(2,1)} %bitcast.131, bf16[768,1664]{1,0:T(8,128)(2,1)} %bitcast.132, bf16[768,1664]{1,0:T(8,128)(2,1)} %bitcast.133), custom_call_target="tpu_custom_call" | custom-call | flops 38338560 | bytes 79872 | tf_op jit(solution)/shard_map/attend/pallas_call | solution.py:96
  79.6 12.6 %collective-permute-done.12.refs_11_.refs_15_ = bf16[2,192,1536]{2,1,0:T(8,128)(2,1)S(1)} collective-permute-done((bf16[2,192,1536]{2,1,0:T(8,128)(2,1)S(1)}, bf16[2,192,1536]{2,1,0:T(8,128)(2,1)S(1)}, u32[]{:S(2)}, u32[]{:S(2)}) %collective-permute-start.12) | collective-permute-done | bytes 1179680 | tf_op jit(solution)/shard_map/ppermute | solution.py:547
  94.4 6.4 %find_slots.1 = (s32[4,2,832]{2,1,0:T(2,128)}, s32[4,832,2]{2,1,0:T(8,128)}) custom-call(s32[2]{0:T(128)} %pad_add_fusion.1.place_ref, s32[4,2,832]{2,1,0:T(2,128)} %pad_add_fusion.ids_ref), custom_call_target="tpu_custom_call" | custom-call | flops 2768896 | bytes 3328 | tf_op jit(solution)/shard_map/find_slots/pallas_call | solution.py:252
  102.9 20.3 %collective-permute-done.14.refs_10_.refs_14_ = bf16[2,192,1536]{2,1,0:T(8,128)(2,1)S(1)} collective-permute-done((bf16[2,192,1536]{2,1,0:T(8,128)(2,1)}, bf16[2,192,1536]{2,1,0:T(8,128)(2,1)S(1)}, u32[]{:S(2)}, u32[]{:S(2)}) %collective-permute-start.14) | collective-permute-done | bytes 1179680 | tf_op jit(solution)/shard_map/ppermute | solution.py:547
  130.9 27.7 %collective-permute-done.15.refs_9_.refs_13_ = bf16[2,192,1536]{2,1,0:T(8,128)(2,1)} collective-permute-done((bf16[2,192,1536]{2,1,0:T(8,128)(2,1)}, bf16[2,192,1536]{2,1,0:T(8,128)(2,1)}, u32[]{:S(2)}, u32[]{:S(2)}) %collective-permute-start.15) | collective-permute-done | bytes 1179680 | tf_op jit(solution)/shard_map/ppermute | solution.py:547
  163.7 28.1 %expert.2 = (bf16[2,4,288,768]{3,2,1,0:T(8,128)(2,1)}, bf16[2,4,288,1536]{3,2,1,0:T(8,128)(2,1)}, f32[4,1,832]{2,1,0:T(1,128)}, bf16[4,288,768]{2,1,0:T(8,128)(2...) custom-call(s32[2]{0:T(128)} %pad_add_fusion.1.place_ref, s32[4,2,832]{2,1,0:T(2,128)} %get-tuple-element.88.slot_ref, ...), custom_call_target="tpu_custom_call" | custom-call | flops 215875584 | bytes 221184 | tf_op jit(solution)/shard_map/expert/pallas_call | solution.py:355
  191.8 11.9 %weight_grad.2 = (bf16[2,192,1536]{2,1,0:T(8,128)(2,1)}, bf16[2,192,1536]{2,1,0:T(8,128)(2,1)}, bf16[2,192,1536]{2,1,0:T(8,128)(2,1)}, bf16[2,192,1536]{2,1,0:T(8,128)(2,1)}) custom-call(s32[2]{0:T(128)} %pad_add_fusion.1.place_ref, bf16[2,4,288,768]{3,2,1,0:T(8,128)(2,1)} %get-tuple-element.93.rows_ref, bf16[2,4,288,1536]{3,2,1,0:T(8,128)(2,1)} %get-tuple-element.94.cols_ref), custom_call_target="tpu_custom_call" | custom-call | flops 84934656 | bytes 239616 | tf_op jit(solution)/shard_map/weight_grad/pallas_call | solution.py:403
  203.7 4.2 collective-permute-start.27
  208.6 5.9 %collective-permute-done.23.refs_10_.refs_14_ = bf16[2,192,1536]{2,1,0:T(8,128)(2,1)} collective-permute-done((bf16[2,192,1536]{2,1,0:T(8,128)(2,1)}, bf16[2,192,1536]{2,1,0:T(8,128)(2,1)}, u32[]{:S(2)}, u32[]{:S(2)}) %collective-permute-start.23) | collective-permute-done | bytes 1179680 | tf_op jit(solution)/shard_map/ppermute | solution.py:547
  214.5 28.3 %expert.3 = (bf16[2,4,288,768]{3,2,1,0:T(8,128)(2,1)}, bf16[2,4,288,1536]{3,2,1,0:T(8,128)(2,1)}, f32[4,1,832]{2,1,0:T(1,128)}, bf16[4,288,768]{2,1,0:T(8,128)(2...) custom-call(s32[2]{0:T(128)} %pad_add_fusion.2.place_ref, s32[4,2,832]{2,1,0:T(2,128)} %get-tuple-element.88.slot_ref, ...), custom_call_target="tpu_custom_call" | custom-call | flops 215875584 | bytes 221184 | tf_op jit(solution)/shard_map/expert/pallas_call | solution.py:355
  242.7 5.2 %combine_back.5 = (bf16[832,384]{1,0:T(8,128)(2,1)}, bf16[832,384]{1,0:T(8,128)(2,1)}, f32[8,768]{1,0:T(8,128)}) custom-call(s32[2]{0:T(128)} %pad_add_fusion.1.place_ref, s32[4,832,2]{2,1,0:T(8,128)} %get-tuple-element.86.slot_ref, bf16[4,288,768]{2,1,0:T(8,128)(2,1)} %get-tuple-element.96.refs_0_, bf16[4,288,768]{2,1,0:T(8,128)(2,1)} %get-tuple-element.99.refs_1_, ...), custom_call_target="tpu_custom_call" | custom-call | flops 11501568 | bytes 73728 | tf_op jit(solution)/shard_map/combine_back/pallas_call | solution.py:493
  248.5 5.3 %combine_back.4 = (bf16[832,384]{1,0:T(8,128)(2,1)}, bf16[832,384]{1,0:T(8,128)(2,1)}, f32[8,768]{1,0:T(8,128)}) custom-call(s32[2]{0:T(128)} %pad_add_fusion.1.place_ref, s32[4,832,2]{2,1,0:T(8,128)} %get-tuple-element.86.slot_ref, bf16[4,288,768]{2,1,0:T(8,128)(2,1)} %get-tuple-element.96.refs_0_, bf16[4,288,768]{2,1,0:T(8,128)(2,1)} %get-tuple-element.99.refs_1_, ...), custom_call_target="tpu_custom_call" | custom-call | flops 11501568 | bytes 73728 | tf_op jit(solution)/shard_map/combine_back/pallas_call | solution.py:493
  254.3 10.2 %collective-permute-done.27 = bf16[2,192,1536]{2,1,0:T(8,128)(2,1)} collective-permute-done((bf16[2,192,1536]{2,1,0:T(8,128)(2,1)}, bf16[2,192,1536]{2,1,0:T(8,128)(2,1)}, u32[]{:S(2)}, u32[]{:S(2)}) %collective-permute-start.27) | collective-permute-done | bytes 1179680 | tf_op jit(solution)/shard_map/ppermute | solution.py:547
  266.2 5.6 %combine_back.6 = (bf16[832,384]{1,0:T(8,128)(2,1)}, bf16[832,384]{1,0:T(8,128)(2,1)}, f32[8,768]{1,0:T(8,128)}) custom-call(s32[2]{0:T(128)} %pad_add_fusion.1.place_ref, s32[4,832,2]{2,1,0:T(8,128)} %get-tuple-element.86.slot_ref, bf16[4,288,768]{2,1,0:T(8,128)(2,1)} %get-tuple-element.96.refs_0_, bf16[4,288,768]{2,1,0:T(8,128)(2,1)} %get-tuple-element.99.refs_1_, ...), custom_call_target="tpu_custom_call" | custom-call | flops 11501568 | bytes 73728 | tf_op jit(solution)/shard_map/combine_back/pallas_call | solution.py:493
  279.0 5.6 %combine_back.7 = (bf16[832,384]{1,0:T(8,128)(2,1)}, bf16[832,384]{1,0:T(8,128)(2,1)}, f32[8,768]{1,0:T(8,128)}) custom-call(s32[2]{0:T(128)} %pad_add_fusion.1.place_ref, s32[4,832,2]{2,1,0:T(8,128)} %get-tuple-element.86.slot_ref, bf16[4,288,768]{2,1,0:T(8,128)(2,1)} %get-tuple-element.96.refs_0_, bf16[4,288,768]{2,1,0:T(8,128)(2,1)} %get-tuple-element.99.refs_1_, ...), custom_call_target="tpu_custom_call" | custom-call | flops 11501568 | bytes 73728 | tf_op jit(solution)/shard_map/combine_back/pallas_call | solution.py:493
  284.6 12.1 %weight_grad.3 = (bf16[2,192,1536]{2,1,0:T(8,128)(2,1)}, bf16[2,192,1536]{2,1,0:T(8,128)(2,1)}, bf16[2,192,1536]{2,1,0:T(8,128)(2,1)}, bf16[2,192,1536]{2,1,0:T(8,128)(2,1)}) custom-call(s32[2]{0:T(128)} %pad_add_fusion.2.place_ref, bf16[2,4,288,768]{3,2,1,0:T(8,128)(2,1)} %get-tuple-element.119.rows_ref, bf16[2,4,288,1536]{3,2,1,0:T(8,128)(2,1)} %get-tuple-element.120.cols_ref), custom_call_target="tpu_custom_call" | custom-call | flops 84934656 | bytes 239616 | tf_op jit(solution)/shard_map/weight_grad/pallas_call | solution.py:403
  316.7 14.4 %collective-permute-done.32 = bf16[832,384]{1,0:T(8,128)(2,1)S(1)} collective-permute-done((bf16[832,384]{1,0:T(8,128)(2,1)S(1)}, bf16[832,384]{1,0:T(8,128)(2,1)S(1)}, u32[]{:S(2)}, u32[]{:S(2)}) %collective-permute-start.32) | collective-permute-done | bytes 639008 | tf_op jit(solution)/shard_map/ppermute | solution.py:541
  333.5 4.2 combine.6
  343.5 20.5 %attend_back.1 = (bf16[2,832,384]{2,1,0:T(8,128)(2,1)}, f32[832,128]{1,0:T(8,128)}, bf16[384,1664]{1,0:T(8,128)(2,1)}, bf16[384,1664]{1,0:T(8,128)(2,1)}) custom-call(s32[1]{0:T(128)} %bitcast.35.core_ref, bf16[832,768]{1,0:T(8,128)(2,1)} %pad_maximum_fusion.3.x_ref, f32[1,768]{1,0:T(1,128)} %copy.165.gain_ref, ...), custom_call_target="tpu_custom_call" | custom-call | flops 107347968 | bytes 119808 | tf_op jit(solution)/shard_map/attend_back/pallas_call | solution.py:193
  364.0 4.5 %collective-permute-done.38 = bf16[832,768]{1,0:T(8,128)(2,1)} collective-permute-done((bf16[832,768]{1,0:T(8,128)(2,1)}, bf16[832,768]{1,0:T(8,128)(2,1)}, u32[]{:S(2)}, u32[]{:S(2)}) %collective-permute-start.38) | collective-permute-done | bytes 1277984 | tf_op jit(solution)/shard_map/ppermute | solution.py:541
  385.3 21.7 %collective-permute-done.43 = bf16[2,192,1536]{2,1,0:T(8,128)(2,1)S(1)} collective-permute-done((bf16[2,192,1536]{2,1,0:T(8,128)(2,1)}, bf16[2,192,1536]{2,1,0:T(8,128)(2,1)S(1)}, u32[]{:S(2)}, u32[]{:S(2)}) %collective-permute-start.43) | collective-permute-done | bytes 1179680 | tf_op jit(solution)/shard_map/ppermute | solution.py:547
  421.2 5.6 %collective-permute-done.45 = bf16[48,1664]{1,0:T(8,128)(2,1)S(1)} collective-permute-done((bf16[48,1664]{1,0:T(8,128)(2,1)S(1)}, bf16[48,1664]{1,0:T(8,128)(2,1)S(1)}, u32[]{:S(2)}, u32[]{:S(2)}) %collective-permute-start.45) | collective-permute-done | bytes 159776 | tf_op jit(solution)/shard_map/ppermute | solution.py:547
  (267 shorter events, 155.0 us)
Async XLA Ops:
  34.4 29.5 %collective-permute-start.9 = (bf16[2,192,1536]{2,1,0:T(8,128)(2,1)S(1)}, bf16[2,192,1536]{2,1,0:T(8,128)(2,1)}, u32[]{:S(2)}, u32[]{:S(2)}) collective-permute-start(bf16[2,192,1536]{2,1,0:T(8,128)(2,1)S(1)} %get-tuple-element.212.refs_8_.refs_12_), channel_id=1, source_target_pairs={{0,8},{4,12},{8,16},{12,20},{16,24},{20,28},{24,0},{28,4},{1,9},{5... | collective-permute-start | bytes 3538952 | tf_op jit(solution)/shard_map/ppermute | solution.py:547
  63.9 28.4 %collective-permute-start.12 = (bf16[2,192,1536]{2,1,0:T(8,128)(2,1)S(1)}, bf16[2,192,1536]{2,1,0:T(8,128)(2,1)S(1)}, u32[]{:S(2)}, u32[]{:S(2)}) collective-permute-start(bf16[2,192,1536]{2,1,0:T(8,128)(2,1)S(1)} %get-tuple-element.212.refs_8_.refs_12_), channel_id=1, source_target_pairs={{0,24},{4,28},{8,0},{12,4},{16,8},{20,12},{24,16},{28,20},{1,25},{... | collective-permute-start | bytes 3538952 | tf_op jit(solution)/shard_map/ppermute | solution.py:547
  93.3 30.0 %collective-permute-start.13 = (bf16[832,768]{1,0:T(8,128)(2,1)}, bf16[832,768]{1,0:T(8,128)(2,1)}, u32[]{:S(2)}, u32[]{:S(2)}) collective-permute-start(bf16[832,768]{1,0:T(8,128)(2,1)} %get-tuple-element.85), channel_id=1, source_target_pairs={{0,2},{2,0},{1,3},{3,1},{4,6},{6,4},{5,7},{7,5},{8,10},{10,8},{9,1... | collective-permute-start | bytes 3833864 | tf_op jit(solution)/shard_map/ppermute | solution.py:541
  93.8 29.3 %collective-permute-start.14 = (bf16[2,192,1536]{2,1,0:T(8,128)(2,1)}, bf16[2,192,1536]{2,1,0:T(8,128)(2,1)S(1)}, u32[]{:S(2)}, u32[]{:S(2)}) collective-permute-start(bf16[2,192,1536]{2,1,0:T(8,128)(2,1)} %collective-permute-done.9.refs_9_.refs_13_), channel_id=1, source_target_pairs={{0,8},{4,12},{8,16},{12,20},{16,24},{20,28},{24,0},{28,4},{1,9},{5... | collective-permute-start | bytes 3538952 | tf_op jit(solution)/shard_map/ppermute | solution.py:547
  100.8 29.7 %collective-permute-start.19 = (bf16[832,768]{1,0:T(8,128)(2,1)}, bf16[832,768]{1,0:T(8,128)(2,1)}, u32[]{:S(2)}, u32[]{:S(2)}) collective-permute-start(bf16[832,768]{1,0:T(8,128)(2,1)} %pad_maximum_fusion.5.refs_4_), channel_id=1, source_target_pairs={{0,1},{1,0},{2,3},{3,2},{4,5},{5,4},{6,7},{7,6},{8,9},{9,8},{10,11... | collective-permute-start | bytes 3833864 | tf_op jit(solution)/shard_map/ppermute | solution.py:541
  129.7 28.8 %collective-permute-start.16 = (bf16[832,768]{1,0:T(8,128)(2,1)}, bf16[832,768]{1,0:T(8,128)(2,1)}, u32[]{:S(2)}, u32[]{:S(2)}) collective-permute-start(bf16[832,768]{1,0:T(8,128)(2,1)} %multiply_convert_fusion.refs_0_.refs_6_), channel_id=1, source_target_pairs={{0,1},{1,0},{2,3},{3,2},{4,5},{5,4},{6,7},{7,6},{8,9},{9,8},{10,11... | collective-permute-start | bytes 3833864 | tf_op jit(solution)/shard_map/ppermute | solution.py:541
  130.3 28.2 %collective-permute-start.15 = (bf16[2,192,1536]{2,1,0:T(8,128)(2,1)}, bf16[2,192,1536]{2,1,0:T(8,128)(2,1)}, u32[]{:S(2)}, u32[]{:S(2)}) collective-permute-start(bf16[2,192,1536]{2,1,0:T(8,128)(2,1)} %get-tuple-element.98.refs_8_.refs_12_), channel_id=1, source_target_pairs={{0,8},{4,12},{8,16},{12,20},{16,24},{20,28},{24,0},{28,4},{1,9},{5... | collective-permute-start | bytes 3538952 | tf_op jit(solution)/shard_map/ppermute | solution.py:547
  130.3 31.9 %collective-permute-start.20 = (bf16[832,768]{1,0:T(8,128)(2,1)}, bf16[832,768]{1,0:T(8,128)(2,1)}, u32[]{:S(2)}, u32[]{:S(2)}) collective-permute-start(bf16[832,768]{1,0:T(8,128)(2,1)} %pad_maximum_fusion.5.refs_4_), channel_id=1, source_target_pairs={{0,4},{4,0},{8,12},{12,8},{16,20},{20,16},{24,28},{28,24},{1,5},{5... | collective-permute-start | bytes 3833864 | tf_op jit(solution)/shard_map/ppermute | solution.py:550
  130.6 31.9 %collective-permute-start.21 = (bf16[832,768]{1,0:T(8,128)(2,1)}, bf16[832,768]{1,0:T(8,128)(2,1)}, u32[]{:S(2)}, u32[]{:S(2)}) collective-permute-start(bf16[832,768]{1,0:T(8,128)(2,1)} %collective-permute-done.19.refs_5_), channel_id=1, source_target_pairs={{0,4},{4,0},{8,12},{12,8},{16,20},{20,16},{24,28},{28,24},{1,5},{5... | collective-permute-start | bytes 3833864 | tf_op jit(solution)/shard_map/ppermute | solution.py:550
  159.1 49.5 %collective-permute-start.24 = (bf16[2,192,1536]{2,1,0:T(8,128)(2,1)}, bf16[2,192,1536]{2,1,0:T(8,128)(2,1)}, u32[]{:S(2)}, u32[]{:S(2)}) collective-permute-start(bf16[2,192,1536]{2,1,0:T(8,128)(2,1)} %get-tuple-element.98.refs_8_.refs_12_), channel_id=1, source_target_pairs={{0,24},{4,28},{8,0},{12,4},{16,8},{20,12},{24,16},{28,20},{1,25},{... | collective-permute-start | bytes 3538952 | tf_op jit(solution)/shard_map/ppermute | solution.py:547
  162.2 52.2 %collective-permute-start.23 = (bf16[2,192,1536]{2,1,0:T(8,128)(2,1)}, bf16[2,192,1536]{2,1,0:T(8,128)(2,1)}, u32[]{:S(2)}, u32[]{:S(2)}) collective-permute-start(bf16[2,192,1536]{2,1,0:T(8,128)(2,1)} %collective-permute-done.15.refs_9_.refs_13_), channel_id=1, source_target_pairs={{0,8},{4,12},{8,16},{12,20},{16,24},{20,28},{24,0},{28,4},{1,9},{5... | collective-permute-start | bytes 3538952 | tf_op jit(solution)/shard_map/ppermute | solution.py:547
  203.7 39.0 %collective-permute-start.22 = (bf16[2,192,1536]{2,1,0:T(8,128)(2,1)}, bf16[2,192,1536]{2,1,0:T(8,128)(2,1)}, u32[]{:S(2)}, u32[]{:S(2)}) collective-permute-start(bf16[2,192,1536]{2,1,0:T(8,128)(2,1)} %get-tuple-element.95), channel_id=1, source_target_pairs={{0,8},{4,12},{8,16},{12,20},{16,24},{20,28},{24,0},{28,4},{1,9},{5... | collective-permute-start | bytes 3538952 | tf_op jit(solution)/shard_map/ppermute | solution.py:547
  203.7 60.8 %collective-permute-start.27 = (bf16[2,192,1536]{2,1,0:T(8,128)(2,1)}, bf16[2,192,1536]{2,1,0:T(8,128)(2,1)}, u32[]{:S(2)}, u32[]{:S(2)}) collective-permute-start(bf16[2,192,1536]{2,1,0:T(8,128)(2,1)} %get-tuple-element.105), channel_id=1, source_target_pairs={{0,24},{4,28},{8,0},{12,4},{16,8},{20,12},{24,16},{28,20},{1,25},{... | collective-permute-start | bytes 3538952 | tf_op jit(solution)/shard_map/ppermute | solution.py:547
  271.8 29.2 %collective-permute-start.34 = (bf16[832,384]{1,0:T(8,128)(2,1)}, bf16[832,384]{1,0:T(8,128)(2,1)}, u32[]{:S(2)}, u32[]{:S(2)}) collective-permute-start(bf16[832,384]{1,0:T(8,128)(2,1)} %get-tuple-element.123), channel_id=1, source_target_pairs={{0,1},{1,0},{2,3},{3,2},{4,5},{5,4},{6,7},{7,6},{8,9},{9,8},{10,11... | collective-permute-start | bytes 1916936 | tf_op jit(solution)/shard_map/ppermute | solution.py:541
  274.9 38.3 %collective-permute-start.33 = (bf16[2,192,1536]{2,1,0:T(8,128)(2,1)}, bf16[2,192,1536]{2,1,0:T(8,128)(2,1)}, u32[]{:S(2)}, u32[]{:S(2)}) collective-permute-start(bf16[2,192,1536]{2,1,0:T(8,128)(2,1)} %add_convert_fusion.3), channel_id=1, source_target_pairs={{0,8},{4,12},{8,16},{12,20},{16,24},{20,28},{24,0},{28,4},{1,9},{5... | collective-permute-start | bytes 3538952 | tf_op jit(solution)/shard_map/ppermute | solution.py:547
  276.7 27.2 %collective-permute-start.30 = (bf16[832,384]{1,0:T(8,128)(2,1)}, bf16[832,384]{1,0:T(8,128)(2,1)}, u32[]{:S(2)}, u32[]{:S(2)}) collective-permute-start(bf16[832,384]{1,0:T(8,128)(2,1)} %get-tuple-element.108), channel_id=1, source_target_pairs={{0,1},{1,0},{2,3},{3,2},{4,5},{5,4},{6,7},{7,6},{8,9},{9,8},{10,11... | collective-permute-start | bytes 1916936 | tf_op jit(solution)/shard_map/ppermute | solution.py:541
  296.9 44.0 %collective-permute-start.36 = (bf16[2,192,1536]{2,1,0:T(8,128)(2,1)}, bf16[2,192,1536]{2,1,0:T(8,128)(2,1)}, u32[]{:S(2)}, u32[]{:S(2)}) collective-permute-start(bf16[2,192,1536]{2,1,0:T(8,128)(2,1)} %get-tuple-element.124), channel_id=1, source_target_pairs={{0,8},{4,12},{8,16},{12,20},{16,24},{20,28},{24,0},{28,4},{1,9},{5... | collective-permute-start | bytes 3538952 | tf_op jit(solution)/shard_map/ppermute | solution.py:547
  297.6 66.4 %collective-permute-start.39 = (bf16[2,192,1536]{2,1,0:T(8,128)(2,1)}, bf16[2,192,1536]{2,1,0:T(8,128)(2,1)}, u32[]{:S(2)}, u32[]{:S(2)}) collective-permute-start(bf16[2,192,1536]{2,1,0:T(8,128)(2,1)} %get-tuple-element.136), channel_id=1, source_target_pairs={{0,24},{4,28},{8,0},{12,4},{16,8},{20,12},{24,16},{28,20},{1,25},{... | collective-permute-start | bytes 3538952 | tf_op jit(solution)/shard_map/ppermute | solution.py:547
  302.4 28.8 %collective-permute-start.35 = (bf16[832,384]{1,0:T(8,128)(2,1)S(1)}, bf16[832,384]{1,0:T(8,128)(2,1)S(1)}, u32[]{:S(2)}, u32[]{:S(2)}) collective-permute-start(bf16[832,384]{1,0:T(8,128)(2,1)S(1)} %add_convert_fusion.5), channel_id=1, source_target_pairs={{0,2},{2,0},{1,3},{3,1},{4,6},{6,4},{5,7},{7,5},{8,10},{10,8},{9,1... | collective-permute-start | bytes 1916936 | tf_op jit(solution)/shard_map/ppermute | solution.py:541
  337.7 30.8 %collective-permute-start.38 = (bf16[832,768]{1,0:T(8,128)(2,1)}, bf16[832,768]{1,0:T(8,128)(2,1)}, u32[]{:S(2)}, u32[]{:S(2)}) collective-permute-start(bf16[832,768]{1,0:T(8,128)(2,1)} %combine.6), channel_id=1, source_target_pairs={{0,1},{1,0},{2,3},{3,2},{4,5},{5,4},{6,7},{7,6},{8,9},{9,8},{10,11... | collective-permute-start | bytes 3833864 | tf_op jit(solution)/shard_map/ppermute | solution.py:541
  368.7 38.3 %collective-permute-start.43 = (bf16[2,192,1536]{2,1,0:T(8,128)(2,1)}, bf16[2,192,1536]{2,1,0:T(8,128)(2,1)S(1)}, u32[]{:S(2)}, u32[]{:S(2)}) collective-permute-start(bf16[2,192,1536]{2,1,0:T(8,128)(2,1)} %add_convert_fusion.2), channel_id=1, source_target_pairs={{0,8},{4,12},{8,16},{12,20},{16,24},{20,28},{24,0},{28,4},{1,9},{5... | collective-permute-start | bytes 3538952 | tf_op jit(solution)/shard_map/ppermute | solution.py:547
  373.6 53.3 %collective-permute-start.48 = (f32[2,832]{0,1:T(8,128)}, f32[2,832]{0,1:T(8,128)}, u32[]{:S(2)}, u32[]{:S(2)}) collective-permute-start(f32[2,832]{0,1:T(8,128)} %slice_bitcast_fusion.2), channel_id=1, source_target_pairs={{0,2},{2,0},{1,3},{3,1},{4,6},{6,4},{5,7},{7,5},{8,10},{10,8},{9,1... | collective-permute-start | bytes 19976 | tf_op jit(solution)/shard_map/ppermute | solution.py:541
  377.2 31.5 %collective-permute-start.42 = (bf16[4,48,1664]{2,1,0:T(8,128)(2,1)S(1)}, bf16[4,48,1664]{2,1,0:T(8,128)(2,1)}, u32[]{:S(2)}, u32[]{:S(2)}) collective-permute-start(bf16[4,48,1664]{2,1,0:T(8,128)(2,1)S(1)} %dynamic-slice_bitcast_fusion.1), channel_id=1, source_target_pairs={{0,1},{1,0},{2,3},{3,2},{4,5},{5,4},{6,7},{7,6},{8,9},{9,8},{10,11... | collective-permute-start | bytes 1916936 | tf_op jit(solution)/shard_map/ppermute | solution.py:541
  378.5 51.3 %collective-permute-start.47 = (bf16[832,384]{1,0:T(8,128)(2,1)S(1)}, bf16[832,384]{1,0:T(8,128)(2,1)S(1)}, u32[]{:S(2)}, u32[]{:S(2)}) collective-permute-start(bf16[832,384]{1,0:T(8,128)(2,1)S(1)} %dynamic-slice_bitcast_fusion), channel_id=1, source_target_pairs={{0,2},{2,0},{1,3},{3,1},{4,6},{6,4},{5,7},{7,5},{8,10},{10,8},{9,1... | collective-permute-start | bytes 1916936 | tf_op jit(solution)/shard_map/ppermute | solution.py:541
  (65 other events, 708.9 us)

commit v2 on v1

--- a/solution.py
+++ b/solution.py
@@ -653,9 +653,9 @@
     def ring_first(e):
         return shift_z(rings[e][-ways_up % n_z], 1)
 
-    def ring_down(e):
+    def ring_down(e, *hold):
         chunks = rings[e]
-        downward = chunks[ways_down]
+        downward = after(chunks[ways_down], *hold)
         for k in range(ways_down - 1, 0, -1):
             downward = (shift_z(downward, -1).astype(F32) + chunks[k].astype(F32)).astype(BF16)
         return shift_z(downward, -1)
@@ -711,12 +711,12 @@
         if k:
             from_exp.append([shift(part, "expert", -k) for part in total])
         if k == 1:
-            begin_rings(last, total[0])
             early = ring_middle(0, arrived_zero, total[0])
-    arrived_last, down_last = ring_first(last), ring_down(last)
     ends = [ring_end(0, early, down_zero)]
     dsum, dsum_other = [], []
     for p in range(PARTS):
+        if p == 1:
+            begin_rings(last, dsum[0])
         value = (after(total[p], rings[last][0]) if p else total[p]).astype(F32)
         for came in from_exp:
             value = value + came[p].astype(F32)
@@ -725,6 +725,7 @@
         for k in range(2, n_heads):
             other = other + shift(dsum[p], "heads", k)
         dsum_other.append(other)
+    arrived_last, down_last = ring_first(last), ring_down(last)
     dsum_other[0] = after(dsum_other[0], ends[0])
 
     yrows[0] = after(yrows[0], dsum[0])
@@ -744,7 +745,7 @@
         - unit_two * jnp.mean(scaled * unit_two, axis=-1, keepdims=True)
     )
     late = ring_middle(last, arrived_last, dsum_other[-1])
-    datt = after(dmiddle.astype(BF16), late, *y_came)
+    datt = after(dmiddle.astype(BF16), *y_came)
 
     dside = jnp.concatenate(
         [drouter, jnp.zeros((1, model), F32), grad_gain_two[None, :],
@@ -764,15 +765,23 @@
         y_own = y_own + value.astype(F32)
     y_own = y_own.astype(BF16)
 
-    ends.append(ring_end(last, late, down_last, dcame))
     dtotal = take(dpack, exp, 1).astype(F32)
     for k in range(1, n_exp):
         came = shift(take(dpack, (exp + k) % n_exp, 1), "expert", k)
-        dtotal = dtotal + after(came, ends[last]).astype(F32)
+        dtotal = dtotal + came.astype(F32)
     dpack = dtotal.astype(BF16)
+
+    came = [shift_z(take(dpack, (z + k) % n_z), k) for k in range(1, n_z)]
     dtotal = take(dpack, z).astype(F32)
-    for k in range(1, n_z):
-        dtotal = dtotal + shift_z(take(dpack, (z + k) % n_z), k).astype(F32)
+    for value in came:
+        dtotal = dtotal + value.astype(F32)
+
+    ends.append(ring_end(last, late, down_last, came[0]))
+    stacked = jnp.stack(ends).reshape(local, 2, CORES, part_rows, hidden_width)
+    other = swap_core(take(stacked, 1 - core, 2).astype(BF16)).astype(F32)
+    own = take(stacked, core, 2)
+    joined = jnp.concatenate([jnp.where(low, own, other), jnp.where(low, other, own)], axis=0)
+    grads = joined.transpose(1, 2, 0, 3)
     dside = dtotal[:, 4 * width :]
     over_heads = dside[:, : expert_count + 1].T
     summed = over_heads
@@ -791,8 +800,8 @@
     sums_total = sums
     for k in range(1, n_heads):
         came = shift(take(dnorm, (head + k) % n_heads), "heads", k)
-        dn_own = dn_own + after(came, dtotal).astype(F32)
-        sums_total = sums_total + after(shift(sums, "heads", k), dtotal)
+        dn_own = dn_own + after(came, dpack).astype(F32)
+        sums_total = sums_total + after(shift(sums, "heads", k), dpack)
     unit_one, scale_one = norm_parts(inputs.astype(F32))
     grad_in = own_half(dmiddle) + scale_one * (
         dn_own * own_half(gain_one)
@@ -804,14 +813,8 @@
     for k in range(1, n_heads):
         there = (head + k) % n_heads
         part_y = lax.dynamic_slice_in_dim(y_own, there * half_width, half_width, 1)
-        y_total = y_total + after(shift(part_y, "heads", k), dtotal).astype(F32)
+        y_total = y_total + after(shift(part_y, "heads", k), dpack).astype(F32)
     block_out = own_half(middle) + y_total
-
-    stacked = jnp.stack(ends).reshape(local, 2, CORES, part_rows, hidden_width)
-    other = swap_core(take(stacked, 1 - core, 2).astype(BF16)).astype(F32)
-    own = take(stacked, core, 2)
-    joined = jnp.concatenate([jnp.where(low, own, other), jnp.where(low, other, own)], axis=0)
-    grads = joined.transpose(1, 2, 0, 3)
 
     return (
         cut(block_out),

time: 459 us -> 444 us (0.967)
  waiting for transfers between devices: 170 us -> 150 us
    ppermute x18, waiting for transfers between devices: 124 us -> 96.2 us  [shift_z(): return lax.ppermute(value, 'dp', pairs)]
    ppermute x17, waiting for transfers between devices: 38.7 us -> 49.1 us  [shift(): lax.ppermute(value, axis, [(i, (i + step) % size) for i in range(size)])]
  transfers between devices with their start and end apart: 51 -> 51, of which waited for: 22 -> 22; matrix products, arithmetic and copies ran while one was open for 14% -> 15% of each run, Pallas kernels for 35% -> 36%
where the time goes in v2:
time: 444 us; the launch traced here: 435 us
  Pallas kernels  155 us (35%)
  waiting for transfers between devices  150 us (34%)
  other arithmetic  49 us (11%)
  starting transfers between devices  47.3 us (11%)
  local copies, waits for them, and re-layouts  32 us (7%)
    ppermute x18, waiting for transfers between devices, shift_z(): return lax.ppermute(value, 'dp', pairs)  96.2 us
    pallas_call x2, Pallas kernels, run_expert(): pl.pallas_call(functools.partial(expert_kernel, index, depth, blocks), gr...  56.3 us
    ppermute x17, waiting for transfers between devices, shift(): lax.ppermute(value, axis, [(i, (i + step) % size) for i in range(size)])  49.1 us
    ppermute x18, starting transfers between devices, shift_z(): return lax.ppermute(value, 'dp', pairs)  25 us
    pallas_call x2, Pallas kernels, weight_grad(): pl.pallas_call(functools.partial(weight_grad_kernel, depth), grid_spec=pl...  23.8 us
    pallas_call x4, Pallas kernels, combine_back(): pl.pallas_call(functools.partial(combine_back_kernel, local, add is not N...  21.8 us
    pallas_call x1, Pallas kernels, attend_back(): pl.pallas_call(functools.partial(attend_back_kernel, seq, gain_at, depth)...  20.5 us
    ppermute x17, starting transfers between devices, shift(): lax.ppermute(value, axis, [(i, (i + step) % size) for i in range(size)])  19.7 us
  transfers between devices with their start and end apart: 51, of which 22 were waited for; matrix products, arithmetic and copies ran while one was open for 15% of the time, Pallas kernels for 36%

profile of v2, /device:TPU:0, one launch (start us, length us, event | category | flops | bytes accessed | tf_op | source)
XLA Modules:
  0.0 435.0 jit_solution(7562580307815099609)
XLA Ops:
  39.9 8.3 %collective-permute-done.8 = bf16[4,48,1664]{2,1,0:T(8,128)(2,1)S(1)} collective-permute-done((bf16[4,48,1664]{2,1,0:T(8,128)(2,1)}, bf16[4,48,1664]{2,1,0:T(8,128)(2,1)S(1)}, u32[]{:S(2)}, u32[]{:S(2)}) %collective-permute-start.8) | collective-permute-done | bytes 639008 | tf_op jit(solution)/shard_map/ppermute | solution.py:541
  49.6 14.3 %collective-permute-done.9.refs_9_.refs_13_ = bf16[2,192,1536]{2,1,0:T(8,128)(2,1)} collective-permute-done((bf16[2,192,1536]{2,1,0:T(8,128)(2,1)S(1)}, bf16[2,192,1536]{2,1,0:T(8,128)(2,1)}, u32[]{:S(2)}, u32[]{:S(2)}) %collective-permute-start.9) | collective-permute-done | bytes 1179680 | tf_op jit(solution)/shard_map/ppermute | solution.py:547
  68.8 10.8 %attend.1 = (bf16[832,768]{1,0:T(8,128)(2,1)}, bf16[832,1152]{1,0:T(8,128)(2,1)}, bf16[832,384]{1,0:T(8,128)(2,1)}) custom-call(bf16[832,768]{1,0:T(8,128)(2,1)} %pad_maximum_fusion.3.x_ref, bf16[768,1664]{1,0:T(8,128)(2,1)} %bitcast.131, bf16[768,1664]{1,0:T(8,128)(2,1)} %bitcast.132, bf16[768,1664]{1,0:T(8,128)(2,1)} %bitcast.133), custom_call_target="tpu_custom_call" | custom-call | flops 38338560 | bytes 79872 | tf_op jit(solution)/shard_map/attend/pallas_call | solution.py:96
  79.6 12.6 %collective-permute-done.12.refs_11_.refs_15_ = bf16[2,192,1536]{2,1,0:T(8,128)(2,1)S(1)} collective-permute-done((bf16[2,192,1536]{2,1,0:T(8,128)(2,1)S(1)}, bf16[2,192,1536]{2,1,0:T(8,128)(2,1)S(1)}, u32[]{:S(2)}, u32[]{:S(2)}) %collective-permute-start.12) | collective-permute-done | bytes 1179680 | tf_op jit(solution)/shard_map/ppermute | solution.py:547
  94.4 6.4 %find_slots.1 = (s32[4,2,832]{2,1,0:T(2,128)}, s32[4,832,2]{2,1,0:T(8,128)}) custom-call(s32[2]{0:T(128)} %pad_add_fusion.1.place_ref, s32[4,2,832]{2,1,0:T(2,128)} %pad_add_fusion.ids_ref), custom_call_target="tpu_custom_call" | custom-call | flops 2768896 | bytes 3328 | tf_op jit(solution)/shard_map/find_slots/pallas_call | solution.py:252
  102.9 20.3 %collective-permute-done.14.refs_10_.refs_14_ = bf16[2,192,1536]{2,1,0:T(8,128)(2,1)S(1)} collective-permute-done((bf16[2,192,1536]{2,1,0:T(8,128)(2,1)}, bf16[2,192,1536]{2,1,0:T(8,128)(2,1)S(1)}, u32[]{:S(2)}, u32[]{:S(2)}) %collective-permute-start.14) | collective-permute-done | bytes 1179680 | tf_op jit(solution)/shard_map/ppermute | solution.py:547
  130.9 27.7 %collective-permute-done.15.refs_9_.refs_13_ = bf16[2,192,1536]{2,1,0:T(8,128)(2,1)} collective-permute-done((bf16[2,192,1536]{2,1,0:T(8,128)(2,1)}, bf16[2,192,1536]{2,1,0:T(8,128)(2,1)}, u32[]{:S(2)}, u32[]{:S(2)}) %collective-permute-start.15) | collective-permute-done | bytes 1179680 | tf_op jit(solution)/shard_map/ppermute | solution.py:547
  163.7 28.1 %expert.2 = (bf16[2,4,288,768]{3,2,1,0:T(8,128)(2,1)}, bf16[2,4,288,1536]{3,2,1,0:T(8,128)(2,1)}, f32[4,1,832]{2,1,0:T(1,128)}, bf16[4,288,768]{2,1,0:T(8,128)(2...) custom-call(s32[2]{0:T(128)} %pad_add_fusion.1.place_ref, s32[4,2,832]{2,1,0:T(2,128)} %get-tuple-element.87.slot_ref, ...), custom_call_target="tpu_custom_call" | custom-call | flops 215875584 | bytes 221184 | tf_op jit(solution)/shard_map/expert/pallas_call | solution.py:355
  191.8 11.9 %weight_grad.2 = (bf16[2,192,1536]{2,1,0:T(8,128)(2,1)}, bf16[2,192,1536]{2,1,0:T(8,128)(2,1)}, bf16[2,192,1536]{2,1,0:T(8,128)(2,1)}, bf16[2,192,1536]{2,1,0:T(8,128)(2,1)}) custom-call(s32[2]{0:T(128)} %pad_add_fusion.1.place_ref, bf16[2,4,288,768]{3,2,1,0:T(8,128)(2,1)} %get-tuple-element.92.rows_ref, bf16[2,4,288,1536]{3,2,1,0:T(8,128)(2,1)} %get-tuple-element.93.cols_ref), custom_call_target="tpu_custom_call" | custom-call | flops 84934656 | bytes 239616 | tf_op jit(solution)/shard_map/weight_grad/pallas_call | solution.py:403
  203.7 4.2 collective-permute-start.27
  208.6 5.9 %collective-permute-done.23.refs_10_.refs_14_ = bf16[2,192,1536]{2,1,0:T(8,128)(2,1)} collective-permute-done((bf16[2,192,1536]{2,1,0:T(8,128)(2,1)}, bf16[2,192,1536]{2,1,0:T(8,128)(2,1)}, u32[]{:S(2)}, u32[]{:S(2)}) %collective-permute-start.23) | collective-permute-done | bytes 1179680 | tf_op jit(solution)/shard_map/ppermute | solution.py:547
  214.5 28.3 %expert.3 = (bf16[2,4,288,768]{3,2,1,0:T(8,128)(2,1)}, bf16[2,4,288,1536]{3,2,1,0:T(8,128)(2,1)}, f32[4,1,832]{2,1,0:T(1,128)}, bf16[4,288,768]{2,1,0:T(8,128)(2...) custom-call(s32[2]{0:T(128)} %pad_add_fusion.2.place_ref, s32[4,2,832]{2,1,0:T(2,128)} %get-tuple-element.87.slot_ref, ...), custom_call_target="tpu_custom_call" | custom-call | flops 215875584 | bytes 221184 | tf_op jit(solution)/shard_map/expert/pallas_call | solution.py:355
  242.7 5.3 %combine_back.5 = (bf16[832,384]{1,0:T(8,128)(2,1)}, bf16[832,384]{1,0:T(8,128)(2,1)}, f32[8,768]{1,0:T(8,128)}) custom-call(s32[2]{0:T(128)} %pad_add_fusion.1.place_ref, s32[4,832,2]{2,1,0:T(8,128)} %get-tuple-element.85.slot_ref, bf16[4,288,768]{2,1,0:T(8,128)(2,1)} %get-tuple-element.95.refs_0_, bf16[4,288,768]{2,1,0:T(8,128)(2,1)} %get-tuple-element.98.refs_1_, ...), custom_call_target="tpu_custom_call" | custom-call | flops 11501568 | bytes 73728 | tf_op jit(solution)/shard_map/combine_back/pallas_call | solution.py:493
  248.5 5.2 %combine_back.4 = (bf16[832,384]{1,0:T(8,128)(2,1)}, bf16[832,384]{1,0:T(8,128)(2,1)}, f32[8,768]{1,0:T(8,128)}) custom-call(s32[2]{0:T(128)} %pad_add_fusion.1.place_ref, s32[4,832,2]{2,1,0:T(8,128)} %get-tuple-element.85.slot_ref, bf16[4,288,768]{2,1,0:T(8,128)(2,1)} %get-tuple-element.95.refs_0_, bf16[4,288,768]{2,1,0:T(8,128)(2,1)} %get-tuple-element.98.refs_1_, ...), custom_call_target="tpu_custom_call" | custom-call | flops 11501568 | bytes 73728 | tf_op jit(solution)/shard_map/combine_back/pallas_call | solution.py:493
  254.3 10.2 %collective-permute-done.27 = bf16[2,192,1536]{2,1,0:T(8,128)(2,1)} collective-permute-done((bf16[2,192,1536]{2,1,0:T(8,128)(2,1)}, bf16[2,192,1536]{2,1,0:T(8,128)(2,1)}, u32[]{:S(2)}, u32[]{:S(2)}) %collective-permute-start.27) | collective-permute-done | bytes 1179680 | tf_op jit(solution)/shard_map/ppermute | solution.py:547
  266.2 5.6 %combine_back.6 = (bf16[832,384]{1,0:T(8,128)(2,1)}, bf16[832,384]{1,0:T(8,128)(2,1)}, f32[8,768]{1,0:T(8,128)}) custom-call(s32[2]{0:T(128)} %pad_add_fusion.1.place_ref, s32[4,832,2]{2,1,0:T(8,128)} %get-tuple-element.85.slot_ref, bf16[4,288,768]{2,1,0:T(8,128)(2,1)} %get-tuple-element.95.refs_0_, bf16[4,288,768]{2,1,0:T(8,128)(2,1)} %get-tuple-element.98.refs_1_, ...), custom_call_target="tpu_custom_call" | custom-call | flops 11501568 | bytes 73728 | tf_op jit(solution)/shard_map/combine_back/pallas_call | solution.py:493
  279.0 5.7 %combine_back.7 = (bf16[832,384]{1,0:T(8,128)(2,1)}, bf16[832,384]{1,0:T(8,128)(2,1)}, f32[8,768]{1,0:T(8,128)}) custom-call(s32[2]{0:T(128)} %pad_add_fusion.1.place_ref, s32[4,832,2]{2,1,0:T(8,128)} %get-tuple-element.85.slot_ref, bf16[4,288,768]{2,1,0:T(8,128)(2,1)} %get-tuple-element.95.refs_0_, bf16[4,288,768]{2,1,0:T(8,128)(2,1)} %get-tuple-element.98.refs_1_, ...), custom_call_target="tpu_custom_call" | custom-call | flops 11501568 | bytes 73728 | tf_op jit(solution)/shard_map/combine_back/pallas_call | solution.py:493
  292.3 12.0 %weight_grad.3 = (bf16[2,192,1536]{2,1,0:T(8,128)(2,1)}, bf16[2,192,1536]{2,1,0:T(8,128)(2,1)}, bf16[2,192,1536]{2,1,0:T(8,128)(2,1)}, bf16[2,192,1536]{2,1,0:T(8,128)(2,1)}) custom-call(s32[2]{0:T(128)} %pad_add_fusion.2.place_ref, bf16[2,4,288,768]{3,2,1,0:T(8,128)(2,1)} %get-tuple-element.118.rows_ref, bf16[2,4,288,1536]{3,2,1,0:T(8,128)(2,1)} %get-tuple-element.119.cols_ref), custom_call_target="tpu_custom_call" | custom-call | flops 84934656 | bytes 239616 | tf_op jit(solution)/shard_map/weight_grad/pallas_call | solution.py:403
  320.8 5.4 %collective-permute-done.35 = bf16[832,384]{1,0:T(8,128)(2,1)S(1)} collective-permute-done((bf16[832,384]{1,0:T(8,128)(2,1)S(1)}, bf16[832,384]{1,0:T(8,128)(2,1)S(1)}, u32[]{:S(2)}, u32[]{:S(2)}) %collective-permute-start.35) | collective-permute-done | bytes 639008 | tf_op jit(solution)/shard_map/ppermute | solution.py:541
  326.3 4.1 combine.6
  335.7 20.5 %attend_back.1 = (bf16[2,832,384]{2,1,0:T(8,128)(2,1)}, f32[832,128]{1,0:T(8,128)}, bf16[384,1664]{1,0:T(8,128)(2,1)}, bf16[384,1664]{1,0:T(8,128)(2,1)}) custom-call(s32[1]{0:T(128)} %bitcast.35.core_ref, bf16[832,768]{1,0:T(8,128)(2,1)} %pad_maximum_fusion.3.x_ref, f32[1,768]{1,0:T(1,128)} %copy.165.gain_ref, ...), custom_call_target="tpu_custom_call" | custom-call | flops 107347968 | bytes 119808 | tf_op jit(solution)/shard_map/attend_back/pallas_call | solution.py:193
  356.2 4.3 collective-permute-done.37
  393.0 7.2 %collective-permute-done.42 = bf16[832,384]{1,0:T(8,128)(2,1)} collective-permute-done((bf16[832,384]{1,0:T(8,128)(2,1)}, bf16[832,384]{1,0:T(8,128)(2,1)}, u32[]{:S(2)}, u32[]{:S(2)}) %collective-permute-start.42) | collective-permute-done | bytes 639008 | tf_op jit(solution)/shard_map/ppermute | solution.py:541
  402.6 9.0 %collective-permute-done.40 = bf16[832,384]{1,0:T(8,128)(2,1)S(1)} collective-permute-done((bf16[832,384]{1,0:T(8,128)(2,1)S(1)}, bf16[832,384]{1,0:T(8,128)(2,1)S(1)}, u32[]{:S(2)}, u32[]{:S(2)}) %collective-permute-start.40) | collective-permute-done | bytes 639008 | tf_op jit(solution)/shard_map/ppermute | solution.py:541
  (267 shorter events, 160.0 us)
Async XLA Ops:
  34.4 29.5 %collective-permute-start.9 = (bf16[2,192,1536]{2,1,0:T(8,128)(2,1)S(1)}, bf16[2,192,1536]{2,1,0:T(8,128)(2,1)}, u32[]{:S(2)}, u32[]{:S(2)}) collective-permute-start(bf16[2,192,1536]{2,1,0:T(8,128)(2,1)S(1)} %get-tuple-element.210.refs_8_.refs_12_), channel_id=1, source_target_pairs={{0,8},{4,12},{8,16},{12,20},{16,24},{20,28},{24,0},{28,4},{1,9},{5... | collective-permute-start | bytes 3538952 | tf_op jit(solution)/shard_map/ppermute | solution.py:547
  63.9 28.4 %collective-permute-start.12 = (bf16[2,192,1536]{2,1,0:T(8,128)(2,1)S(1)}, bf16[2,192,1536]{2,1,0:T(8,128)(2,1)S(1)}, u32[]{:S(2)}, u32[]{:S(2)}) collective-permute-start(bf16[2,192,1536]{2,1,0:T(8,128)(2,1)S(1)} %get-tuple-element.210.refs_8_.refs_12_), channel_id=1, source_target_pairs={{0,24},{4,28},{8,0},{12,4},{16,8},{20,12},{24,16},{28,20},{1,25},{... | collective-permute-start | bytes 3538952 | tf_op jit(solution)/shard_map/ppermute | solution.py:547
  93.3 30.0 %collective-permute-start.13 = (bf16[832,768]{1,0:T(8,128)(2,1)}, bf16[832,768]{1,0:T(8,128)(2,1)}, u32[]{:S(2)}, u32[]{:S(2)}) collective-permute-start(bf16[832,768]{1,0:T(8,128)(2,1)} %get-tuple-element.84), channel_id=1, source_target_pairs={{0,2},{2,0},{1,3},{3,1},{4,6},{6,4},{5,7},{7,5},{8,10},{10,8},{9,1... | collective-permute-start | bytes 3833864 | tf_op jit(solution)/shard_map/ppermute | solution.py:541
  93.8 29.3 %collective-permute-start.14 = (bf16[2,192,1536]{2,1,0:T(8,128)(2,1)}, bf16[2,192,1536]{2,1,0:T(8,128)(2,1)S(1)}, u32[]{:S(2)}, u32[]{:S(2)}) collective-permute-start(bf16[2,192,1536]{2,1,0:T(8,128)(2,1)} %collective-permute-done.9.refs_9_.refs_13_), channel_id=1, source_target_pairs={{0,8},{4,12},{8,16},{12,20},{16,24},{20,28},{24,0},{28,4},{1,9},{5... | collective-permute-start | bytes 3538952 | tf_op jit(solution)/shard_map/ppermute | solution.py:547
  100.8 29.7 %collective-permute-start.19 = (bf16[832,768]{1,0:T(8,128)(2,1)}, bf16[832,768]{1,0:T(8,128)(2,1)}, u32[]{:S(2)}, u32[]{:S(2)}) collective-permute-start(bf16[832,768]{1,0:T(8,128)(2,1)} %pad_maximum_fusion.5.refs_4_), channel_id=1, source_target_pairs={{0,1},{1,0},{2,3},{3,2},{4,5},{5,4},{6,7},{7,6},{8,9},{9,8},{10,11... | collective-permute-start | bytes 3833864 | tf_op jit(solution)/shard_map/ppermute | solution.py:541
  129.7 28.8 %collective-permute-start.16 = (bf16[832,768]{1,0:T(8,128)(2,1)}, bf16[832,768]{1,0:T(8,128)(2,1)}, u32[]{:S(2)}, u32[]{:S(2)}) collective-permute-start(bf16[832,768]{1,0:T(8,128)(2,1)} %multiply_convert_fusion.refs_0_.refs_6_), channel_id=1, source_target_pairs={{0,1},{1,0},{2,3},{3,2},{4,5},{5,4},{6,7},{7,6},{8,9},{9,8},{10,11... | collective-permute-start | bytes 3833864 | tf_op jit(solution)/shard_map/ppermute | solution.py:541
  130.3 28.2 %collective-permute-start.15 = (bf16[2,192,1536]{2,1,0:T(8,128)(2,1)}, bf16[2,192,1536]{2,1,0:T(8,128)(2,1)}, u32[]{:S(2)}, u32[]{:S(2)}) collective-permute-start(bf16[2,192,1536]{2,1,0:T(8,128)(2,1)} %get-tuple-element.97.refs_8_.refs_12_), channel_id=1, source_target_pairs={{0,8},{4,12},{8,16},{12,20},{16,24},{20,28},{24,0},{28,4},{1,9},{5... | collective-permute-start | bytes 3538952 | tf_op jit(solution)/shard_map/ppermute | solution.py:547
  130.3 31.9 %collective-permute-start.20 = (bf16[832,768]{1,0:T(8,128)(2,1)}, bf16[832,768]{1,0:T(8,128)(2,1)}, u32[]{:S(2)}, u32[]{:S(2)}) collective-permute-start(bf16[832,768]{1,0:T(8,128)(2,1)} %pad_maximum_fusion.5.refs_4_), channel_id=1, source_target_pairs={{0,4},{4,0},{8,12},{12,8},{16,20},{20,16},{24,28},{28,24},{1,5},{5... | collective-permute-start | bytes 3833864 | tf_op jit(solution)/shard_map/ppermute | solution.py:550
  130.6 31.9 %collective-permute-start.21 = (bf16[832,768]{1,0:T(8,128)(2,1)}, bf16[832,768]{1,0:T(8,128)(2,1)}, u32[]{:S(2)}, u32[]{:S(2)}) collective-permute-start(bf16[832,768]{1,0:T(8,128)(2,1)} %collective-permute-done.19.refs_5_), channel_id=1, source_target_pairs={{0,4},{4,0},{8,12},{12,8},{16,20},{20,16},{24,28},{28,24},{1,5},{5... | collective-permute-start | bytes 3833864 | tf_op jit(solution)/shard_map/ppermute | solution.py:550
  159.1 49.5 %collective-permute-start.24 = (bf16[2,192,1536]{2,1,0:T(8,128)(2,1)}, bf16[2,192,1536]{2,1,0:T(8,128)(2,1)}, u32[]{:S(2)}, u32[]{:S(2)}) collective-permute-start(bf16[2,192,1536]{2,1,0:T(8,128)(2,1)} %get-tuple-element.97.refs_8_.refs_12_), channel_id=1, source_target_pairs={{0,24},{4,28},{8,0},{12,4},{16,8},{20,12},{24,16},{28,20},{1,25},{... | collective-permute-start | bytes 3538952 | tf_op jit(solution)/shard_map/ppermute | solution.py:547
  162.2 52.2 %collective-permute-start.23 = (bf16[2,192,1536]{2,1,0:T(8,128)(2,1)}, bf16[2,192,1536]{2,1,0:T(8,128)(2,1)}, u32[]{:S(2)}, u32[]{:S(2)}) collective-permute-start(bf16[2,192,1536]{2,1,0:T(8,128)(2,1)} %collective-permute-done.15.refs_9_.refs_13_), channel_id=1, source_target_pairs={{0,8},{4,12},{8,16},{12,20},{16,24},{20,28},{24,0},{28,4},{1,9},{5... | collective-permute-start | bytes 3538952 | tf_op jit(solution)/shard_map/ppermute | solution.py:547
  203.7 39.0 %collective-permute-start.22 = (bf16[2,192,1536]{2,1,0:T(8,128)(2,1)}, bf16[2,192,1536]{2,1,0:T(8,128)(2,1)}, u32[]{:S(2)}, u32[]{:S(2)}) collective-permute-start(bf16[2,192,1536]{2,1,0:T(8,128)(2,1)} %get-tuple-element.94), channel_id=1, source_target_pairs={{0,8},{4,12},{8,16},{12,20},{16,24},{20,28},{24,0},{28,4},{1,9},{5... | collective-permute-start | bytes 3538952 | tf_op jit(solution)/shard_map/ppermute | solution.py:547
  203.7 60.8 %collective-permute-start.27 = (bf16[2,192,1536]{2,1,0:T(8,128)(2,1)}, bf16[2,192,1536]{2,1,0:T(8,128)(2,1)}, u32[]{:S(2)}, u32[]{:S(2)}) collective-permute-start(bf16[2,192,1536]{2,1,0:T(8,128)(2,1)} %get-tuple-element.104), channel_id=1, source_target_pairs={{0,24},{4,28},{8,0},{12,4},{16,8},{20,12},{24,16},{28,20},{1,25},{... | collective-permute-start | bytes 3538952 | tf_op jit(solution)/shard_map/ppermute | solution.py:547
  253.8 25.3 %collective-permute-start.25 = (bf16[832,384]{1,0:T(8,128)(2,1)}, bf16[832,384]{1,0:T(8,128)(2,1)}, u32[]{:S(2)}, u32[]{:S(2)}) collective-permute-start(bf16[832,384]{1,0:T(8,128)(2,1)} %get-tuple-element.102), channel_id=1, source_target_pairs={{0,4},{4,0},{8,12},{12,8},{16,20},{20,16},{24,28},{28,24},{1,5},{5... | collective-permute-start | bytes 1916936 | tf_op jit(solution)/shard_map/ppermute | solution.py:550
  274.9 42.2 %collective-permute-start.33 = (bf16[2,192,1536]{2,1,0:T(8,128)(2,1)}, bf16[2,192,1536]{2,1,0:T(8,128)(2,1)}, u32[]{:S(2)}, u32[]{:S(2)}) collective-permute-start(bf16[2,192,1536]{2,1,0:T(8,128)(2,1)} %add_convert_fusion.3), channel_id=1, source_target_pairs={{0,8},{4,12},{8,16},{12,20},{16,24},{20,28},{24,0},{28,4},{1,9},{5... | collective-permute-start | bytes 3538952 | tf_op jit(solution)/shard_map/ppermute | solution.py:547
  276.7 31.3 %collective-permute-start.34 = (bf16[832,384]{1,0:T(8,128)(2,1)}, bf16[832,384]{1,0:T(8,128)(2,1)}, u32[]{:S(2)}, u32[]{:S(2)}) collective-permute-start(bf16[832,384]{1,0:T(8,128)(2,1)} %get-tuple-element.122), channel_id=1, source_target_pairs={{0,1},{1,0},{2,3},{3,2},{4,5},{5,4},{6,7},{7,6},{8,9},{9,8},{10,11... | collective-permute-start | bytes 1916936 | tf_op jit(solution)/shard_map/ppermute | solution.py:541
  290.7 29.9 %collective-permute-start.32 = (bf16[832,384]{1,0:T(8,128)(2,1)S(1)}, bf16[832,384]{1,0:T(8,128)(2,1)S(1)}, u32[]{:S(2)}, u32[]{:S(2)}) collective-permute-start(bf16[832,384]{1,0:T(8,128)(2,1)S(1)} %add_convert_fusion.6), channel_id=1, source_target_pairs={{0,2},{2,0},{1,3},{3,1},{4,6},{6,4},{5,7},{7,5},{8,10},{10,8},{9,1... | collective-permute-start | bytes 1916936 | tf_op jit(solution)/shard_map/ppermute | solution.py:541
  309.9 46.3 %collective-permute-start.38 = (bf16[2,192,1536]{2,1,0:T(8,128)(2,1)}, bf16[2,192,1536]{2,1,0:T(8,128)(2,1)}, u32[]{:S(2)}, u32[]{:S(2)}) collective-permute-start(bf16[2,192,1536]{2,1,0:T(8,128)(2,1)} %get-tuple-element.132), channel_id=1, source_target_pairs={{0,24},{4,28},{8,0},{12,4},{16,8},{20,12},{24,16},{28,20},{1,25},{... | collective-permute-start | bytes 3538952 | tf_op jit(solution)/shard_map/ppermute | solution.py:547
  317.2 48.3 %collective-permute-start.48 = (bf16[2,192,1536]{2,1,0:T(8,128)(2,1)}, bf16[2,192,1536]{2,1,0:T(8,128)(2,1)}, u32[]{:S(2)}, u32[]{:S(2)}) collective-permute-start(bf16[2,192,1536]{2,1,0:T(8,128)(2,1)} %get-tuple-element.144), channel_id=1, source_target_pairs={{0,8},{4,12},{8,16},{12,20},{16,24},{20,28},{24,0},{28,4},{1,9},{5... | collective-permute-start | bytes 3538952 | tf_op jit(solution)/shard_map/ppermute | solution.py:547
  330.4 30.1 %collective-permute-start.37 = (bf16[832,768]{1,0:T(8,128)(2,1)}, bf16[832,768]{1,0:T(8,128)(2,1)}, u32[]{:S(2)}, u32[]{:S(2)}) collective-permute-start(bf16[832,768]{1,0:T(8,128)(2,1)} %combine.6), channel_id=1, source_target_pairs={{0,1},{1,0},{2,3},{3,2},{4,5},{5,4},{6,7},{7,6},{8,9},{9,8},{10,11... | collective-permute-start | bytes 3833864 | tf_op jit(solution)/shard_map/ppermute | solution.py:541
  367.3 48.9 %collective-permute-start.49 = (bf16[2,192,1536]{2,1,0:T(8,128)(2,1)S(1)}, bf16[2,192,1536]{2,1,0:T(8,128)(2,1)S(1)}, u32[]{:S(2)}, u32[]{:S(2)}) collective-permute-start(bf16[2,192,1536]{2,1,0:T(8,128)(2,1)S(1)} %add_convert_fusion.2), channel_id=1, source_target_pairs={{0,8},{4,12},{8,16},{12,20},{16,24},{20,28},{24,0},{28,4},{1,9},{5... | collective-permute-start | bytes 3538952 | tf_op jit(solution)/shard_map/ppermute | solution.py:547
  382.6 29.0 %collective-permute-start.40 = (bf16[832,384]{1,0:T(8,128)(2,1)S(1)}, bf16[832,384]{1,0:T(8,128)(2,1)S(1)}, u32[]{:S(2)}, u32[]{:S(2)}) collective-permute-start(bf16[832,384]{1,0:T(8,128)(2,1)S(1)} %constant_dynamic-slice_fusion), channel_id=1, source_target_pairs={{0,2},{2,0},{1,3},{3,1},{4,6},{6,4},{5,7},{7,5},{8,10},{10,8},{9,1... | collective-permute-start | bytes 1916936 | tf_op jit(solution)/shard_map/ppermute | solution.py:541
  389.1 27.1 %collective-permute-start.44 = (bf16[48,1664]{1,0:T(8,128)(2,1)S(1)}, bf16[48,1664]{1,0:T(8,128)(2,1)S(1)}, u32[]{:S(2)}, u32[]{:S(2)}) collective-permute-start(bf16[48,1664]{1,0:T(8,128)(2,1)S(1)} %get-tuple-element.221), channel_id=1, source_target_pairs={{0,8},{4,12},{8,16},{12,20},{16,24},{20,28},{24,0},{28,4},{1,9},{5... | collective-permute-start | bytes 479240 | tf_op jit(solution)/shard_map/ppermute | solution.py:547
  391.2 28.9 %collective-permute-start.46 = (bf16[48,1664]{1,0:T(8,128)(2,1)S(1)}, bf16[48,1664]{1,0:T(8,128)(2,1)S(1)}, u32[]{:S(2)}, u32[]{:S(2)}) collective-permute-start(bf16[48,1664]{1,0:T(8,128)(2,1)S(1)} %get-tuple-element.222), channel_id=1, source_target_pairs={{0,24},{4,28},{8,0},{12,4},{16,8},{20,12},{24,16},{28,20},{1,25},{... | collective-permute-start | bytes 479240 | tf_op jit(solution)/shard_map/ppermute | solution.py:547
  (65 other events, 706.8 us)

commit v3 on v2

--- a/solution.py
+++ b/solution.py
@@ -728,7 +728,7 @@
     arrived_last, down_last = ring_first(last), ring_down(last)
     dsum_other[0] = after(dsum_other[0], ends[0])
 
-    yrows[0] = after(yrows[0], dsum[0])
+    yrows[0] = after(yrows[0], dsum_other[0])
     y_came = [swap_core(combine(slot_cols, yrows, n_exp + k)) for k in range(n_exp)]
     y_from = [
         shift(combine(slot_cols, yrows, k, after(y_came[k], dsum[-1])), "expert", -k)
@@ -776,7 +776,7 @@
     for value in came:
         dtotal = dtotal + value.astype(F32)
 
-    ends.append(ring_end(last, late, down_last, came[0]))
+    ends.append(ring_end(last, late, down_last, dpack))
     stacked = jnp.stack(ends).reshape(local, 2, CORES, part_rows, hidden_width)
     other = swap_core(take(stacked, 1 - core, 2).astype(BF16)).astype(F32)
     own = take(stacked, core, 2)
@@ -784,6 +784,7 @@
     grads = joined.transpose(1, 2, 0, 3)
     dside = dtotal[:, 4 * width :]
     over_heads = dside[:, : expert_count + 1].T
+    grad_w_out, grad_w_in, over_heads = lax.optimization_barrier((grads[0], grads[1], over_heads))
     summed = over_heads
     for k in range(1, n_heads):
         summed = summed + shift(over_heads, "heads", k)
@@ -799,9 +800,9 @@
     sums = stats[:, :2].T
     sums_total = sums
     for k in range(1, n_heads):
-        came = shift(take(dnorm, (head + k) % n_heads), "heads", k)
-        dn_own = dn_own + after(came, dpack).astype(F32)
-        sums_total = sums_total + after(shift(sums, "heads", k), dpack)
+        there = shift(take(dnorm, (head + k) % n_heads), "heads", k)
+        dn_own = dn_own + after(there, came[0]).astype(F32)
+        sums_total = sums_total + after(shift(sums, "heads", k), came[0])
     unit_one, scale_one = norm_parts(inputs.astype(F32))
     grad_in = own_half(dmiddle) + scale_one * (
         dn_own * own_half(gain_one)
@@ -813,7 +814,7 @@
     for k in range(1, n_heads):
         there = (head + k) % n_heads
         part_y = lax.dynamic_slice_in_dim(y_own, there * half_width, half_width, 1)
-        y_total = y_total + after(shift(part_y, "heads", k), dpack).astype(F32)
+        y_total = y_total + after(shift(part_y, "heads", k), came[0]).astype(F32)
     block_out = own_half(middle) + y_total
 
     return (
@@ -824,8 +825,8 @@
         dtotal[:, 3 * width : 4 * width],
         dside[:, expert_count + 1],
         summed[:expert_count].T,
-        grads[1],
-        grads[0],
+        grad_w_in,
+        grad_w_out,
     )
 
 

time: 444 us -> 454 us (1.023)
  waiting for transfers between devices: 150 us -> 162 us
    ppermute x18, waiting for transfers between devices: 96.2 us -> 115 us  [shift_z(): return lax.ppermute(value, 'dp', pairs)]
    ppermute x17, waiting for transfers between devices: 49.1 us -> 41.5 us  [shift(): lax.ppermute(value, axis, [(i, (i + step) % size) for i in range(size)])]
    unnamed x87 -> x99, local copies, waits for them, and re-layouts: 16.3 us -> 17.7 us
  transfers between devices with their start and end apart: 51 -> 51, of which waited for: 22 -> 24; matrix products, arithmetic and copies ran while one was open for 15% -> 15% of each run, Pallas kernels for 36% -> 34%
where the time goes in v3:
time: 454 us; the launch traced here: 445 us
  waiting for transfers between devices  162 us (36%)
  Pallas kernels  156 us (34%)
  other arithmetic  46.5 us (10%)
  starting transfers between devices  45.3 us (10%)
  local copies, waits for them, and re-layouts  34.1 us (8%)
    ppermute x18, waiting for transfers between devices, shift_z(): return lax.ppermute(value, 'dp', pairs)  115 us
    pallas_call x2, Pallas kernels, run_expert(): pl.pallas_call(functools.partial(expert_kernel, index, depth, blocks), gr...  56.2 us
    ppermute x17, waiting for transfers between devices, shift(): lax.ppermute(value, axis, [(i, (i + step) % size) for i in range(size)])  41.5 us
    pallas_call x2, Pallas kernels, weight_grad(): pl.pallas_call(functools.partial(weight_grad_kernel, depth), grid_spec=pl...  23.9 us
    ppermute x18, starting transfers between devices, shift_z(): return lax.ppermute(value, 'dp', pairs)  23.7 us
    pallas_call x4, Pallas kernels, combine_back(): pl.pallas_call(functools.partial(combine_back_kernel, local, add is not N...  21.7 us
    pallas_call x1, Pallas kernels, attend_back(): pl.pallas_call(functools.partial(attend_back_kernel, seq, gain_at, depth)...  21 us
    ppermute x17, starting transfers between devices, shift(): lax.ppermute(value, axis, [(i, (i + step) % size) for i in range(size)])  18.9 us
  transfers between devices with their start and end apart: 51, of which 24 were waited for; matrix products, arithmetic and copies ran while one was open for 15% of the time, Pallas kernels for 34%

profile of v3, /device:TPU:0, one launch (start us, length us, event | category | flops | bytes accessed | tf_op | source)
XLA Modules:
  0.0 445.1 jit_solution(294242467886687535)
XLA Ops:
  40.0 8.3 %collective-permute-done.8 = bf16[4,48,1664]{2,1,0:T(8,128)(2,1)S(1)} collective-permute-done((bf16[4,48,1664]{2,1,0:T(8,128)(2,1)}, bf16[4,48,1664]{2,1,0:T(8,128)(2,1)S(1)}, u32[]{:S(2)}, u32[]{:S(2)}) %collective-permute-start.8) | collective-permute-done | bytes 639008 | tf_op jit(solution)/shard_map/ppermute | solution.py:541
  49.6 14.2 %collective-permute-done.9.refs_9_.refs_13_ = bf16[2,192,1536]{2,1,0:T(8,128)(2,1)} collective-permute-done((bf16[2,192,1536]{2,1,0:T(8,128)(2,1)S(1)}, bf16[2,192,1536]{2,1,0:T(8,128)(2,1)}, u32[]{:S(2)}, u32[]{:S(2)}) %collective-permute-start.9) | collective-permute-done | bytes 1179680 | tf_op jit(solution)/shard_map/ppermute | solution.py:547
  68.8 10.8 %attend.1 = (bf16[832,768]{1,0:T(8,128)(2,1)}, bf16[832,1152]{1,0:T(8,128)(2,1)}, bf16[832,384]{1,0:T(8,128)(2,1)}) custom-call(bf16[832,768]{1,0:T(8,128)(2,1)} %pad_maximum_fusion.3.x_ref, bf16[768,1664]{1,0:T(8,128)(2,1)} %bitcast.129, bf16[768,1664]{1,0:T(8,128)(2,1)} %bitcast.130, bf16[768,1664]{1,0:T(8,128)(2,1)} %bitcast.131), custom_call_target="tpu_custom_call" | custom-call | flops 38338560 | bytes 79872 | tf_op jit(solution)/shard_map/attend/pallas_call | solution.py:96
  79.6 12.6 %collective-permute-done.12.refs_11_.refs_15_ = bf16[2,192,1536]{2,1,0:T(8,128)(2,1)S(1)} collective-permute-done((bf16[2,192,1536]{2,1,0:T(8,128)(2,1)S(1)}, bf16[2,192,1536]{2,1,0:T(8,128)(2,1)S(1)}, u32[]{:S(2)}, u32[]{:S(2)}) %collective-permute-start.12) | collective-permute-done | bytes 1179680 | tf_op jit(solution)/shard_map/ppermute | solution.py:547
  94.4 6.4 %find_slots.1 = (s32[4,2,832]{2,1,0:T(2,128)}, s32[4,832,2]{2,1,0:T(8,128)}) custom-call(s32[2]{0:T(128)} %pad_add_fusion.1.place_ref, s32[4,2,832]{2,1,0:T(2,128)} %pad_add_fusion.ids_ref), custom_call_target="tpu_custom_call" | custom-call | flops 2768896 | bytes 3328 | tf_op jit(solution)/shard_map/find_slots/pallas_call | solution.py:252
  102.9 20.2 %collective-permute-done.14.refs_10_.refs_14_ = bf16[2,192,1536]{2,1,0:T(8,128)(2,1)S(1)} collective-permute-done((bf16[2,192,1536]{2,1,0:T(8,128)(2,1)}, bf16[2,192,1536]{2,1,0:T(8,128)(2,1)S(1)}, u32[]{:S(2)}, u32[]{:S(2)}) %collective-permute-start.14) | collective-permute-done | bytes 1179680 | tf_op jit(solution)/shard_map/ppermute | solution.py:547
  130.9 27.7 %collective-permute-done.15.refs_9_.refs_13_ = bf16[2,192,1536]{2,1,0:T(8,128)(2,1)} collective-permute-done((bf16[2,192,1536]{2,1,0:T(8,128)(2,1)}, bf16[2,192,1536]{2,1,0:T(8,128)(2,1)}, u32[]{:S(2)}, u32[]{:S(2)}) %collective-permute-start.15) | collective-permute-done | bytes 1179680 | tf_op jit(solution)/shard_map/ppermute | solution.py:547
  163.8 28.1 %expert.2 = (bf16[2,4,288,768]{3,2,1,0:T(8,128)(2,1)}, bf16[2,4,288,1536]{3,2,1,0:T(8,128)(2,1)}, f32[4,1,832]{2,1,0:T(1,128)}, bf16[4,288,768]{2,1,0:T(8,128)(2...) custom-call(s32[2]{0:T(128)} %pad_add_fusion.1.place_ref, s32[4,2,832]{2,1,0:T(2,128)} %get-tuple-element.90.slot_ref, ...), custom_call_target="tpu_custom_call" | custom-call | flops 215875584 | bytes 221184 | tf_op jit(solution)/shard_map/expert/pallas_call | solution.py:355
  191.9 11.9 %weight_grad.2 = (bf16[2,192,1536]{2,1,0:T(8,128)(2,1)}, bf16[2,192,1536]{2,1,0:T(8,128)(2,1)}, bf16[2,192,1536]{2,1,0:T(8,128)(2,1)}, bf16[2,192,1536]{2,1,0:T(8,128)(2,1)}) custom-call(s32[2]{0:T(128)} %pad_add_fusion.1.place_ref, bf16[2,4,288,768]{3,2,1,0:T(8,128)(2,1)} %get-tuple-element.95.rows_ref, bf16[2,4,288,1536]{3,2,1,0:T(8,128)(2,1)} %get-tuple-element.96.cols_ref), custom_call_target="tpu_custom_call" | custom-call | flops 84934656 | bytes 239616 | tf_op jit(solution)/shard_map/weight_grad/pallas_call | solution.py:403
  203.8 4.2 collective-permute-start.27
  208.7 5.8 %collective-permute-done.23.refs_10_.refs_14_ = bf16[2,192,1536]{2,1,0:T(8,128)(2,1)} collective-permute-done((bf16[2,192,1536]{2,1,0:T(8,128)(2,1)}, bf16[2,192,1536]{2,1,0:T(8,128)(2,1)}, u32[]{:S(2)}, u32[]{:S(2)}) %collective-permute-start.23) | collective-permute-done | bytes 1179680 | tf_op jit(solution)/shard_map/ppermute | solution.py:547
  214.5 28.1 %expert.3 = (bf16[2,4,288,768]{3,2,1,0:T(8,128)(2,1)}, bf16[2,4,288,1536]{3,2,1,0:T(8,128)(2,1)}, f32[4,1,832]{2,1,0:T(1,128)}, bf16[4,288,768]{2,1,0:T(8,128)(2...) custom-call(s32[2]{0:T(128)} %pad_add_fusion.2.place_ref, s32[4,2,832]{2,1,0:T(2,128)} %get-tuple-element.90.slot_ref, ...), custom_call_target="tpu_custom_call" | custom-call | flops 215875584 | bytes 221184 | tf_op jit(solution)/shard_map/expert/pallas_call | solution.py:355
  242.6 5.3 %combine_back.5 = (bf16[832,384]{1,0:T(8,128)(2,1)}, bf16[832,384]{1,0:T(8,128)(2,1)}, f32[8,768]{1,0:T(8,128)}) custom-call(s32[2]{0:T(128)} %pad_add_fusion.1.place_ref, s32[4,832,2]{2,1,0:T(8,128)} %get-tuple-element.88.slot_ref, bf16[4,288,768]{2,1,0:T(8,128)(2,1)} %get-tuple-element.98.refs_0_, bf16[4,288,768]{2,1,0:T(8,128)(2,1)} %get-tuple-element.101.refs_1_, ...), custom_call_target="tpu_custom_call" | custom-call | flops 11501568 | bytes 73728 | tf_op jit(solution)/shard_map/combine_back/pallas_call | solution.py:493
  248.4 16.1 %collective-permute-done.27 = bf16[2,192,1536]{2,1,0:T(8,128)(2,1)} collective-permute-done((bf16[2,192,1536]{2,1,0:T(8,128)(2,1)}, bf16[2,192,1536]{2,1,0:T(8,128)(2,1)}, u32[]{:S(2)}, u32[]{:S(2)}) %collective-permute-start.27) | collective-permute-done | bytes 1179680 | tf_op jit(solution)/shard_map/ppermute | solution.py:547
  266.2 5.6 %combine_back.6 = (bf16[832,384]{1,0:T(8,128)(2,1)}, bf16[832,384]{1,0:T(8,128)(2,1)}, f32[8,768]{1,0:T(8,128)}) custom-call(s32[2]{0:T(128)} %pad_add_fusion.1.place_ref, s32[4,832,2]{2,1,0:T(8,128)} %get-tuple-element.88.slot_ref, bf16[4,288,768]{2,1,0:T(8,128)(2,1)} %get-tuple-element.98.refs_0_, bf16[4,288,768]{2,1,0:T(8,128)(2,1)} %get-tuple-element.101.refs_1_, ...), custom_call_target="tpu_custom_call" | custom-call | flops 11501568 | bytes 73728 | tf_op jit(solution)/shard_map/combine_back/pallas_call | solution.py:493
  274.1 5.2 %combine_back.4 = (bf16[832,384]{1,0:T(8,128)(2,1)}, bf16[832,384]{1,0:T(8,128)(2,1)}, f32[8,768]{1,0:T(8,128)}) custom-call(s32[2]{0:T(128)} %pad_add_fusion.1.place_ref, s32[4,832,2]{2,1,0:T(8,128)} %get-tuple-element.88.slot_ref, bf16[4,288,768]{2,1,0:T(8,128)(2,1)} %get-tuple-element.98.refs_0_, bf16[4,288,768]{2,1,0:T(8,128)(2,1)} %get-tuple-element.101.refs_1_, ...), custom_call_target="tpu_custom_call" | custom-call | flops 11501568 | bytes 73728 | tf_op jit(solution)/shard_map/combine_back/pallas_call | solution.py:493
  283.4 5.6 %combine_back.7 = (bf16[832,384]{1,0:T(8,128)(2,1)}, bf16[832,384]{1,0:T(8,128)(2,1)}, f32[8,768]{1,0:T(8,128)}) custom-call(s32[2]{0:T(128)} %pad_add_fusion.1.place_ref, s32[4,832,2]{2,1,0:T(8,128)} %get-tuple-element.88.slot_ref, bf16[4,288,768]{2,1,0:T(8,128)(2,1)} %get-tuple-element.98.refs_0_, bf16[4,288,768]{2,1,0:T(8,128)(2,1)} %get-tuple-element.101.refs_1_, ...), custom_call_target="tpu_custom_call" | custom-call | flops 11501568 | bytes 73728 | tf_op jit(solution)/shard_map/combine_back/pallas_call | solution.py:493
  289.0 8.3 %collective-permute-done.30 = bf16[832,384]{1,0:T(8,128)(2,1)S(1)} collective-permute-done((bf16[832,384]{1,0:T(8,128)(2,1)}, bf16[832,384]{1,0:T(8,128)(2,1)S(1)}, u32[]{:S(2)}, u32[]{:S(2)}) %collective-permute-start.30) | collective-permute-done | bytes 639008 | tf_op jit(solution)/shard_map/ppermute | solution.py:541
  301.2 12.0 %weight_grad.3 = (bf16[2,192,1536]{2,1,0:T(8,128)(2,1)}, bf16[2,192,1536]{2,1,0:T(8,128)(2,1)}, bf16[2,192,1536]{2,1,0:T(8,128)(2,1)}, bf16[2,192,1536]{2,1,0:T(8,128)(2,1)}) custom-call(s32[2]{0:T(128)} %pad_add_fusion.2.place_ref, bf16[2,4,288,768]{3,2,1,0:T(8,128)(2,1)} %get-tuple-element.121.rows_ref, bf16[2,4,288,1536]{3,2,1,0:T(8,128)(2,1)} %get-tuple-element.122.cols_ref), custom_call_target="tpu_custom_call" | custom-call | flops 84934656 | bytes 239616 | tf_op jit(solution)/shard_map/weight_grad/pallas_call | solution.py:403
  333.8 5.7 %collective-permute-done.35 = bf16[832,384]{1,0:T(8,128)(2,1)} collective-permute-done((bf16[832,384]{1,0:T(8,128)(2,1)}, bf16[832,384]{1,0:T(8,128)(2,1)}, u32[]{:S(2)}, u32[]{:S(2)}) %collective-permute-start.35) | collective-permute-done | bytes 639008 | tf_op jit(solution)/shard_map/ppermute | solution.py:541
  350.4 21.0 %attend_back.1 = (bf16[2,832,384]{2,1,0:T(8,128)(2,1)}, f32[832,128]{1,0:T(8,128)}, bf16[384,1664]{1,0:T(8,128)(2,1)}, bf16[384,1664]{1,0:T(8,128)(2,1)}) custom-call(s32[1]{0:T(128)} %bitcast.35.core_ref, bf16[832,768]{1,0:T(8,128)(2,1)} %pad_maximum_fusion.3.x_ref, f32[1,768]{1,0:T(1,128)} %copy.165.gain_ref, ...), custom_call_target="tpu_custom_call" | custom-call | flops 107347968 | bytes 119808 | tf_op jit(solution)/shard_map/attend_back/pallas_call | solution.py:193
  376.5 6.6 %collective-permute-done.45 = bf16[2,192,1536]{2,1,0:T(8,128)(2,1)} collective-permute-done((bf16[2,192,1536]{2,1,0:T(8,128)(2,1)}, bf16[2,192,1536]{2,1,0:T(8,128)(2,1)}, u32[]{:S(2)}, u32[]{:S(2)}) %collective-permute-start.45) | collective-permute-done | bytes 1179680 | tf_op jit(solution)/shard_map/ppermute | solution.py:547
  407.7 8.3 %collective-permute-done.46 = bf16[2,192,1536]{2,1,0:T(8,128)(2,1)S(1)} collective-permute-done((bf16[2,192,1536]{2,1,0:T(8,128)(2,1)S(1)}, bf16[2,192,1536]{2,1,0:T(8,128)(2,1)S(1)}, u32[]{:S(2)}, u32[]{:S(2)}) %collective-permute-start.46) | collective-permute-done | bytes 1179680 | tf_op jit(solution)/shard_map/ppermute | solution.py:547
  423.4 4.5 %collective-permute-done.40 = bf16[832,384]{1,0:T(8,128)(2,1)S(1)} collective-permute-done((bf16[832,384]{1,0:T(8,128)(2,1)S(1)}, bf16[832,384]{1,0:T(8,128)(2,1)S(1)}, u32[]{:S(2)}, u32[]{:S(2)}) %collective-permute-start.40) | collective-permute-done | bytes 639008 | tf_op jit(solution)/shard_map/ppermute | solution.py:541
  (279 shorter events, 160.4 us)
Async XLA Ops:
  3.7 22.9 %collective-permute-start.2 = (bf16[2,2,96,1536]{3,2,1,0:T(8,128)(2,1)}, bf16[2,2,96,1536]{3,2,1,0:T(8,128)(2,1)}, u32[]{:S(2)}, u32[]{:S(2)}) collective-permute-start(bf16[2,2,96,1536]{3,2,1,0:T(8,128)(2,1)} %fusion.15), channel_id=1, source_target_pairs={{0,4},{4,0},{8,12},{12,8},{16,20},{20,16},{24,28},{28,24},{1,5},{5... | collective-permute-start | bytes 3538952 | tf_op jit(solution)/shard_map/ppermute | solution.py:550
  34.4 29.5 %collective-permute-start.9 = (bf16[2,192,1536]{2,1,0:T(8,128)(2,1)S(1)}, bf16[2,192,1536]{2,1,0:T(8,128)(2,1)}, u32[]{:S(2)}, u32[]{:S(2)}) collective-permute-start(bf16[2,192,1536]{2,1,0:T(8,128)(2,1)S(1)} %get-tuple-element.216.refs_8_.refs_12_), channel_id=1, source_target_pairs={{0,8},{4,12},{8,16},{12,20},{16,24},{20,28},{24,0},{28,4},{1,9},{5... | collective-permute-start | bytes 3538952 | tf_op jit(solution)/shard_map/ppermute | solution.py:547
  63.8 28.4 %collective-permute-start.12 = (bf16[2,192,1536]{2,1,0:T(8,128)(2,1)S(1)}, bf16[2,192,1536]{2,1,0:T(8,128)(2,1)S(1)}, u32[]{:S(2)}, u32[]{:S(2)}) collective-permute-start(bf16[2,192,1536]{2,1,0:T(8,128)(2,1)S(1)} %get-tuple-element.216.refs_8_.refs_12_), channel_id=1, source_target_pairs={{0,24},{4,28},{8,0},{12,4},{16,8},{20,12},{24,16},{28,20},{1,25},{... | collective-permute-start | bytes 3538952 | tf_op jit(solution)/shard_map/ppermute | solution.py:547
  93.3 30.0 %collective-permute-start.13 = (bf16[832,768]{1,0:T(8,128)(2,1)}, bf16[832,768]{1,0:T(8,128)(2,1)}, u32[]{:S(2)}, u32[]{:S(2)}) collective-permute-start(bf16[832,768]{1,0:T(8,128)(2,1)} %get-tuple-element.87), channel_id=1, source_target_pairs={{0,2},{2,0},{1,3},{3,1},{4,6},{6,4},{5,7},{7,5},{8,10},{10,8},{9,1... | collective-permute-start | bytes 3833864 | tf_op jit(solution)/shard_map/ppermute | solution.py:541
  93.8 29.3 %collective-permute-start.14 = (bf16[2,192,1536]{2,1,0:T(8,128)(2,1)}, bf16[2,192,1536]{2,1,0:T(8,128)(2,1)S(1)}, u32[]{:S(2)}, u32[]{:S(2)}) collective-permute-start(bf16[2,192,1536]{2,1,0:T(8,128)(2,1)} %collective-permute-done.9.refs_9_.refs_13_), channel_id=1, source_target_pairs={{0,8},{4,12},{8,16},{12,20},{16,24},{20,28},{24,0},{28,4},{1,9},{5... | collective-permute-start | bytes 3538952 | tf_op jit(solution)/shard_map/ppermute | solution.py:547
  100.9 29.7 %collective-permute-start.19 = (bf16[832,768]{1,0:T(8,128)(2,1)}, bf16[832,768]{1,0:T(8,128)(2,1)}, u32[]{:S(2)}, u32[]{:S(2)}) collective-permute-start(bf16[832,768]{1,0:T(8,128)(2,1)} %pad_maximum_fusion.5.refs_4_), channel_id=1, source_target_pairs={{0,1},{1,0},{2,3},{3,2},{4,5},{5,4},{6,7},{7,6},{8,9},{9,8},{10,11... | collective-permute-start | bytes 3833864 | tf_op jit(solution)/shard_map/ppermute | solution.py:541
  129.8 28.9 %collective-permute-start.16 = (bf16[832,768]{1,0:T(8,128)(2,1)}, bf16[832,768]{1,0:T(8,128)(2,1)}, u32[]{:S(2)}, u32[]{:S(2)}) collective-permute-start(bf16[832,768]{1,0:T(8,128)(2,1)} %multiply_convert_fusion.refs_0_.refs_6_), channel_id=1, source_target_pairs={{0,1},{1,0},{2,3},{3,2},{4,5},{5,4},{6,7},{7,6},{8,9},{9,8},{10,11... | collective-permute-start | bytes 3833864 | tf_op jit(solution)/shard_map/ppermute | solution.py:541
  130.4 28.2 %collective-permute-start.15 = (bf16[2,192,1536]{2,1,0:T(8,128)(2,1)}, bf16[2,192,1536]{2,1,0:T(8,128)(2,1)}, u32[]{:S(2)}, u32[]{:S(2)}) collective-permute-start(bf16[2,192,1536]{2,1,0:T(8,128)(2,1)} %get-tuple-element.100.refs_8_.refs_12_), channel_id=1, source_target_pairs={{0,8},{4,12},{8,16},{12,20},{16,24},{20,28},{24,0},{28,4},{1,9},{5... | collective-permute-start | bytes 3538952 | tf_op jit(solution)/shard_map/ppermute | solution.py:547
  130.4 31.8 %collective-permute-start.20 = (bf16[832,768]{1,0:T(8,128)(2,1)}, bf16[832,768]{1,0:T(8,128)(2,1)}, u32[]{:S(2)}, u32[]{:S(2)}) collective-permute-start(bf16[832,768]{1,0:T(8,128)(2,1)} %pad_maximum_fusion.5.refs_4_), channel_id=1, source_target_pairs={{0,4},{4,0},{8,12},{12,8},{16,20},{20,16},{24,28},{28,24},{1,5},{5... | collective-permute-start | bytes 3833864 | tf_op jit(solution)/shard_map/ppermute | solution.py:550
  130.6 31.9 %collective-permute-start.21 = (bf16[832,768]{1,0:T(8,128)(2,1)}, bf16[832,768]{1,0:T(8,128)(2,1)}, u32[]{:S(2)}, u32[]{:S(2)}) collective-permute-start(bf16[832,768]{1,0:T(8,128)(2,1)} %collective-permute-done.19.refs_5_), channel_id=1, source_target_pairs={{0,4},{4,0},{8,12},{12,8},{16,20},{20,16},{24,28},{28,24},{1,5},{5... | collective-permute-start | bytes 3833864 | tf_op jit(solution)/shard_map/ppermute | solution.py:550
  159.2 49.5 %collective-permute-start.24 = (bf16[2,192,1536]{2,1,0:T(8,128)(2,1)}, bf16[2,192,1536]{2,1,0:T(8,128)(2,1)}, u32[]{:S(2)}, u32[]{:S(2)}) collective-permute-start(bf16[2,192,1536]{2,1,0:T(8,128)(2,1)} %get-tuple-element.100.refs_8_.refs_12_), channel_id=1, source_target_pairs={{0,24},{4,28},{8,0},{12,4},{16,8},{20,12},{24,16},{28,20},{1,25},{... | collective-permute-start | bytes 3538952 | tf_op jit(solution)/shard_map/ppermute | solution.py:547
  162.3 52.2 %collective-permute-start.23 = (bf16[2,192,1536]{2,1,0:T(8,128)(2,1)}, bf16[2,192,1536]{2,1,0:T(8,128)(2,1)}, u32[]{:S(2)}, u32[]{:S(2)}) collective-permute-start(bf16[2,192,1536]{2,1,0:T(8,128)(2,1)} %collective-permute-done.15.refs_9_.refs_13_), channel_id=1, source_target_pairs={{0,8},{4,12},{8,16},{12,20},{16,24},{20,28},{24,0},{28,4},{1,9},{5... | collective-permute-start | bytes 3538952 | tf_op jit(solution)/shard_map/ppermute | solution.py:547
  203.8 38.8 %collective-permute-start.22 = (bf16[2,192,1536]{2,1,0:T(8,128)(2,1)}, bf16[2,192,1536]{2,1,0:T(8,128)(2,1)}, u32[]{:S(2)}, u32[]{:S(2)}) collective-permute-start(bf16[2,192,1536]{2,1,0:T(8,128)(2,1)} %get-tuple-element.97), channel_id=1, source_target_pairs={{0,8},{4,12},{8,16},{12,20},{16,24},{20,28},{24,0},{28,4},{1,9},{5... | collective-permute-start | bytes 3538952 | tf_op jit(solution)/shard_map/ppermute | solution.py:547
  203.8 60.7 %collective-permute-start.27 = (bf16[2,192,1536]{2,1,0:T(8,128)(2,1)}, bf16[2,192,1536]{2,1,0:T(8,128)(2,1)}, u32[]{:S(2)}, u32[]{:S(2)}) collective-permute-start(bf16[2,192,1536]{2,1,0:T(8,128)(2,1)} %get-tuple-element.107), channel_id=1, source_target_pairs={{0,24},{4,28},{8,0},{12,4},{16,8},{20,12},{24,16},{28,20},{1,25},{... | collective-permute-start | bytes 3538952 | tf_op jit(solution)/shard_map/ppermute | solution.py:547
  273.4 39.9 %collective-permute-start.32 = (bf16[2,192,1536]{2,1,0:T(8,128)(2,1)S(1)}, bf16[2,192,1536]{2,1,0:T(8,128)(2,1)S(1)}, u32[]{:S(2)}, u32[]{:S(2)}) collective-permute-start(bf16[2,192,1536]{2,1,0:T(8,128)(2,1)S(1)} %add_convert_fusion.3), channel_id=1, source_target_pairs={{0,8},{4,12},{8,16},{12,20},{16,24},{20,28},{24,0},{28,4},{1,9},{5... | collective-permute-start | bytes 3538952 | tf_op jit(solution)/shard_map/ppermute | solution.py:547
  281.7 38.7 %collective-permute-start.34 = (bf16[832,384]{1,0:T(8,128)(2,1)}, bf16[832,384]{1,0:T(8,128)(2,1)}, u32[]{:S(2)}, u32[]{:S(2)}) collective-permute-start(bf16[832,384]{1,0:T(8,128)(2,1)} %get-tuple-element.125), channel_id=1, source_target_pairs={{0,1},{1,0},{2,3},{3,2},{4,5},{5,4},{6,7},{7,6},{8,9},{9,8},{10,11... | collective-permute-start | bytes 1916936 | tf_op jit(solution)/shard_map/ppermute | solution.py:541
  326.6 44.8 %collective-permute-start.38 = (bf16[2,192,1536]{2,1,0:T(8,128)(2,1)}, bf16[2,192,1536]{2,1,0:T(8,128)(2,1)}, u32[]{:S(2)}, u32[]{:S(2)}) collective-permute-start(bf16[2,192,1536]{2,1,0:T(8,128)(2,1)} %get-tuple-element.135), channel_id=1, source_target_pairs={{0,24},{4,28},{8,0},{12,4},{16,8},{20,12},{24,16},{28,20},{1,25},{... | collective-permute-start | bytes 3538952 | tf_op jit(solution)/shard_map/ppermute | solution.py:547
  329.8 53.2 %collective-permute-start.45 = (bf16[2,192,1536]{2,1,0:T(8,128)(2,1)}, bf16[2,192,1536]{2,1,0:T(8,128)(2,1)}, u32[]{:S(2)}, u32[]{:S(2)}) collective-permute-start(bf16[2,192,1536]{2,1,0:T(8,128)(2,1)} %get-tuple-element.147), channel_id=1, source_target_pairs={{0,8},{4,12},{8,16},{12,20},{16,24},{20,28},{24,0},{28,4},{1,9},{5... | collective-permute-start | bytes 3538952 | tf_op jit(solution)/shard_map/ppermute | solution.py:547
  345.1 30.0 %collective-permute-start.37 = (bf16[832,768]{1,0:T(8,128)(2,1)}, bf16[832,768]{1,0:T(8,128)(2,1)}, u32[]{:S(2)}, u32[]{:S(2)}) collective-permute-start(bf16[832,768]{1,0:T(8,128)(2,1)} %combine.6), channel_id=1, source_target_pairs={{0,1},{1,0},{2,3},{3,2},{4,5},{5,4},{6,7},{7,6},{8,9},{9,8},{10,11... | collective-permute-start | bytes 3833864 | tf_op jit(solution)/shard_map/ppermute | solution.py:541
  385.0 31.1 %collective-permute-start.46 = (bf16[2,192,1536]{2,1,0:T(8,128)(2,1)S(1)}, bf16[2,192,1536]{2,1,0:T(8,128)(2,1)S(1)}, u32[]{:S(2)}, u32[]{:S(2)}) collective-permute-start(bf16[2,192,1536]{2,1,0:T(8,128)(2,1)S(1)} %add_convert_fusion.2), channel_id=1, source_target_pairs={{0,8},{4,12},{8,16},{12,20},{16,24},{20,28},{24,0},{28,4},{1,9},{5... | collective-permute-start | bytes 3538952 | tf_op jit(solution)/shard_map/ppermute | solution.py:547
  389.8 28.7 %collective-permute-start.44 = (f32[2,832]{0,1:T(8,128)}, f32[2,832]{0,1:T(8,128)S(1)}, u32[]{:S(2)}, u32[]{:S(2)}) collective-permute-start(f32[2,832]{0,1:T(8,128)} %slice_bitcast_fusion.2), channel_id=1, source_target_pairs={{0,2},{2,0},{1,3},{3,1},{4,6},{6,4},{5,7},{7,5},{8,10},{10,8},{9,1... | collective-permute-start | bytes 19976 | tf_op jit(solution)/shard_map/ppermute | solution.py:541
  392.2 31.2 %collective-permute-start.43 = (bf16[832,384]{1,0:T(8,128)(2,1)}, bf16[832,384]{1,0:T(8,128)(2,1)}, u32[]{:S(2)}, u32[]{:S(2)}) collective-permute-start(bf16[832,384]{1,0:T(8,128)(2,1)} %dynamic-slice_bitcast_fusion), channel_id=1, source_target_pairs={{0,2},{2,0},{1,3},{3,1},{4,6},{6,4},{5,7},{7,5},{8,10},{10,8},{9,1... | collective-permute-start | bytes 1916936 | tf_op jit(solution)/shard_map/ppermute | solution.py:541
  399.0 29.0 %collective-permute-start.40 = (bf16[832,384]{1,0:T(8,128)(2,1)S(1)}, bf16[832,384]{1,0:T(8,128)(2,1)S(1)}, u32[]{:S(2)}, u32[]{:S(2)}) collective-permute-start(bf16[832,384]{1,0:T(8,128)(2,1)S(1)} %constant_dynamic-slice_fusion), channel_id=1, source_target_pairs={{0,2},{2,0},{1,3},{3,1},{4,6},{6,4},{5,7},{7,5},{8,10},{10,8},{9,1... | collective-permute-start | bytes 1916936 | tf_op jit(solution)/shard_map/ppermute | solution.py:541
  405.3 23.0 %collective-permute-start.48 = (bf16[48,1664]{1,0:T(8,128)(2,1)S(1)}, bf16[48,1664]{1,0:T(8,128)(2,1)S(1)}, u32[]{:S(2)}, u32[]{:S(2)}) collective-permute-start(bf16[48,1664]{1,0:T(8,128)(2,1)S(1)} %get-tuple-element.227), channel_id=1, source_target_pairs={{0,16},{4,20},{8,24},{12,28},{16,0},{20,4},{24,8},{28,12},{1,17},{... | collective-permute-start | bytes 479240 | tf_op jit(solution)/shard_map/ppermute | solution.py:547
  (71 other events, 679.2 us)

commit v4 on v3

--- a/solution.py
+++ b/solution.py
@@ -728,7 +728,7 @@
     arrived_last, down_last = ring_first(last), ring_down(last)
     dsum_other[0] = after(dsum_other[0], ends[0])
 
-    yrows[0] = after(yrows[0], dsum_other[0])
+    yrows[0] = after(yrows[0], dsum[0])
     y_came = [swap_core(combine(slot_cols, yrows, n_exp + k)) for k in range(n_exp)]
     y_from = [
         shift(combine(slot_cols, yrows, k, after(y_came[k], dsum[-1])), "expert", -k)

time: 454 us -> 438 us (0.965)
  waiting for transfers between devices: 162 us -> 147 us
    ppermute x18, waiting for transfers between devices: 115 us -> 105 us  [shift_z(): return lax.ppermute(value, 'dp', pairs)]
    unnamed x99 -> x85, local copies, waits for them, and re-layouts: 17.7 us -> 16 us
  transfers between devices with their start and end apart: 51 -> 51, of which waited for: 24 -> 22; matrix products, arithmetic and copies ran while one was open for 15% -> 16% of each run, Pallas kernels for 34% -> 36%
where the time goes in v4:
time: 438 us; the launch traced here: 429 us
  Pallas kernels  155 us (35%)
  waiting for transfers between devices  147 us (34%)
  starting transfers between devices  47.8 us (11%)
  other arithmetic  45.7 us (10%)
  local copies, waits for them, and re-layouts  31.7 us (7%)
    ppermute x18, waiting for transfers between devices, shift_z(): return lax.ppermute(value, 'dp', pairs)  105 us
    pallas_call x2, Pallas kernels, run_expert(): pl.pallas_call(functools.partial(expert_kernel, index, depth, blocks), gr...  56.3 us
    ppermute x17, waiting for transfers between devices, shift(): lax.ppermute(value, axis, [(i, (i + step) % size) for i in range(size)])  37.4 us
    ppermute x18, starting transfers between devices, shift_z(): return lax.ppermute(value, 'dp', pairs)  25.8 us
    pallas_call x2, Pallas kernels, weight_grad(): pl.pallas_call(functools.partial(weight_grad_kernel, depth), grid_spec=pl...  23.9 us
    pallas_call x4, Pallas kernels, combine_back(): pl.pallas_call(functools.partial(combine_back_kernel, local, add is not N...  21.8 us
    pallas_call x1, Pallas kernels, attend_back(): pl.pallas_call(functools.partial(attend_back_kernel, seq, gain_at, depth)...  20.5 us
    ppermute x17, starting transfers between devices, shift(): lax.ppermute(value, axis, [(i, (i + step) % size) for i in range(size)])  19.6 us
  transfers between devices with their start and end apart: 51, of which 22 were waited for; matrix products, arithmetic and copies ran while one was open for 16% of the time, Pallas kernels for 36%

profile of v4, /device:TPU:0, one launch (start us, length us, event | category | flops | bytes accessed | tf_op | source)
XLA Modules:
  0.0 428.9 jit_solution(12597606066126143190)
XLA Ops:
  39.9 8.3 %collective-permute-done.8 = bf16[4,48,1664]{2,1,0:T(8,128)(2,1)S(1)} collective-permute-done((bf16[4,48,1664]{2,1,0:T(8,128)(2,1)}, bf16[4,48,1664]{2,1,0:T(8,128)(2,1)S(1)}, u32[]{:S(2)}, u32[]{:S(2)}) %collective-permute-start.8) | collective-permute-done | bytes 639008 | tf_op jit(solution)/shard_map/ppermute | solution.py:541
  49.6 14.3 %collective-permute-done.9.refs_9_.refs_13_ = bf16[2,192,1536]{2,1,0:T(8,128)(2,1)} collective-permute-done((bf16[2,192,1536]{2,1,0:T(8,128)(2,1)S(1)}, bf16[2,192,1536]{2,1,0:T(8,128)(2,1)}, u32[]{:S(2)}, u32[]{:S(2)}) %collective-permute-start.9) | collective-permute-done | bytes 1179680 | tf_op jit(solution)/shard_map/ppermute | solution.py:547
  68.9 10.8 %attend.1 = (bf16[832,768]{1,0:T(8,128)(2,1)}, bf16[832,1152]{1,0:T(8,128)(2,1)}, bf16[832,384]{1,0:T(8,128)(2,1)}) custom-call(bf16[832,768]{1,0:T(8,128)(2,1)} %pad_maximum_fusion.3.x_ref, bf16[768,1664]{1,0:T(8,128)(2,1)} %bitcast.129, bf16[768,1664]{1,0:T(8,128)(2,1)} %bitcast.130, bf16[768,1664]{1,0:T(8,128)(2,1)} %bitcast.131), custom_call_target="tpu_custom_call" | custom-call | flops 38338560 | bytes 79872 | tf_op jit(solution)/shard_map/attend/pallas_call | solution.py:96
  79.7 12.6 %collective-permute-done.12.refs_11_.refs_15_ = bf16[2,192,1536]{2,1,0:T(8,128)(2,1)S(1)} collective-permute-done((bf16[2,192,1536]{2,1,0:T(8,128)(2,1)S(1)}, bf16[2,192,1536]{2,1,0:T(8,128)(2,1)S(1)}, u32[]{:S(2)}, u32[]{:S(2)}) %collective-permute-start.12) | collective-permute-done | bytes 1179680 | tf_op jit(solution)/shard_map/ppermute | solution.py:547
  94.5 6.4 %find_slots.1 = (s32[4,2,832]{2,1,0:T(2,128)}, s32[4,832,2]{2,1,0:T(8,128)}) custom-call(s32[2]{0:T(128)} %pad_add_fusion.1.place_ref, s32[4,2,832]{2,1,0:T(2,128)} %pad_add_fusion.ids_ref), custom_call_target="tpu_custom_call" | custom-call | flops 2768896 | bytes 3328 | tf_op jit(solution)/shard_map/find_slots/pallas_call | solution.py:252
  103.0 20.2 %collective-permute-done.14.refs_10_.refs_14_ = bf16[2,192,1536]{2,1,0:T(8,128)(2,1)S(1)} collective-permute-done((bf16[2,192,1536]{2,1,0:T(8,128)(2,1)}, bf16[2,192,1536]{2,1,0:T(8,128)(2,1)S(1)}, u32[]{:S(2)}, u32[]{:S(2)}) %collective-permute-start.14) | collective-permute-done | bytes 1179680 | tf_op jit(solution)/shard_map/ppermute | solution.py:547
  130.9 27.7 %collective-permute-done.15.refs_9_.refs_13_ = bf16[2,192,1536]{2,1,0:T(8,128)(2,1)} collective-permute-done((bf16[2,192,1536]{2,1,0:T(8,128)(2,1)}, bf16[2,192,1536]{2,1,0:T(8,128)(2,1)}, u32[]{:S(2)}, u32[]{:S(2)}) %collective-permute-start.15) | collective-permute-done | bytes 1179680 | tf_op jit(solution)/shard_map/ppermute | solution.py:547
  163.7 28.1 %expert.2 = (bf16[2,4,288,768]{3,2,1,0:T(8,128)(2,1)}, bf16[2,4,288,1536]{3,2,1,0:T(8,128)(2,1)}, f32[4,1,832]{2,1,0:T(1,128)}, bf16[4,288,768]{2,1,0:T(8,128)(2...) custom-call(s32[2]{0:T(128)} %pad_add_fusion.1.place_ref, s32[4,2,832]{2,1,0:T(2,128)} %get-tuple-element.90.slot_ref, ...), custom_call_target="tpu_custom_call" | custom-call | flops 215875584 | bytes 221184 | tf_op jit(solution)/shard_map/expert/pallas_call | solution.py:355
  191.8 11.9 %weight_grad.2 = (bf16[2,192,1536]{2,1,0:T(8,128)(2,1)}, bf16[2,192,1536]{2,1,0:T(8,128)(2,1)}, bf16[2,192,1536]{2,1,0:T(8,128)(2,1)}, bf16[2,192,1536]{2,1,0:T(8,128)(2,1)}) custom-call(s32[2]{0:T(128)} %pad_add_fusion.1.place_ref, bf16[2,4,288,768]{3,2,1,0:T(8,128)(2,1)} %get-tuple-element.95.rows_ref, bf16[2,4,288,1536]{3,2,1,0:T(8,128)(2,1)} %get-tuple-element.96.cols_ref), custom_call_target="tpu_custom_call" | custom-call | flops 84934656 | bytes 239616 | tf_op jit(solution)/shard_map/weight_grad/pallas_call | solution.py:403
  203.7 4.2 collective-permute-start.27
  208.5 6.1 %collective-permute-done.23.refs_10_.refs_14_ = bf16[2,192,1536]{2,1,0:T(8,128)(2,1)} collective-permute-done((bf16[2,192,1536]{2,1,0:T(8,128)(2,1)}, bf16[2,192,1536]{2,1,0:T(8,128)(2,1)}, u32[]{:S(2)}, u32[]{:S(2)}) %collective-permute-start.23) | collective-permute-done | bytes 1179680 | tf_op jit(solution)/shard_map/ppermute | solution.py:547
  214.6 28.2 %expert.3 = (bf16[2,4,288,768]{3,2,1,0:T(8,128)(2,1)}, bf16[2,4,288,1536]{3,2,1,0:T(8,128)(2,1)}, f32[4,1,832]{2,1,0:T(1,128)}, bf16[4,288,768]{2,1,0:T(8,128)(2...) custom-call(s32[2]{0:T(128)} %pad_add_fusion.2.place_ref, s32[4,2,832]{2,1,0:T(2,128)} %get-tuple-element.90.slot_ref, ...), custom_call_target="tpu_custom_call" | custom-call | flops 215875584 | bytes 221184 | tf_op jit(solution)/shard_map/expert/pallas_call | solution.py:355
  242.8 5.3 %combine_back.5 = (bf16[832,384]{1,0:T(8,128)(2,1)}, bf16[832,384]{1,0:T(8,128)(2,1)}, f32[8,768]{1,0:T(8,128)}) custom-call(s32[2]{0:T(128)} %pad_add_fusion.1.place_ref, s32[4,832,2]{2,1,0:T(8,128)} %get-tuple-element.88.slot_ref, bf16[4,288,768]{2,1,0:T(8,128)(2,1)} %get-tuple-element.98.refs_0_, bf16[4,288,768]{2,1,0:T(8,128)(2,1)} %get-tuple-element.101.refs_1_, ...), custom_call_target="tpu_custom_call" | custom-call | flops 11501568 | bytes 73728 | tf_op jit(solution)/shard_map/combine_back/pallas_call | solution.py:493
  248.6 5.2 %combine_back.4 = (bf16[832,384]{1,0:T(8,128)(2,1)}, bf16[832,384]{1,0:T(8,128)(2,1)}, f32[8,768]{1,0:T(8,128)}) custom-call(s32[2]{0:T(128)} %pad_add_fusion.1.place_ref, s32[4,832,2]{2,1,0:T(8,128)} %get-tuple-element.88.slot_ref, bf16[4,288,768]{2,1,0:T(8,128)(2,1)} %get-tuple-element.98.refs_0_, bf16[4,288,768]{2,1,0:T(8,128)(2,1)} %get-tuple-element.101.refs_1_, ...), custom_call_target="tpu_custom_call" | custom-call | flops 11501568 | bytes 73728 | tf_op jit(solution)/shard_map/combine_back/pallas_call | solution.py:493
  254.4 10.3 %collective-permute-done.27 = bf16[2,192,1536]{2,1,0:T(8,128)(2,1)} collective-permute-done((bf16[2,192,1536]{2,1,0:T(8,128)(2,1)}, bf16[2,192,1536]{2,1,0:T(8,128)(2,1)}, u32[]{:S(2)}, u32[]{:S(2)}) %collective-permute-start.27) | collective-permute-done | bytes 1179680 | tf_op jit(solution)/shard_map/ppermute | solution.py:547
  266.3 5.6 %combine_back.6 = (bf16[832,384]{1,0:T(8,128)(2,1)}, bf16[832,384]{1,0:T(8,128)(2,1)}, f32[8,768]{1,0:T(8,128)}) custom-call(s32[2]{0:T(128)} %pad_add_fusion.1.place_ref, s32[4,832,2]{2,1,0:T(8,128)} %get-tuple-element.88.slot_ref, bf16[4,288,768]{2,1,0:T(8,128)(2,1)} %get-tuple-element.98.refs_0_, bf16[4,288,768]{2,1,0:T(8,128)(2,1)} %get-tuple-element.101.refs_1_, ...), custom_call_target="tpu_custom_call" | custom-call | flops 11501568 | bytes 73728 | tf_op jit(solution)/shard_map/combine_back/pallas_call | solution.py:493
  279.1 5.7 %combine_back.7 = (bf16[832,384]{1,0:T(8,128)(2,1)}, bf16[832,384]{1,0:T(8,128)(2,1)}, f32[8,768]{1,0:T(8,128)}) custom-call(s32[2]{0:T(128)} %pad_add_fusion.1.place_ref, s32[4,832,2]{2,1,0:T(8,128)} %get-tuple-element.88.slot_ref, bf16[4,288,768]{2,1,0:T(8,128)(2,1)} %get-tuple-element.98.refs_0_, bf16[4,288,768]{2,1,0:T(8,128)(2,1)} %get-tuple-element.101.refs_1_, ...), custom_call_target="tpu_custom_call" | custom-call | flops 11501568 | bytes 73728 | tf_op jit(solution)/shard_map/combine_back/pallas_call | solution.py:493
  292.4 12.0 %weight_grad.3 = (bf16[2,192,1536]{2,1,0:T(8,128)(2,1)}, bf16[2,192,1536]{2,1,0:T(8,128)(2,1)}, bf16[2,192,1536]{2,1,0:T(8,128)(2,1)}, bf16[2,192,1536]{2,1,0:T(8,128)(2,1)}) custom-call(s32[2]{0:T(128)} %pad_add_fusion.2.place_ref, bf16[2,4,288,768]{3,2,1,0:T(8,128)(2,1)} %get-tuple-element.121.rows_ref, bf16[2,4,288,1536]{3,2,1,0:T(8,128)(2,1)} %get-tuple-element.122.cols_ref), custom_call_target="tpu_custom_call" | custom-call | flops 84934656 | bytes 239616 | tf_op jit(solution)/shard_map/weight_grad/pallas_call | solution.py:403
  320.9 5.4 %collective-permute-done.35 = bf16[832,384]{1,0:T(8,128)(2,1)S(1)} collective-permute-done((bf16[832,384]{1,0:T(8,128)(2,1)S(1)}, bf16[832,384]{1,0:T(8,128)(2,1)S(1)}, u32[]{:S(2)}, u32[]{:S(2)}) %collective-permute-start.35) | collective-permute-done | bytes 639008 | tf_op jit(solution)/shard_map/ppermute | solution.py:541
  326.4 4.1 combine.6
  335.8 20.5 %attend_back.1 = (bf16[2,832,384]{2,1,0:T(8,128)(2,1)}, f32[832,128]{1,0:T(8,128)}, bf16[384,1664]{1,0:T(8,128)(2,1)}, bf16[384,1664]{1,0:T(8,128)(2,1)}) custom-call(s32[1]{0:T(128)} %bitcast.35.core_ref, bf16[832,768]{1,0:T(8,128)(2,1)} %pad_maximum_fusion.3.x_ref, f32[1,768]{1,0:T(1,128)} %copy.165.gain_ref, ...), custom_call_target="tpu_custom_call" | custom-call | flops 107347968 | bytes 119808 | tf_op jit(solution)/shard_map/attend_back/pallas_call | solution.py:193
  356.3 4.4 %collective-permute-done.37 = bf16[832,768]{1,0:T(8,128)(2,1)} collective-permute-done((bf16[832,768]{1,0:T(8,128)(2,1)}, bf16[832,768]{1,0:T(8,128)(2,1)}, u32[]{:S(2)}, u32[]{:S(2)}) %collective-permute-start.37) | collective-permute-done | bytes 1277984 | tf_op jit(solution)/shard_map/ppermute | solution.py:541
  392.3 6.2 %collective-permute-done.46 = bf16[2,192,1536]{2,1,0:T(8,128)(2,1)S(1)} collective-permute-done((bf16[2,192,1536]{2,1,0:T(8,128)(2,1)S(1)}, bf16[2,192,1536]{2,1,0:T(8,128)(2,1)S(1)}, u32[]{:S(2)}, u32[]{:S(2)}) %collective-permute-start.46) | collective-permute-done | bytes 1179680 | tf_op jit(solution)/shard_map/ppermute | solution.py:547
  407.2 4.6 %collective-permute-done.40 = bf16[832,384]{1,0:T(8,128)(2,1)S(1)} collective-permute-done((bf16[832,384]{1,0:T(8,128)(2,1)S(1)}, bf16[832,384]{1,0:T(8,128)(2,1)S(1)}, u32[]{:S(2)}, u32[]{:S(2)}) %collective-permute-start.40) | collective-permute-done | bytes 639008 | tf_op jit(solution)/shard_map/ppermute | solution.py:541
  (265 shorter events, 159.0 us)
Async XLA Ops:
  34.4 29.5 %collective-permute-start.9 = (bf16[2,192,1536]{2,1,0:T(8,128)(2,1)S(1)}, bf16[2,192,1536]{2,1,0:T(8,128)(2,1)}, u32[]{:S(2)}, u32[]{:S(2)}) collective-permute-start(bf16[2,192,1536]{2,1,0:T(8,128)(2,1)S(1)} %get-tuple-element.216.refs_8_.refs_12_), channel_id=1, source_target_pairs={{0,8},{4,12},{8,16},{12,20},{16,24},{20,28},{24,0},{28,4},{1,9},{5... | collective-permute-start | bytes 3538952 | tf_op jit(solution)/shard_map/ppermute | solution.py:547
  63.9 28.4 %collective-permute-start.12 = (bf16[2,192,1536]{2,1,0:T(8,128)(2,1)S(1)}, bf16[2,192,1536]{2,1,0:T(8,128)(2,1)S(1)}, u32[]{:S(2)}, u32[]{:S(2)}) collective-permute-start(bf16[2,192,1536]{2,1,0:T(8,128)(2,1)S(1)} %get-tuple-element.216.refs_8_.refs_12_), channel_id=1, source_target_pairs={{0,24},{4,28},{8,0},{12,4},{16,8},{20,12},{24,16},{28,20},{1,25},{... | collective-permute-start | bytes 3538952 | tf_op jit(solution)/shard_map/ppermute | solution.py:547
  93.3 30.0 %collective-permute-start.13 = (bf16[832,768]{1,0:T(8,128)(2,1)}, bf16[832,768]{1,0:T(8,128)(2,1)}, u32[]{:S(2)}, u32[]{:S(2)}) collective-permute-start(bf16[832,768]{1,0:T(8,128)(2,1)} %get-tuple-element.87), channel_id=1, source_target_pairs={{0,2},{2,0},{1,3},{3,1},{4,6},{6,4},{5,7},{7,5},{8,10},{10,8},{9,1... | collective-permute-start | bytes 3833864 | tf_op jit(solution)/shard_map/ppermute | solution.py:541
  93.8 29.3 %collective-permute-start.14 = (bf16[2,192,1536]{2,1,0:T(8,128)(2,1)}, bf16[2,192,1536]{2,1,0:T(8,128)(2,1)S(1)}, u32[]{:S(2)}, u32[]{:S(2)}) collective-permute-start(bf16[2,192,1536]{2,1,0:T(8,128)(2,1)} %collective-permute-done.9.refs_9_.refs_13_), channel_id=1, source_target_pairs={{0,8},{4,12},{8,16},{12,20},{16,24},{20,28},{24,0},{28,4},{1,9},{5... | collective-permute-start | bytes 3538952 | tf_op jit(solution)/shard_map/ppermute | solution.py:547
  100.9 29.7 %collective-permute-start.19 = (bf16[832,768]{1,0:T(8,128)(2,1)}, bf16[832,768]{1,0:T(8,128)(2,1)}, u32[]{:S(2)}, u32[]{:S(2)}) collective-permute-start(bf16[832,768]{1,0:T(8,128)(2,1)} %pad_maximum_fusion.5.refs_4_), channel_id=1, source_target_pairs={{0,1},{1,0},{2,3},{3,2},{4,5},{5,4},{6,7},{7,6},{8,9},{9,8},{10,11... | collective-permute-start | bytes 3833864 | tf_op jit(solution)/shard_map/ppermute | solution.py:541
  129.8 28.8 %collective-permute-start.16 = (bf16[832,768]{1,0:T(8,128)(2,1)}, bf16[832,768]{1,0:T(8,128)(2,1)}, u32[]{:S(2)}, u32[]{:S(2)}) collective-permute-start(bf16[832,768]{1,0:T(8,128)(2,1)} %multiply_convert_fusion.refs_0_.refs_6_), channel_id=1, source_target_pairs={{0,1},{1,0},{2,3},{3,2},{4,5},{5,4},{6,7},{7,6},{8,9},{9,8},{10,11... | collective-permute-start | bytes 3833864 | tf_op jit(solution)/shard_map/ppermute | solution.py:541
  130.3 28.2 %collective-permute-start.15 = (bf16[2,192,1536]{2,1,0:T(8,128)(2,1)}, bf16[2,192,1536]{2,1,0:T(8,128)(2,1)}, u32[]{:S(2)}, u32[]{:S(2)}) collective-permute-start(bf16[2,192,1536]{2,1,0:T(8,128)(2,1)} %get-tuple-element.100.refs_8_.refs_12_), channel_id=1, source_target_pairs={{0,8},{4,12},{8,16},{12,20},{16,24},{20,28},{24,0},{28,4},{1,9},{5... | collective-permute-start | bytes 3538952 | tf_op jit(solution)/shard_map/ppermute | solution.py:547
  130.4 32.0 %collective-permute-start.20 = (bf16[832,768]{1,0:T(8,128)(2,1)}, bf16[832,768]{1,0:T(8,128)(2,1)}, u32[]{:S(2)}, u32[]{:S(2)}) collective-permute-start(bf16[832,768]{1,0:T(8,128)(2,1)} %pad_maximum_fusion.5.refs_4_), channel_id=1, source_target_pairs={{0,4},{4,0},{8,12},{12,8},{16,20},{20,16},{24,28},{28,24},{1,5},{5... | collective-permute-start | bytes 3833864 | tf_op jit(solution)/shard_map/ppermute | solution.py:550
  130.7 31.8 %collective-permute-start.21 = (bf16[832,768]{1,0:T(8,128)(2,1)}, bf16[832,768]{1,0:T(8,128)(2,1)}, u32[]{:S(2)}, u32[]{:S(2)}) collective-permute-start(bf16[832,768]{1,0:T(8,128)(2,1)} %collective-permute-done.19.refs_5_), channel_id=1, source_target_pairs={{0,4},{4,0},{8,12},{12,8},{16,20},{20,16},{24,28},{28,24},{1,5},{5... | collective-permute-start | bytes 3833864 | tf_op jit(solution)/shard_map/ppermute | solution.py:550
  159.1 49.4 %collective-permute-start.24 = (bf16[2,192,1536]{2,1,0:T(8,128)(2,1)}, bf16[2,192,1536]{2,1,0:T(8,128)(2,1)}, u32[]{:S(2)}, u32[]{:S(2)}) collective-permute-start(bf16[2,192,1536]{2,1,0:T(8,128)(2,1)} %get-tuple-element.100.refs_8_.refs_12_), channel_id=1, source_target_pairs={{0,24},{4,28},{8,0},{12,4},{16,8},{20,12},{24,16},{28,20},{1,25},{... | collective-permute-start | bytes 3538952 | tf_op jit(solution)/shard_map/ppermute | solution.py:547
  162.3 52.3 %collective-permute-start.23 = (bf16[2,192,1536]{2,1,0:T(8,128)(2,1)}, bf16[2,192,1536]{2,1,0:T(8,128)(2,1)}, u32[]{:S(2)}, u32[]{:S(2)}) collective-permute-start(bf16[2,192,1536]{2,1,0:T(8,128)(2,1)} %collective-permute-done.15.refs_9_.refs_13_), channel_id=1, source_target_pairs={{0,8},{4,12},{8,16},{12,20},{16,24},{20,28},{24,0},{28,4},{1,9},{5... | collective-permute-start | bytes 3538952 | tf_op jit(solution)/shard_map/ppermute | solution.py:547
  203.7 39.1 %collective-permute-start.22 = (bf16[2,192,1536]{2,1,0:T(8,128)(2,1)}, bf16[2,192,1536]{2,1,0:T(8,128)(2,1)}, u32[]{:S(2)}, u32[]{:S(2)}) collective-permute-start(bf16[2,192,1536]{2,1,0:T(8,128)(2,1)} %get-tuple-element.97), channel_id=1, source_target_pairs={{0,8},{4,12},{8,16},{12,20},{16,24},{20,28},{24,0},{28,4},{1,9},{5... | collective-permute-start | bytes 3538952 | tf_op jit(solution)/shard_map/ppermute | solution.py:547
  203.7 60.9 %collective-permute-start.27 = (bf16[2,192,1536]{2,1,0:T(8,128)(2,1)}, bf16[2,192,1536]{2,1,0:T(8,128)(2,1)}, u32[]{:S(2)}, u32[]{:S(2)}) collective-permute-start(bf16[2,192,1536]{2,1,0:T(8,128)(2,1)} %get-tuple-element.107), channel_id=1, source_target_pairs={{0,24},{4,28},{8,0},{12,4},{16,8},{20,12},{24,16},{28,20},{1,25},{... | collective-permute-start | bytes 3538952 | tf_op jit(solution)/shard_map/ppermute | solution.py:547
  253.8 25.3 %collective-permute-start.25 = (bf16[832,384]{1,0:T(8,128)(2,1)}, bf16[832,384]{1,0:T(8,128)(2,1)}, u32[]{:S(2)}, u32[]{:S(2)}) collective-permute-start(bf16[832,384]{1,0:T(8,128)(2,1)} %get-tuple-element.105), channel_id=1, source_target_pairs={{0,4},{4,0},{8,12},{12,8},{16,20},{20,16},{24,28},{28,24},{1,5},{5... | collective-permute-start | bytes 1916936 | tf_op jit(solution)/shard_map/ppermute | solution.py:550
  275.0 42.3 %collective-permute-start.33 = (bf16[2,192,1536]{2,1,0:T(8,128)(2,1)}, bf16[2,192,1536]{2,1,0:T(8,128)(2,1)}, u32[]{:S(2)}, u32[]{:S(2)}) collective-permute-start(bf16[2,192,1536]{2,1,0:T(8,128)(2,1)} %add_convert_fusion.3), channel_id=1, source_target_pairs={{0,8},{4,12},{8,16},{12,20},{16,24},{20,28},{24,0},{28,4},{1,9},{5... | collective-permute-start | bytes 3538952 | tf_op jit(solution)/shard_map/ppermute | solution.py:547
  276.8 31.4 %collective-permute-start.34 = (bf16[832,384]{1,0:T(8,128)(2,1)}, bf16[832,384]{1,0:T(8,128)(2,1)}, u32[]{:S(2)}, u32[]{:S(2)}) collective-permute-start(bf16[832,384]{1,0:T(8,128)(2,1)} %get-tuple-element.125), channel_id=1, source_target_pairs={{0,1},{1,0},{2,3},{3,2},{4,5},{5,4},{6,7},{7,6},{8,9},{9,8},{10,11... | collective-permute-start | bytes 1916936 | tf_op jit(solution)/shard_map/ppermute | solution.py:541
  290.9 29.9 %collective-permute-start.32 = (bf16[832,384]{1,0:T(8,128)(2,1)S(1)}, bf16[832,384]{1,0:T(8,128)(2,1)S(1)}, u32[]{:S(2)}, u32[]{:S(2)}) collective-permute-start(bf16[832,384]{1,0:T(8,128)(2,1)S(1)} %add_convert_fusion.6), channel_id=1, source_target_pairs={{0,2},{2,0},{1,3},{3,1},{4,6},{6,4},{5,7},{7,5},{8,10},{10,8},{9,1... | collective-permute-start | bytes 1916936 | tf_op jit(solution)/shard_map/ppermute | solution.py:541
  310.0 46.3 %collective-permute-start.38 = (bf16[2,192,1536]{2,1,0:T(8,128)(2,1)}, bf16[2,192,1536]{2,1,0:T(8,128)(2,1)}, u32[]{:S(2)}, u32[]{:S(2)}) collective-permute-start(bf16[2,192,1536]{2,1,0:T(8,128)(2,1)} %get-tuple-element.135), channel_id=1, source_target_pairs={{0,24},{4,28},{8,0},{12,4},{16,8},{20,12},{24,16},{28,20},{1,25},{... | collective-permute-start | bytes 3538952 | tf_op jit(solution)/shard_map/ppermute | solution.py:547
  317.3 48.3 %collective-permute-start.45 = (bf16[2,192,1536]{2,1,0:T(8,128)(2,1)}, bf16[2,192,1536]{2,1,0:T(8,128)(2,1)}, u32[]{:S(2)}, u32[]{:S(2)}) collective-permute-start(bf16[2,192,1536]{2,1,0:T(8,128)(2,1)} %get-tuple-element.147), channel_id=1, source_target_pairs={{0,8},{4,12},{8,16},{12,20},{16,24},{20,28},{24,0},{28,4},{1,9},{5... | collective-permute-start | bytes 3538952 | tf_op jit(solution)/shard_map/ppermute | solution.py:547
  330.6 30.1 %collective-permute-start.37 = (bf16[832,768]{1,0:T(8,128)(2,1)}, bf16[832,768]{1,0:T(8,128)(2,1)}, u32[]{:S(2)}, u32[]{:S(2)}) collective-permute-start(bf16[832,768]{1,0:T(8,128)(2,1)} %combine.6), channel_id=1, source_target_pairs={{0,1},{1,0},{2,3},{3,2},{4,5},{5,4},{6,7},{7,6},{8,9},{9,8},{10,11... | collective-permute-start | bytes 3833864 | tf_op jit(solution)/shard_map/ppermute | solution.py:541
  367.5 31.0 %collective-permute-start.46 = (bf16[2,192,1536]{2,1,0:T(8,128)(2,1)S(1)}, bf16[2,192,1536]{2,1,0:T(8,128)(2,1)S(1)}, u32[]{:S(2)}, u32[]{:S(2)}) collective-permute-start(bf16[2,192,1536]{2,1,0:T(8,128)(2,1)S(1)} %add_convert_fusion.2), channel_id=1, source_target_pairs={{0,8},{4,12},{8,16},{12,20},{16,24},{20,28},{24,0},{28,4},{1,9},{5... | collective-permute-start | bytes 3538952 | tf_op jit(solution)/shard_map/ppermute | solution.py:547
  373.6 29.4 %collective-permute-start.44 = (f32[2,832]{0,1:T(8,128)}, f32[2,832]{0,1:T(8,128)S(1)}, u32[]{:S(2)}, u32[]{:S(2)}) collective-permute-start(f32[2,832]{0,1:T(8,128)} %slice_bitcast_fusion.2), channel_id=1, source_target_pairs={{0,2},{2,0},{1,3},{3,1},{4,6},{6,4},{5,7},{7,5},{8,10},{10,8},{9,1... | collective-permute-start | bytes 19976 | tf_op jit(solution)/shard_map/ppermute | solution.py:541
  376.0 31.2 %collective-permute-start.43 = (bf16[832,384]{1,0:T(8,128)(2,1)}, bf16[832,384]{1,0:T(8,128)(2,1)}, u32[]{:S(2)}, u32[]{:S(2)}) collective-permute-start(bf16[832,384]{1,0:T(8,128)(2,1)} %dynamic-slice_bitcast_fusion), channel_id=1, source_target_pairs={{0,2},{2,0},{1,3},{3,1},{4,6},{6,4},{5,7},{7,5},{8,10},{10,8},{9,1... | collective-permute-start | bytes 1916936 | tf_op jit(solution)/shard_map/ppermute | solution.py:541
  382.7 29.0 %collective-permute-start.40 = (bf16[832,384]{1,0:T(8,128)(2,1)S(1)}, bf16[832,384]{1,0:T(8,128)(2,1)S(1)}, u32[]{:S(2)}, u32[]{:S(2)}) collective-permute-start(bf16[832,384]{1,0:T(8,128)(2,1)S(1)} %constant_dynamic-slice_fusion), channel_id=1, source_target_pairs={{0,2},{2,0},{1,3},{3,1},{4,6},{6,4},{5,7},{7,5},{8,10},{10,8},{9,1... | collective-permute-start | bytes 1916936 | tf_op jit(solution)/shard_map/ppermute | solution.py:541
  (64 other events, 651.0 us)

commit v5 on v4

--- a/solution.py
+++ b/solution.py
@@ -305,8 +305,6 @@
     gate = jnp.sum(jnp.where(mask, own, 0.0), axis=1, keepdims=True)
     grows, rows = rows_ref[0, 0], rows_ref[1, 0]
     dgate = jnp.zeros((slots, 1), F32)
-    drows = jnp.zeros((slots, model), F32)
-    yrows = jnp.zeros((slots, model), F32)
     tile = 512 if width % 512 == 0 else width
     curve = 0.7978845608028654
 
@@ -332,11 +330,9 @@
         dhid = (gate * pulled * slope).astype(BF16)
         mids_ref[0, 0, :, cols] = gact
         mids_ref[1, 0, :, cols] = dhid
-        drows = drows + dot(dhid, win_all[:, cols], 1, 1)
-        yrows = yrows + dot(gact, wout_all[:, cols], 1, 1)
     dchosen_ref[0] = jnp.sum(jnp.where(mask, dgate, 0.0), axis=0, keepdims=True)
-    drows_ref[0] = drows.astype(BF16)
-    yrows_ref[0] = yrows.astype(BF16)
+    drows_ref[0] = dot(mids_ref[1, 0], win_all[...], 1, 1).astype(BF16)
+    yrows_ref[0] = dot(mids_ref[0, 0], wout_all[...], 1, 1).astype(BF16)
 
 
 def run_expert(index, place, slot_of, router_rows, xs, grads, pieces, slots):

time: 438 us -> 438 us (level)
  no operation moved by 1% of the time
where the time goes in v5:
time: 438 us; the launch traced here: 429 us
  Pallas kernels  156 us (36%)
  waiting for transfers between devices  146 us (33%)
  starting transfers between devices  47.8 us (11%)
  other arithmetic  45.7 us (10%)
  local copies, waits for them, and re-layouts  31.7 us (7%)
    ppermute x18, waiting for transfers between devices, shift_z(): return lax.ppermute(value, 'dp', pairs)  104 us
    pallas_call x2, Pallas kernels, run_expert(): pl.pallas_call(functools.partial(expert_kernel, index, depth, blocks), gr...  57.3 us
    ppermute x17, waiting for transfers between devices, shift(): lax.ppermute(value, axis, [(i, (i + step) % size) for i in range(size)])  37.4 us
    ppermute x18, starting transfers between devices, shift_z(): return lax.ppermute(value, 'dp', pairs)  25.8 us
    pallas_call x2, Pallas kernels, weight_grad(): pl.pallas_call(functools.partial(weight_grad_kernel, depth), grid_spec=pl...  23.9 us
    pallas_call x4, Pallas kernels, combine_back(): pl.pallas_call(functools.partial(combine_back_kernel, local, add is not N...  21.8 us
    pallas_call x1, Pallas kernels, attend_back(): pl.pallas_call(functools.partial(attend_back_kernel, seq, gain_at, depth)...  20.5 us
    ppermute x17, starting transfers between devices, shift(): lax.ppermute(value, axis, [(i, (i + step) % size) for i in range(size)])  19.6 us
  transfers between devices with their start and end apart: 51, of which 22 were waited for; matrix products, arithmetic and copies ran while one was open for 16% of the time, Pallas kernels for 36%

profile of v5, /device:TPU:0, one launch (start us, length us, event | category | flops | bytes accessed | tf_op | source)
XLA Modules:
  0.0 428.9 jit_solution(11217187882439141001)
XLA Ops:
  39.9 8.3 %collective-permute-done.8 = bf16[4,48,1664]{2,1,0:T(8,128)(2,1)S(1)} collective-permute-done((bf16[4,48,1664]{2,1,0:T(8,128)(2,1)}, bf16[4,48,1664]{2,1,0:T(8,128)(2,1)S(1)}, u32[]{:S(2)}, u32[]{:S(2)}) %collective-permute-start.8) | collective-permute-done | bytes 639008 | tf_op jit(solution)/shard_map/ppermute | solution.py:537
  49.6 14.3 %collective-permute-done.9.refs_9_.refs_13_ = bf16[2,192,1536]{2,1,0:T(8,128)(2,1)} collective-permute-done((bf16[2,192,1536]{2,1,0:T(8,128)(2,1)S(1)}, bf16[2,192,1536]{2,1,0:T(8,128)(2,1)}, u32[]{:S(2)}, u32[]{:S(2)}) %collective-permute-start.9) | collective-permute-done | bytes 1179680 | tf_op jit(solution)/shard_map/ppermute | solution.py:543
  68.9 10.8 %attend.1 = (bf16[832,768]{1,0:T(8,128)(2,1)}, bf16[832,1152]{1,0:T(8,128)(2,1)}, bf16[832,384]{1,0:T(8,128)(2,1)}) custom-call(bf16[832,768]{1,0:T(8,128)(2,1)} %pad_maximum_fusion.3.x_ref, bf16[768,1664]{1,0:T(8,128)(2,1)} %bitcast.129, bf16[768,1664]{1,0:T(8,128)(2,1)} %bitcast.130, bf16[768,1664]{1,0:T(8,128)(2,1)} %bitcast.131), custom_call_target="tpu_custom_call" | custom-call | flops 38338560 | bytes 79872 | tf_op jit(solution)/shard_map/attend/pallas_call | solution.py:96
  79.7 12.6 %collective-permute-done.12.refs_11_.refs_15_ = bf16[2,192,1536]{2,1,0:T(8,128)(2,1)S(1)} collective-permute-done((bf16[2,192,1536]{2,1,0:T(8,128)(2,1)S(1)}, bf16[2,192,1536]{2,1,0:T(8,128)(2,1)S(1)}, u32[]{:S(2)}, u32[]{:S(2)}) %collective-permute-start.12) | collective-permute-done | bytes 1179680 | tf_op jit(solution)/shard_map/ppermute | solution.py:543
  94.5 6.4 %find_slots.1 = (s32[4,2,832]{2,1,0:T(2,128)}, s32[4,832,2]{2,1,0:T(8,128)}) custom-call(s32[2]{0:T(128)} %pad_add_fusion.1.place_ref, s32[4,2,832]{2,1,0:T(2,128)} %pad_add_fusion.ids_ref), custom_call_target="tpu_custom_call" | custom-call | flops 2768896 | bytes 3328 | tf_op jit(solution)/shard_map/find_slots/pallas_call | solution.py:252
  103.0 20.2 %collective-permute-done.14.refs_10_.refs_14_ = bf16[2,192,1536]{2,1,0:T(8,128)(2,1)S(1)} collective-permute-done((bf16[2,192,1536]{2,1,0:T(8,128)(2,1)}, bf16[2,192,1536]{2,1,0:T(8,128)(2,1)S(1)}, u32[]{:S(2)}, u32[]{:S(2)}) %collective-permute-start.14) | collective-permute-done | bytes 1179680 | tf_op jit(solution)/shard_map/ppermute | solution.py:543
  130.9 27.7 %collective-permute-done.15.refs_9_.refs_13_ = bf16[2,192,1536]{2,1,0:T(8,128)(2,1)} collective-permute-done((bf16[2,192,1536]{2,1,0:T(8,128)(2,1)}, bf16[2,192,1536]{2,1,0:T(8,128)(2,1)}, u32[]{:S(2)}, u32[]{:S(2)}) %collective-permute-start.15) | collective-permute-done | bytes 1179680 | tf_op jit(solution)/shard_map/ppermute | solution.py:543
  163.7 28.6 %expert.2 = (bf16[2,4,288,768]{3,2,1,0:T(8,128)(2,1)}, bf16[2,4,288,1536]{3,2,1,0:T(8,128)(2,1)}, f32[4,1,832]{2,1,0:T(1,128)}, bf16[4,288,768]{2,1,0:T(8,128)(2...) custom-call(s32[2]{0:T(128)} %pad_add_fusion.1.place_ref, s32[4,2,832]{2,1,0:T(2,128)} %get-tuple-element.90.slot_ref, ...), custom_call_target="tpu_custom_call" | custom-call | flops 215875584 | bytes 221184 | tf_op jit(solution)/shard_map/expert/pallas_call | solution.py:351
  192.3 11.9 %weight_grad.2 = (bf16[2,192,1536]{2,1,0:T(8,128)(2,1)}, bf16[2,192,1536]{2,1,0:T(8,128)(2,1)}, bf16[2,192,1536]{2,1,0:T(8,128)(2,1)}, bf16[2,192,1536]{2,1,0:T(8,128)(2,1)}) custom-call(s32[2]{0:T(128)} %pad_add_fusion.1.place_ref, bf16[2,4,288,768]{3,2,1,0:T(8,128)(2,1)} %get-tuple-element.95.rows_ref, bf16[2,4,288,1536]{3,2,1,0:T(8,128)(2,1)} %get-tuple-element.96.cols_ref), custom_call_target="tpu_custom_call" | custom-call | flops 84934656 | bytes 239616 | tf_op jit(solution)/shard_map/weight_grad/pallas_call | solution.py:399
  204.2 4.2 collective-permute-start.27
  209.0 5.6 %collective-permute-done.23.refs_10_.refs_14_ = bf16[2,192,1536]{2,1,0:T(8,128)(2,1)} collective-permute-done((bf16[2,192,1536]{2,1,0:T(8,128)(2,1)}, bf16[2,192,1536]{2,1,0:T(8,128)(2,1)}, u32[]{:S(2)}, u32[]{:S(2)}) %collective-permute-start.23) | collective-permute-done | bytes 1179680 | tf_op jit(solution)/shard_map/ppermute | solution.py:543
  214.6 28.7 %expert.3 = (bf16[2,4,288,768]{3,2,1,0:T(8,128)(2,1)}, bf16[2,4,288,1536]{3,2,1,0:T(8,128)(2,1)}, f32[4,1,832]{2,1,0:T(1,128)}, bf16[4,288,768]{2,1,0:T(8,128)(2...) custom-call(s32[2]{0:T(128)} %pad_add_fusion.2.place_ref, s32[4,2,832]{2,1,0:T(2,128)} %get-tuple-element.90.slot_ref, ...), custom_call_target="tpu_custom_call" | custom-call | flops 215875584 | bytes 221184 | tf_op jit(solution)/shard_map/expert/pallas_call | solution.py:351
  243.3 5.3 %combine_back.5 = (bf16[832,384]{1,0:T(8,128)(2,1)}, bf16[832,384]{1,0:T(8,128)(2,1)}, f32[8,768]{1,0:T(8,128)}) custom-call(s32[2]{0:T(128)} %pad_add_fusion.1.place_ref, s32[4,832,2]{2,1,0:T(8,128)} %get-tuple-element.88.slot_ref, bf16[4,288,768]{2,1,0:T(8,128)(2,1)} %get-tuple-element.98.refs_0_, bf16[4,288,768]{2,1,0:T(8,128)(2,1)} %get-tuple-element.101.refs_1_, ...), custom_call_target="tpu_custom_call" | custom-call | flops 11501568 | bytes 73728 | tf_op jit(solution)/shard_map/combine_back/pallas_call | solution.py:489
  249.1 5.2 %combine_back.4 = (bf16[832,384]{1,0:T(8,128)(2,1)}, bf16[832,384]{1,0:T(8,128)(2,1)}, f32[8,768]{1,0:T(8,128)}) custom-call(s32[2]{0:T(128)} %pad_add_fusion.1.place_ref, s32[4,832,2]{2,1,0:T(8,128)} %get-tuple-element.88.slot_ref, bf16[4,288,768]{2,1,0:T(8,128)(2,1)} %get-tuple-element.98.refs_0_, bf16[4,288,768]{2,1,0:T(8,128)(2,1)} %get-tuple-element.101.refs_1_, ...), custom_call_target="tpu_custom_call" | custom-call | flops 11501568 | bytes 73728 | tf_op jit(solution)/shard_map/combine_back/pallas_call | solution.py:489
  254.8 9.8 %collective-permute-done.27 = bf16[2,192,1536]{2,1,0:T(8,128)(2,1)} collective-permute-done((bf16[2,192,1536]{2,1,0:T(8,128)(2,1)}, bf16[2,192,1536]{2,1,0:T(8,128)(2,1)}, u32[]{:S(2)}, u32[]{:S(2)}) %collective-permute-start.27) | collective-permute-done | bytes 1179680 | tf_op jit(solution)/shard_map/ppermute | solution.py:543
  266.3 5.6 %combine_back.6 = (bf16[832,384]{1,0:T(8,128)(2,1)}, bf16[832,384]{1,0:T(8,128)(2,1)}, f32[8,768]{1,0:T(8,128)}) custom-call(s32[2]{0:T(128)} %pad_add_fusion.1.place_ref, s32[4,832,2]{2,1,0:T(8,128)} %get-tuple-element.88.slot_ref, bf16[4,288,768]{2,1,0:T(8,128)(2,1)} %get-tuple-element.98.refs_0_, bf16[4,288,768]{2,1,0:T(8,128)(2,1)} %get-tuple-element.101.refs_1_, ...), custom_call_target="tpu_custom_call" | custom-call | flops 11501568 | bytes 73728 | tf_op jit(solution)/shard_map/combine_back/pallas_call | solution.py:489
  279.1 5.7 %combine_back.7 = (bf16[832,384]{1,0:T(8,128)(2,1)}, bf16[832,384]{1,0:T(8,128)(2,1)}, f32[8,768]{1,0:T(8,128)}) custom-call(s32[2]{0:T(128)} %pad_add_fusion.1.place_ref, s32[4,832,2]{2,1,0:T(8,128)} %get-tuple-element.88.slot_ref, bf16[4,288,768]{2,1,0:T(8,128)(2,1)} %get-tuple-element.98.refs_0_, bf16[4,288,768]{2,1,0:T(8,128)(2,1)} %get-tuple-element.101.refs_1_, ...), custom_call_target="tpu_custom_call" | custom-call | flops 11501568 | bytes 73728 | tf_op jit(solution)/shard_map/combine_back/pallas_call | solution.py:489
  292.4 12.0 %weight_grad.3 = (bf16[2,192,1536]{2,1,0:T(8,128)(2,1)}, bf16[2,192,1536]{2,1,0:T(8,128)(2,1)}, bf16[2,192,1536]{2,1,0:T(8,128)(2,1)}, bf16[2,192,1536]{2,1,0:T(8,128)(2,1)}) custom-call(s32[2]{0:T(128)} %pad_add_fusion.2.place_ref, bf16[2,4,288,768]{3,2,1,0:T(8,128)(2,1)} %get-tuple-element.121.rows_ref, bf16[2,4,288,1536]{3,2,1,0:T(8,128)(2,1)} %get-tuple-element.122.cols_ref), custom_call_target="tpu_custom_call" | custom-call | flops 84934656 | bytes 239616 | tf_op jit(solution)/shard_map/weight_grad/pallas_call | solution.py:399
  320.9 5.4 %collective-permute-done.35 = bf16[832,384]{1,0:T(8,128)(2,1)S(1)} collective-permute-done((bf16[832,384]{1,0:T(8,128)(2,1)S(1)}, bf16[832,384]{1,0:T(8,128)(2,1)S(1)}, u32[]{:S(2)}, u32[]{:S(2)}) %collective-permute-start.35) | collective-permute-done | bytes 639008 | tf_op jit(solution)/shard_map/ppermute | solution.py:537
  326.4 4.1 combine.6
  335.8 20.5 %attend_back.1 = (bf16[2,832,384]{2,1,0:T(8,128)(2,1)}, f32[832,128]{1,0:T(8,128)}, bf16[384,1664]{1,0:T(8,128)(2,1)}, bf16[384,1664]{1,0:T(8,128)(2,1)}) custom-call(s32[1]{0:T(128)} %bitcast.35.core_ref, bf16[832,768]{1,0:T(8,128)(2,1)} %pad_maximum_fusion.3.x_ref, f32[1,768]{1,0:T(1,128)} %copy.165.gain_ref, ...), custom_call_target="tpu_custom_call" | custom-call | flops 107347968 | bytes 119808 | tf_op jit(solution)/shard_map/attend_back/pallas_call | solution.py:193
  356.3 4.4 %collective-permute-done.37 = bf16[832,768]{1,0:T(8,128)(2,1)} collective-permute-done((bf16[832,768]{1,0:T(8,128)(2,1)}, bf16[832,768]{1,0:T(8,128)(2,1)}, u32[]{:S(2)}, u32[]{:S(2)}) %collective-permute-start.37) | collective-permute-done | bytes 1277984 | tf_op jit(solution)/shard_map/ppermute | solution.py:537
  392.3 6.2 %collective-permute-done.46 = bf16[2,192,1536]{2,1,0:T(8,128)(2,1)S(1)} collective-permute-done((bf16[2,192,1536]{2,1,0:T(8,128)(2,1)S(1)}, bf16[2,192,1536]{2,1,0:T(8,128)(2,1)S(1)}, u32[]{:S(2)}, u32[]{:S(2)}) %collective-permute-start.46) | collective-permute-done | bytes 1179680 | tf_op jit(solution)/shard_map/ppermute | solution.py:543
  407.2 4.6 %collective-permute-done.40 = bf16[832,384]{1,0:T(8,128)(2,1)S(1)} collective-permute-done((bf16[832,384]{1,0:T(8,128)(2,1)S(1)}, bf16[832,384]{1,0:T(8,128)(2,1)S(1)}, u32[]{:S(2)}, u32[]{:S(2)}) %collective-permute-start.40) | collective-permute-done | bytes 639008 | tf_op jit(solution)/shard_map/ppermute | solution.py:537
  (265 shorter events, 159.0 us)
Async XLA Ops:
  34.4 29.5 %collective-permute-start.9 = (bf16[2,192,1536]{2,1,0:T(8,128)(2,1)S(1)}, bf16[2,192,1536]{2,1,0:T(8,128)(2,1)}, u32[]{:S(2)}, u32[]{:S(2)}) collective-permute-start(bf16[2,192,1536]{2,1,0:T(8,128)(2,1)S(1)} %get-tuple-element.216.refs_8_.refs_12_), channel_id=1, source_target_pairs={{0,8},{4,12},{8,16},{12,20},{16,24},{20,28},{24,0},{28,4},{1,9},{5... | collective-permute-start | bytes 3538952 | tf_op jit(solution)/shard_map/ppermute | solution.py:543
  63.9 28.4 %collective-permute-start.12 = (bf16[2,192,1536]{2,1,0:T(8,128)(2,1)S(1)}, bf16[2,192,1536]{2,1,0:T(8,128)(2,1)S(1)}, u32[]{:S(2)}, u32[]{:S(2)}) collective-permute-start(bf16[2,192,1536]{2,1,0:T(8,128)(2,1)S(1)} %get-tuple-element.216.refs_8_.refs_12_), channel_id=1, source_target_pairs={{0,24},{4,28},{8,0},{12,4},{16,8},{20,12},{24,16},{28,20},{1,25},{... | collective-permute-start | bytes 3538952 | tf_op jit(solution)/shard_map/ppermute | solution.py:543
  93.3 30.0 %collective-permute-start.13 = (bf16[832,768]{1,0:T(8,128)(2,1)}, bf16[832,768]{1,0:T(8,128)(2,1)}, u32[]{:S(2)}, u32[]{:S(2)}) collective-permute-start(bf16[832,768]{1,0:T(8,128)(2,1)} %get-tuple-element.87), channel_id=1, source_target_pairs={{0,2},{2,0},{1,3},{3,1},{4,6},{6,4},{5,7},{7,5},{8,10},{10,8},{9,1... | collective-permute-start | bytes 3833864 | tf_op jit(solution)/shard_map/ppermute | solution.py:537
  93.8 29.3 %collective-permute-start.14 = (bf16[2,192,1536]{2,1,0:T(8,128)(2,1)}, bf16[2,192,1536]{2,1,0:T(8,128)(2,1)S(1)}, u32[]{:S(2)}, u32[]{:S(2)}) collective-permute-start(bf16[2,192,1536]{2,1,0:T(8,128)(2,1)} %collective-permute-done.9.refs_9_.refs_13_), channel_id=1, source_target_pairs={{0,8},{4,12},{8,16},{12,20},{16,24},{20,28},{24,0},{28,4},{1,9},{5... | collective-permute-start | bytes 3538952 | tf_op jit(solution)/shard_map/ppermute | solution.py:543
  100.9 29.7 %collective-permute-start.19 = (bf16[832,768]{1,0:T(8,128)(2,1)}, bf16[832,768]{1,0:T(8,128)(2,1)}, u32[]{:S(2)}, u32[]{:S(2)}) collective-permute-start(bf16[832,768]{1,0:T(8,128)(2,1)} %pad_maximum_fusion.5.refs_4_), channel_id=1, source_target_pairs={{0,1},{1,0},{2,3},{3,2},{4,5},{5,4},{6,7},{7,6},{8,9},{9,8},{10,11... | collective-permute-start | bytes 3833864 | tf_op jit(solution)/shard_map/ppermute | solution.py:537
  129.8 28.8 %collective-permute-start.16 = (bf16[832,768]{1,0:T(8,128)(2,1)}, bf16[832,768]{1,0:T(8,128)(2,1)}, u32[]{:S(2)}, u32[]{:S(2)}) collective-permute-start(bf16[832,768]{1,0:T(8,128)(2,1)} %multiply_convert_fusion.refs_0_.refs_6_), channel_id=1, source_target_pairs={{0,1},{1,0},{2,3},{3,2},{4,5},{5,4},{6,7},{7,6},{8,9},{9,8},{10,11... | collective-permute-start | bytes 3833864 | tf_op jit(solution)/shard_map/ppermute | solution.py:537
  130.3 28.2 %collective-permute-start.15 = (bf16[2,192,1536]{2,1,0:T(8,128)(2,1)}, bf16[2,192,1536]{2,1,0:T(8,128)(2,1)}, u32[]{:S(2)}, u32[]{:S(2)}) collective-permute-start(bf16[2,192,1536]{2,1,0:T(8,128)(2,1)} %get-tuple-element.100.refs_8_.refs_12_), channel_id=1, source_target_pairs={{0,8},{4,12},{8,16},{12,20},{16,24},{20,28},{24,0},{28,4},{1,9},{5... | collective-permute-start | bytes 3538952 | tf_op jit(solution)/shard_map/ppermute | solution.py:543
  130.4 32.0 %collective-permute-start.20 = (bf16[832,768]{1,0:T(8,128)(2,1)}, bf16[832,768]{1,0:T(8,128)(2,1)}, u32[]{:S(2)}, u32[]{:S(2)}) collective-permute-start(bf16[832,768]{1,0:T(8,128)(2,1)} %pad_maximum_fusion.5.refs_4_), channel_id=1, source_target_pairs={{0,4},{4,0},{8,12},{12,8},{16,20},{20,16},{24,28},{28,24},{1,5},{5... | collective-permute-start | bytes 3833864 | tf_op jit(solution)/shard_map/ppermute | solution.py:546
  130.7 31.8 %collective-permute-start.21 = (bf16[832,768]{1,0:T(8,128)(2,1)}, bf16[832,768]{1,0:T(8,128)(2,1)}, u32[]{:S(2)}, u32[]{:S(2)}) collective-permute-start(bf16[832,768]{1,0:T(8,128)(2,1)} %collective-permute-done.19.refs_5_), channel_id=1, source_target_pairs={{0,4},{4,0},{8,12},{12,8},{16,20},{20,16},{24,28},{28,24},{1,5},{5... | collective-permute-start | bytes 3833864 | tf_op jit(solution)/shard_map/ppermute | solution.py:546
  159.1 49.9 %collective-permute-start.24 = (bf16[2,192,1536]{2,1,0:T(8,128)(2,1)}, bf16[2,192,1536]{2,1,0:T(8,128)(2,1)}, u32[]{:S(2)}, u32[]{:S(2)}) collective-permute-start(bf16[2,192,1536]{2,1,0:T(8,128)(2,1)} %get-tuple-element.100.refs_8_.refs_12_), channel_id=1, source_target_pairs={{0,24},{4,28},{8,0},{12,4},{16,8},{20,12},{24,16},{28,20},{1,25},{... | collective-permute-start | bytes 3538952 | tf_op jit(solution)/shard_map/ppermute | solution.py:543
  162.3 52.3 %collective-permute-start.23 = (bf16[2,192,1536]{2,1,0:T(8,128)(2,1)}, bf16[2,192,1536]{2,1,0:T(8,128)(2,1)}, u32[]{:S(2)}, u32[]{:S(2)}) collective-permute-start(bf16[2,192,1536]{2,1,0:T(8,128)(2,1)} %collective-permute-done.15.refs_9_.refs_13_), channel_id=1, source_target_pairs={{0,8},{4,12},{8,16},{12,20},{16,24},{20,28},{24,0},{28,4},{1,9},{5... | collective-permute-start | bytes 3538952 | tf_op jit(solution)/shard_map/ppermute | solution.py:543
  204.2 39.1 %collective-permute-start.22 = (bf16[2,192,1536]{2,1,0:T(8,128)(2,1)}, bf16[2,192,1536]{2,1,0:T(8,128)(2,1)}, u32[]{:S(2)}, u32[]{:S(2)}) collective-permute-start(bf16[2,192,1536]{2,1,0:T(8,128)(2,1)} %get-tuple-element.97), channel_id=1, source_target_pairs={{0,8},{4,12},{8,16},{12,20},{16,24},{20,28},{24,0},{28,4},{1,9},{5... | collective-permute-start | bytes 3538952 | tf_op jit(solution)/shard_map/ppermute | solution.py:543
  204.2 60.5 %collective-permute-start.27 = (bf16[2,192,1536]{2,1,0:T(8,128)(2,1)}, bf16[2,192,1536]{2,1,0:T(8,128)(2,1)}, u32[]{:S(2)}, u32[]{:S(2)}) collective-permute-start(bf16[2,192,1536]{2,1,0:T(8,128)(2,1)} %get-tuple-element.107), channel_id=1, source_target_pairs={{0,24},{4,28},{8,0},{12,4},{16,8},{20,12},{24,16},{28,20},{1,25},{... | collective-permute-start | bytes 3538952 | tf_op jit(solution)/shard_map/ppermute | solution.py:543
  254.3 24.8 %collective-permute-start.25 = (bf16[832,384]{1,0:T(8,128)(2,1)}, bf16[832,384]{1,0:T(8,128)(2,1)}, u32[]{:S(2)}, u32[]{:S(2)}) collective-permute-start(bf16[832,384]{1,0:T(8,128)(2,1)} %get-tuple-element.105), channel_id=1, source_target_pairs={{0,4},{4,0},{8,12},{12,8},{16,20},{20,16},{24,28},{28,24},{1,5},{5... | collective-permute-start | bytes 1916936 | tf_op jit(solution)/shard_map/ppermute | solution.py:546
  275.0 42.3 %collective-permute-start.33 = (bf16[2,192,1536]{2,1,0:T(8,128)(2,1)}, bf16[2,192,1536]{2,1,0:T(8,128)(2,1)}, u32[]{:S(2)}, u32[]{:S(2)}) collective-permute-start(bf16[2,192,1536]{2,1,0:T(8,128)(2,1)} %add_convert_fusion.3), channel_id=1, source_target_pairs={{0,8},{4,12},{8,16},{12,20},{16,24},{20,28},{24,0},{28,4},{1,9},{5... | collective-permute-start | bytes 3538952 | tf_op jit(solution)/shard_map/ppermute | solution.py:543
  276.8 31.4 %collective-permute-start.34 = (bf16[832,384]{1,0:T(8,128)(2,1)}, bf16[832,384]{1,0:T(8,128)(2,1)}, u32[]{:S(2)}, u32[]{:S(2)}) collective-permute-start(bf16[832,384]{1,0:T(8,128)(2,1)} %get-tuple-element.125), channel_id=1, source_target_pairs={{0,1},{1,0},{2,3},{3,2},{4,5},{5,4},{6,7},{7,6},{8,9},{9,8},{10,11... | collective-permute-start | bytes 1916936 | tf_op jit(solution)/shard_map/ppermute | solution.py:537
  290.9 29.9 %collective-permute-start.32 = (bf16[832,384]{1,0:T(8,128)(2,1)S(1)}, bf16[832,384]{1,0:T(8,128)(2,1)S(1)}, u32[]{:S(2)}, u32[]{:S(2)}) collective-permute-start(bf16[832,384]{1,0:T(8,128)(2,1)S(1)} %add_convert_fusion.6), channel_id=1, source_target_pairs={{0,2},{2,0},{1,3},{3,1},{4,6},{6,4},{5,7},{7,5},{8,10},{10,8},{9,1... | collective-permute-start | bytes 1916936 | tf_op jit(solution)/shard_map/ppermute | solution.py:537
  310.0 46.3 %collective-permute-start.38 = (bf16[2,192,1536]{2,1,0:T(8,128)(2,1)}, bf16[2,192,1536]{2,1,0:T(8,128)(2,1)}, u32[]{:S(2)}, u32[]{:S(2)}) collective-permute-start(bf16[2,192,1536]{2,1,0:T(8,128)(2,1)} %get-tuple-element.135), channel_id=1, source_target_pairs={{0,24},{4,28},{8,0},{12,4},{16,8},{20,12},{24,16},{28,20},{1,25},{... | collective-permute-start | bytes 3538952 | tf_op jit(solution)/shard_map/ppermute | solution.py:543
  317.3 48.3 %collective-permute-start.45 = (bf16[2,192,1536]{2,1,0:T(8,128)(2,1)}, bf16[2,192,1536]{2,1,0:T(8,128)(2,1)}, u32[]{:S(2)}, u32[]{:S(2)}) collective-permute-start(bf16[2,192,1536]{2,1,0:T(8,128)(2,1)} %get-tuple-element.147), channel_id=1, source_target_pairs={{0,8},{4,12},{8,16},{12,20},{16,24},{20,28},{24,0},{28,4},{1,9},{5... | collective-permute-start | bytes 3538952 | tf_op jit(solution)/shard_map/ppermute | solution.py:543
  330.6 30.1 %collective-permute-start.37 = (bf16[832,768]{1,0:T(8,128)(2,1)}, bf16[832,768]{1,0:T(8,128)(2,1)}, u32[]{:S(2)}, u32[]{:S(2)}) collective-permute-start(bf16[832,768]{1,0:T(8,128)(2,1)} %combine.6), channel_id=1, source_target_pairs={{0,1},{1,0},{2,3},{3,2},{4,5},{5,4},{6,7},{7,6},{8,9},{9,8},{10,11... | collective-permute-start | bytes 3833864 | tf_op jit(solution)/shard_map/ppermute | solution.py:537
  367.5 31.0 %collective-permute-start.46 = (bf16[2,192,1536]{2,1,0:T(8,128)(2,1)S(1)}, bf16[2,192,1536]{2,1,0:T(8,128)(2,1)S(1)}, u32[]{:S(2)}, u32[]{:S(2)}) collective-permute-start(bf16[2,192,1536]{2,1,0:T(8,128)(2,1)S(1)} %add_convert_fusion.2), channel_id=1, source_target_pairs={{0,8},{4,12},{8,16},{12,20},{16,24},{20,28},{24,0},{28,4},{1,9},{5... | collective-permute-start | bytes 3538952 | tf_op jit(solution)/shard_map/ppermute | solution.py:543
  373.6 29.4 %collective-permute-start.44 = (f32[2,832]{0,1:T(8,128)}, f32[2,832]{0,1:T(8,128)S(1)}, u32[]{:S(2)}, u32[]{:S(2)}) collective-permute-start(f32[2,832]{0,1:T(8,128)} %slice_bitcast_fusion.2), channel_id=1, source_target_pairs={{0,2},{2,0},{1,3},{3,1},{4,6},{6,4},{5,7},{7,5},{8,10},{10,8},{9,1... | collective-permute-start | bytes 19976 | tf_op jit(solution)/shard_map/ppermute | solution.py:537
  376.0 31.2 %collective-permute-start.43 = (bf16[832,384]{1,0:T(8,128)(2,1)}, bf16[832,384]{1,0:T(8,128)(2,1)}, u32[]{:S(2)}, u32[]{:S(2)}) collective-permute-start(bf16[832,384]{1,0:T(8,128)(2,1)} %dynamic-slice_bitcast_fusion), channel_id=1, source_target_pairs={{0,2},{2,0},{1,3},{3,1},{4,6},{6,4},{5,7},{7,5},{8,10},{10,8},{9,1... | collective-permute-start | bytes 1916936 | tf_op jit(solution)/shard_map/ppermute | solution.py:537
  382.7 29.0 %collective-permute-start.40 = (bf16[832,384]{1,0:T(8,128)(2,1)S(1)}, bf16[832,384]{1,0:T(8,128)(2,1)S(1)}, u32[]{:S(2)}, u32[]{:S(2)}) collective-permute-start(bf16[832,384]{1,0:T(8,128)(2,1)S(1)} %constant_dynamic-slice_fusion), channel_id=1, source_target_pairs={{0,2},{2,0},{1,3},{3,1},{4,6},{6,4},{5,7},{7,5},{8,10},{10,8},{9,1... | collective-permute-start | bytes 1916936 | tf_op jit(solution)/shard_map/ppermute | solution.py:537
  (64 other events, 649.1 us)
